TPU v7x, 512 devices: a whole 4x8x8 slice. The times are simulated.
512 devices in a mesh: section: 4 (over x), ha: 16 (over y, core), wa: 8 (over z).
Axes of the slice: x: 4, y: 8, z: 8, core: 2. Of those that a mesh axis runs over, the one named last changes fastest.
Arguments:
- coarse_inputs: bfloat16 [4, 4, 192, 32, 128], P('section', None, None, 'ha', 'wa'), may hold values from -6 to 6
- init_level3: bfloat16 [192, 32, 128], P(None, 'ha', 'wa'), may hold values from -6 to 6
- init_level4: bfloat16 [96, 64, 256], P(None, 'ha', 'wa'), may hold values from -6 to 6
- weight_level3: bfloat16 [576, 9, 384], P('ha'), may hold values from -0.109375 to 0.109375
- weight_level4: bfloat16 [288, 9, 192], P('ha'), may hold values from -0.15625 to 0.15625
- lift_map: bfloat16 [96, 192], replicated, may hold values from -0.4375 to 0.4375
- readout: bfloat16 [16, 96], replicated, may hold values from -0.625 to 0.625
Outputs:
- precip: float32 [4, 4, 16, 64, 256], P('section', None, None, 'ha', 'wa')
All inputs are finite; a program needn't handle non-finite values.
Results may differ from a plain program's by a relative error of at most 0.008.
Values may be sent and summed in bfloat16 or wider, within the bound.
A program may use at most 128 MiB of HBM per device.

v0:
```python
import jax
import jax.numpy as jnp
from jax import lax
from jax.sharding import PartitionSpec as P


def extended(array, sides, width):
    for axis, dim in sides:
        size, length = (lax.axis_size(axis), array.shape[dim])
        up = [(i, (i + 1) % size) for i in range(size - 1)]
        down = [(j, i) for i, j in up]
        last = lax.slice_in_dim(array, length - width, length, axis=dim)
        leading = lax.slice_in_dim(array, 0, width, axis=dim)
        before = lax.ppermute(last, axis, up)
        after = lax.ppermute(leading, axis, down)
        array = jnp.concatenate([before, array, after], axis=dim)
    return array


def unfold(padded, tile_rows, tile_cols):
    shifted = [
        padded[:, down : down + tile_rows, across : across + tile_cols]
        for down in range(3)
        for across in range(3)
    ]
    stacked = jnp.stack(shifted, 0)
    return stacked.reshape(9 * padded.shape[0], tile_rows * tile_cols)


def apply_rows(weight, row_start, row_count, padded, tile_rows, tile_cols):
    matrix = weight[row_start : row_start + row_count].reshape(row_count, -1)
    return jnp.dot(matrix, unfold(padded, tile_rows, tile_cols), preferred_element_type=jnp.float32)


def recur_tile(inputs, previous, weight):
    channels, tile_rows, tile_cols = previous.shape
    joined = jnp.concatenate([inputs, previous], 0)
    padded = extended(joined, (("ha", 1), ("wa", 2)), 1)
    gate_sums = apply_rows(weight, 0, 2 * channels, padded, tile_rows, tile_cols)
    reset_gate = jax.nn.sigmoid(gate_sums[:channels])
    update = jax.nn.sigmoid(gate_sums[channels:])
    prior_flat = previous.reshape(channels, -1).astype(jnp.float32)
    gated_state = (
        (reset_gate * prior_flat).astype(jnp.bfloat16).reshape(channels, tile_rows, tile_cols)
    )
    gated_wide = extended(gated_state, (("ha", 1), ("wa", 2)), 1)
    mixed = jnp.concatenate([padded[:channels], gated_wide], 0)
    candidate = jax.nn.relu(apply_rows(weight, 2 * channels, channels, mixed, tile_rows, tile_cols))
    prior_state = previous.reshape(channels, -1).astype(jnp.float32)
    fresh_state = update * prior_state + (1.0 - update) * candidate
    return fresh_state.astype(jnp.bfloat16).reshape(channels, tile_rows, tile_cols)


def lift_member(level3_state, lift_map):
    channels, tile_rows, tile_cols = level3_state.shape
    coarse_lift = jnp.dot(
        lift_map, level3_state.reshape(channels, -1), preferred_element_type=jnp.float32
    )
    coarse_lift = coarse_lift.astype(jnp.bfloat16).reshape(lift_map.shape[0], tile_rows, tile_cols)
    return jnp.repeat(jnp.repeat(coarse_lift, 2, axis=1), 2, axis=2)


def read_out(readout, states4):
    members, channels, tile_rows, tile_cols = states4.shape
    flat_states = states4.reshape(members, channels, tile_rows * tile_cols)
    field = jnp.einsum("sc,mcn->msn", readout, flat_states, preferred_element_type=jnp.float32)
    return field.reshape(members, readout.shape[0], tile_rows, tile_cols)


def local(coarse_inputs, init_level3, init_level4, weight_level3, weight_level4, lift_map, readout):
    full_level3, full_level4 = (
        lax.all_gather(weight_level3, "ha", axis=0, tiled=True),
        lax.all_gather(weight_level4, "ha", axis=0, tiled=True),
    )
    all_leads = lax.all_to_all(coarse_inputs, "section", split_axis=1, concat_axis=0, tiled=True)
    lead_count = all_leads.shape[0]
    level3_state = init_level3
    level4_state = init_level4
    by_lead = []
    for lead_time in range(lead_count):
        level3_state = recur_tile(all_leads[lead_time, 0], level3_state, full_level3)
        level4_state = recur_tile(lift_member(level3_state, lift_map), level4_state, full_level4)
        by_lead.append(level4_state)
    by_member = [read_out(readout, jnp.stack(by_lead, 0))]
    fields = jnp.stack(by_member, 1)
    return lax.all_to_all(
        fields.astype(jnp.bfloat16), "section", split_axis=0, concat_axis=1, tiled=True
    ).astype(fields.dtype)


def solution(mesh):
    return jax.shard_map(
        local,
        mesh=mesh,
        in_specs=(
            P("section", None, None, "ha", "wa"),
            P(None, "ha", "wa"),
            P(None, "ha", "wa"),
            P("ha", None, None),
            P("ha", None, None),
            P(),
            P(),
        ),
        out_specs=P("section", None, None, "ha", "wa"),
        check_vma=False,
    )
```

profile of v0, /device:TPU:288, one launch (start us, length us, event | category | flops | bytes accessed | tf_op | source)
XLA Modules:
  0.0 381.1 jit_solution(8851988846549568427)
XLA Ops:
  8.4 9.9 %all_to_all.21 = bf16[1,4,192,2,16]{2,4,3,0,1:T(8,128)(2,1)S(1)} all-to-all(bf16[1,4,192,2,16]{2,4,3,0,1:T(8,128)(2,1)} %bitcast.961), channel_id=1, replica_groups=mesh['section'=4,'ha'=16,'wa'=8] {'section'}, dimensions={1} | all-to-all | bytes 98304 | tf_op jit(solution)/shard_map/all_to_all | solution.py:75
  21.0 2.4 collective-permute-start
  24.4 2.9 collective-permute-done
  30.0 3.9 %collective-permute-start.2 = (bf16[384,4,1]{0,2,1:T(2,128)(2,1)S(1)}, bf16[384,4,1]{0,2,1:T(2,128)(2,1)S(1)}, u32[]{:S(2)}, u32[]{:S(2)}) collective-permute-start(bf16[384,4,1]{0,2,1:T(2,128)(2,1)S(1)} %get-tuple-element.46), channel_id=1, source_target_pairs={{0,1},{1,2},{2,3},{3,4},{4,5},{5,6},{6,7},{8,9},{9,10},{10,11},{11... | collective-permute-start | bytes 9224 | tf_op jit(solution)/shard_map/ppermute | solution.py:14
  33.9 39.3 %all_gather.7 = bf16[288,9,192]{2,1,0:T(8,128)(2,1)} all-gather(bf16[18,9,192]{2,1,0:T(8,128)(2,1)S(1)} %copy.50), channel_id=1, replica_groups=mesh['section'=4,'ha'=16,'wa'=8] {'ha'}, dimensions={0}, use_global_device_ids=true | all-gather | bytes 1057536 | tf_op jit(solution)/shard_map/all_gather | solution.py:73
  73.9 5.0 %slice.1019 = bf16[384,9,384]{2,1,0:T(8,128)(2,1)} slice(bf16[576,9,384]{2,1,0:T(8,128)(2,1)} %all-gather.2.cloned.1.call-done), slice={[0:384], [0:9], [0:384]} | slice | bytes 5308416 | tf_op jit(solution)/shard_map/slice | solution.py:31
  78.9 5.5 %copy.76 = bf16[384,9,384]{0,2,1:T(8,128)(2,1)S(1)} copy(bf16[384,9,384]{2,1,0:T(8,128)(2,1)} %slice.1019) | data formatting | bytes 5308416
  91.8 2.6 copy.51
  98.4 3.5 collective-permute-start.6
  102.0 3.3 slice.1033
  105.3 4.2 %copy.48 = bf16[192,9,384]{0,2,1:T(8,128)(2,1)} copy(bf16[192,9,384]{2,1,0:T(8,128)(2,1)} %slice.1033) | data formatting | bytes 2654208 | tf_op jit(solution)/shard_map/slice | solution.py:31
  112.2 3.8 collective-permute-start.9
  118.0 4.8 %collective-permute-start.17 = (bf16[384,1,16]{0,2,1:T(8,128)(2,1)S(1)}, bf16[384,1,16]{0,2,1:T(8,128)(2,1)S(1)}, u32[]{:S(2)}, u32[]{:S(2)}) collective-permute-start(bf16[384,1,16]{0,2,1:T(8,128)(2,1)S(1)} %get-tuple-element.75), channel_id=1, source_target_pairs={{8,0},{16,8},{24,16},{32,24},{40,32},{48,40},{56,48},{64,56},{72,6... | collective-permute-start | bytes 36872 | tf_op jit(solution)/shard_map/ppermute | solution.py:15
  124.9 3.5 collective-permute-start.11
  131.4 4.7 %collective-permute-start.19 = (bf16[384,4,1]{0,2,1:T(2,128)(2,1)}, bf16[384,4,1]{0,2,1:T(2,128)(2,1)S(1)}, u32[]{:S(2)}, u32[]{:S(2)}) collective-permute-start(bf16[384,4,1]{0,2,1:T(2,128)(2,1)} %get-tuple-element.43), channel_id=1, source_target_pairs={{1,0},{2,1},{3,2},{4,3},{5,4},{6,5},{7,6},{9,8},{10,9},{11,10},{12... | collective-permute-start | bytes 9224 | tf_op jit(solution)/shard_map/ppermute | solution.py:15
  140.0 2.5 reshape.216
  144.5 4.0 %collective-permute-start.13 = (bf16[96,1,32]{0,2,1:T(8,128)(2,1)S(1)}, bf16[96,1,32]{0,2,1:T(8,128)(2,1)S(1)}, u32[]{:S(2)}, u32[]{:S(2)}) collective-permute-start(bf16[96,1,32]{0,2,1:T(8,128)(2,1)S(1)} %get-tuple-element.63), channel_id=1, source_target_pairs={{8,0},{16,8},{24,16},{32,24},{40,32},{48,40},{56,48},{64,56},{72,6... | collective-permute-start | bytes 18440 | tf_op jit(solution)/shard_map/ppermute | solution.py:15
  151.7 4.9 %collective-permute-start.21 = (bf16[192,1,16]{0,2,1:T(8,128)(2,1)S(1)}, bf16[192,1,16]{0,2,1:T(8,128)(2,1)S(1)}, u32[]{:S(2)}, u32[]{:S(2)}) collective-permute-start(bf16[192,1,16]{0,2,1:T(8,128)(2,1)S(1)} %get-tuple-element.85), channel_id=1, source_target_pairs={{8,0},{16,8},{24,16},{32,24},{40,32},{48,40},{56,48},{64,56},{72,6... | collective-permute-start | bytes 18440 | tf_op jit(solution)/shard_map/ppermute | solution.py:15
  158.5 4.9 %collective-permute-start.15 = (bf16[96,6,1]{0,2,1:T(2,128)(2,1)S(1)}, bf16[96,6,1]{0,2,1:T(2,128)(2,1)S(1)}, u32[]{:S(2)}, u32[]{:S(2)}) collective-permute-start(bf16[96,6,1]{0,2,1:T(2,128)(2,1)S(1)} %get-tuple-element.55), channel_id=1, source_target_pairs={{1,0},{2,1},{3,2},{4,3},{5,4},{6,5},{7,6},{9,8},{10,9},{11,10},{12... | collective-permute-start | bytes 3464 | tf_op jit(solution)/shard_map/ppermute | solution.py:15
  166.0 5.1 %collective-permute-start.23 = (bf16[192,4,1]{0,2,1:T(2,128)(2,1)}, bf16[192,4,1]{0,2,1:T(2,128)(2,1)}, u32[]{:S(2)}, u32[]{:S(2)}) collective-permute-start(bf16[192,4,1]{0,2,1:T(2,128)(2,1)} %get-tuple-element.73), channel_id=1, source_target_pairs={{1,0},{2,1},{3,2},{4,3},{5,4},{6,5},{7,6},{9,8},{10,9},{11,10},{12... | collective-permute-start | bytes 4616 | tf_op jit(solution)/shard_map/ppermute | solution.py:15
  175.0 2.5 reshape.219
  182.4 4.0 %collective-permute-start.25 = (bf16[192,1,32]{0,2,1:T(8,128)(2,1)S(1)}, bf16[192,1,32]{0,2,1:T(8,128)(2,1)S(1)}, u32[]{:S(2)}, u32[]{:S(2)}) collective-permute-start(bf16[192,1,32]{0,2,1:T(8,128)(2,1)S(1)} %get-tuple-element.26), channel_id=1, source_target_pairs={{8,0},{16,8},{24,16},{32,24},{40,32},{48,40},{56,48},{64,56},{72,6... | collective-permute-start | bytes 36872 | tf_op jit(solution)/shard_map/ppermute | solution.py:15
  188.4 4.8 %collective-permute-start.33 = (bf16[384,1,16]{0,2,1:T(8,128)(2,1)S(1)}, bf16[384,1,16]{0,2,1:T(8,128)(2,1)S(1)}, u32[]{:S(2)}, u32[]{:S(2)}) collective-permute-start(bf16[384,1,16]{0,2,1:T(8,128)(2,1)S(1)} %get-tuple-element.71), channel_id=1, source_target_pairs={{8,0},{16,8},{24,16},{32,24},{40,32},{48,40},{56,48},{64,56},{72,6... | collective-permute-start | bytes 36872 | tf_op jit(solution)/shard_map/ppermute | solution.py:15
  195.3 4.9 %collective-permute-start.27 = (bf16[192,6,1]{0,2,1:T(2,128)(2,1)S(1)}, bf16[192,6,1]{0,2,1:T(2,128)(2,1)S(1)}, u32[]{:S(2)}, u32[]{:S(2)}) collective-permute-start(bf16[192,6,1]{0,2,1:T(2,128)(2,1)S(1)} %get-tuple-element.16), channel_id=1, source_target_pairs={{1,0},{2,1},{3,2},{4,3},{5,4},{6,5},{7,6},{9,8},{10,9},{11,10},{12... | collective-permute-start | bytes 6920 | tf_op jit(solution)/shard_map/ppermute | solution.py:15
  202.2 5.1 %collective-permute-start.35 = (bf16[384,4,1]{0,2,1:T(2,128)(2,1)S(1)}, bf16[384,4,1]{0,2,1:T(2,128)(2,1)S(1)}, u32[]{:S(2)}, u32[]{:S(2)}) collective-permute-start(bf16[384,4,1]{0,2,1:T(2,128)(2,1)S(1)} %get-tuple-element.39), channel_id=1, source_target_pairs={{1,0},{2,1},{3,2},{4,3},{5,4},{6,5},{7,6},{9,8},{10,9},{11,10},{12... | collective-permute-start | bytes 9224 | tf_op jit(solution)/shard_map/ppermute | solution.py:15
  211.2 2.5 reshape.229
  215.7 4.0 %collective-permute-start.29 = (bf16[96,1,32]{0,2,1:T(8,128)(2,1)S(1)}, bf16[96,1,32]{0,2,1:T(8,128)(2,1)S(1)}, u32[]{:S(2)}, u32[]{:S(2)}) collective-permute-start(bf16[96,1,32]{0,2,1:T(8,128)(2,1)S(1)} %get-tuple-element.61), channel_id=1, source_target_pairs={{8,0},{16,8},{24,16},{32,24},{40,32},{48,40},{56,48},{64,56},{72,6... | collective-permute-start | bytes 18440 | tf_op jit(solution)/shard_map/ppermute | solution.py:15
  222.9 4.9 %collective-permute-start.37 = (bf16[192,1,16]{0,2,1:T(8,128)(2,1)S(1)}, bf16[192,1,16]{0,2,1:T(8,128)(2,1)S(1)}, u32[]{:S(2)}, u32[]{:S(2)}) collective-permute-start(bf16[192,1,16]{0,2,1:T(8,128)(2,1)S(1)} %get-tuple-element.83), channel_id=1, source_target_pairs={{8,0},{16,8},{24,16},{32,24},{40,32},{48,40},{56,48},{64,56},{72,6... | collective-permute-start | bytes 18440 | tf_op jit(solution)/shard_map/ppermute | solution.py:15
  229.7 4.9 %collective-permute-start.31 = (bf16[96,6,1]{0,2,1:T(2,128)(2,1)S(1)}, bf16[96,6,1]{0,2,1:T(2,128)(2,1)S(1)}, u32[]{:S(2)}, u32[]{:S(2)}) collective-permute-start(bf16[96,6,1]{0,2,1:T(2,128)(2,1)S(1)} %get-tuple-element.53), channel_id=1, source_target_pairs={{1,0},{2,1},{3,2},{4,3},{5,4},{6,5},{7,6},{9,8},{10,9},{11,10},{12... | collective-permute-start | bytes 3464 | tf_op jit(solution)/shard_map/ppermute | solution.py:15
  237.1 5.1 %collective-permute-start.39 = (bf16[192,4,1]{0,2,1:T(2,128)(2,1)}, bf16[192,4,1]{0,2,1:T(2,128)(2,1)}, u32[]{:S(2)}, u32[]{:S(2)}) collective-permute-start(bf16[192,4,1]{0,2,1:T(2,128)(2,1)} %get-tuple-element.69), channel_id=1, source_target_pairs={{1,0},{2,1},{3,2},{4,3},{5,4},{6,5},{7,6},{9,8},{10,9},{11,10},{12... | collective-permute-start | bytes 4616 | tf_op jit(solution)/shard_map/ppermute | solution.py:15
  246.0 2.5 reshape.231
  253.3 4.0 %collective-permute-start.41 = (bf16[192,1,32]{0,2,1:T(8,128)(2,1)S(1)}, bf16[192,1,32]{0,2,1:T(8,128)(2,1)S(1)}, u32[]{:S(2)}, u32[]{:S(2)}) collective-permute-start(bf16[192,1,32]{0,2,1:T(8,128)(2,1)S(1)} %get-tuple-element.24), channel_id=1, source_target_pairs={{8,0},{16,8},{24,16},{32,24},{40,32},{48,40},{56,48},{64,56},{72,6... | collective-permute-start | bytes 36872 | tf_op jit(solution)/shard_map/ppermute | solution.py:15
  259.4 4.8 %collective-permute-start.49 = (bf16[384,1,16]{0,2,1:T(8,128)(2,1)S(1)}, bf16[384,1,16]{0,2,1:T(8,128)(2,1)S(1)}, u32[]{:S(2)}, u32[]{:S(2)}) collective-permute-start(bf16[384,1,16]{0,2,1:T(8,128)(2,1)S(1)} %get-tuple-element.67), channel_id=1, source_target_pairs={{8,0},{16,8},{24,16},{32,24},{40,32},{48,40},{56,48},{64,56},{72,6... | collective-permute-start | bytes 36872 | tf_op jit(solution)/shard_map/ppermute | solution.py:15
  266.3 4.9 %collective-permute-start.43 = (bf16[192,6,1]{0,2,1:T(2,128)(2,1)S(1)}, bf16[192,6,1]{0,2,1:T(2,128)(2,1)S(1)}, u32[]{:S(2)}, u32[]{:S(2)}) collective-permute-start(bf16[192,6,1]{0,2,1:T(2,128)(2,1)S(1)} %get-tuple-element.12), channel_id=1, source_target_pairs={{1,0},{2,1},{3,2},{4,3},{5,4},{6,5},{7,6},{9,8},{10,9},{11,10},{12... | collective-permute-start | bytes 6920 | tf_op jit(solution)/shard_map/ppermute | solution.py:15
  273.2 5.1 %collective-permute-start.51 = (bf16[384,4,1]{0,2,1:T(2,128)(2,1)S(1)}, bf16[384,4,1]{0,2,1:T(2,128)(2,1)S(1)}, u32[]{:S(2)}, u32[]{:S(2)}) collective-permute-start(bf16[384,4,1]{0,2,1:T(2,128)(2,1)S(1)} %get-tuple-element.35), channel_id=1, source_target_pairs={{1,0},{2,1},{3,2},{4,3},{5,4},{6,5},{7,6},{9,8},{10,9},{11,10},{12... | collective-permute-start | bytes 9224 | tf_op jit(solution)/shard_map/ppermute | solution.py:15
  282.1 2.5 reshape.240
  286.6 4.0 %collective-permute-start.45 = (bf16[96,1,32]{0,2,1:T(8,128)(2,1)S(1)}, bf16[96,1,32]{0,2,1:T(8,128)(2,1)S(1)}, u32[]{:S(2)}, u32[]{:S(2)}) collective-permute-start(bf16[96,1,32]{0,2,1:T(8,128)(2,1)S(1)} %get-tuple-element.59), channel_id=1, source_target_pairs={{8,0},{16,8},{24,16},{32,24},{40,32},{48,40},{56,48},{64,56},{72,6... | collective-permute-start | bytes 18440 | tf_op jit(solution)/shard_map/ppermute | solution.py:15
  294.1 4.9 %collective-permute-start.53 = (bf16[192,1,16]{0,2,1:T(8,128)(2,1)S(1)}, bf16[192,1,16]{0,2,1:T(8,128)(2,1)S(1)}, u32[]{:S(2)}, u32[]{:S(2)}) collective-permute-start(bf16[192,1,16]{0,2,1:T(8,128)(2,1)S(1)} %get-tuple-element.81), channel_id=1, source_target_pairs={{8,0},{16,8},{24,16},{32,24},{40,32},{48,40},{56,48},{64,56},{72,6... | collective-permute-start | bytes 18440 | tf_op jit(solution)/shard_map/ppermute | solution.py:15
  300.9 4.9 %collective-permute-start.47 = (bf16[96,6,1]{0,2,1:T(2,128)(2,1)S(1)}, bf16[96,6,1]{0,2,1:T(2,128)(2,1)S(1)}, u32[]{:S(2)}, u32[]{:S(2)}) collective-permute-start(bf16[96,6,1]{0,2,1:T(2,128)(2,1)S(1)} %get-tuple-element.51), channel_id=1, source_target_pairs={{1,0},{2,1},{3,2},{4,3},{5,4},{6,5},{7,6},{9,8},{10,9},{11,10},{12... | collective-permute-start | bytes 3464 | tf_op jit(solution)/shard_map/ppermute | solution.py:15
  308.3 5.1 %collective-permute-start.55 = (bf16[192,4,1]{0,2,1:T(2,128)(2,1)}, bf16[192,4,1]{0,2,1:T(2,128)(2,1)}, u32[]{:S(2)}, u32[]{:S(2)}) collective-permute-start(bf16[192,4,1]{0,2,1:T(2,128)(2,1)} %get-tuple-element.65), channel_id=1, source_target_pairs={{1,0},{2,1},{3,2},{4,3},{5,4},{6,5},{7,6},{9,8},{10,9},{11,10},{12... | collective-permute-start | bytes 4616 | tf_op jit(solution)/shard_map/ppermute | solution.py:15
  322.4 2.9 collective-permute-start.57
  327.2 4.3 %collective-permute-done.56 = bf16[192,1,32]{0,2,1:T(8,128)(2,1)S(1)} collective-permute-done((bf16[192,1,32]{0,2,1:T(8,128)(2,1)S(1)}, bf16[192,1,32]{0,2,1:T(8,128)(2,1)S(1)}, u32[]{:S(2)}, u32[]{:S(2)}) %collective-permute-start.56) | collective-permute-done | bytes 12320 | tf_op jit(solution)/shard_map/ppermute | solution.py:14
  331.6 4.7 %collective-permute-start.59 = (bf16[192,6,1]{0,2,1:T(2,128)(2,1)S(1)}, bf16[192,6,1]{0,2,1:T(2,128)(2,1)S(1)}, u32[]{:S(2)}, u32[]{:S(2)}) collective-permute-start(bf16[192,6,1]{0,2,1:T(2,128)(2,1)S(1)} %get-tuple-element.8), channel_id=1, source_target_pairs={{1,0},{2,1},{3,2},{4,3},{5,4},{6,5},{7,6},{9,8},{10,9},{11,10},{12... | collective-permute-start | bytes 6920 | tf_op jit(solution)/shard_map/ppermute | solution.py:15
  338.4 4.8 %collective-permute-done.58 = bf16[192,6,1]{0,2,1:T(2,128)(2,1)S(1)} collective-permute-done((bf16[192,6,1]{0,2,1:T(2,128)(2,1)S(1)}, bf16[192,6,1]{0,2,1:T(2,128)(2,1)S(1)}, u32[]{:S(2)}, u32[]{:S(2)}) %collective-permute-start.58) | collective-permute-done | bytes 2336 | tf_op jit(solution)/shard_map/ppermute | solution.py:14
  349.8 3.8 collective-permute-done.60
  355.5 3.9 %collective-permute-start.62 = (bf16[96,6,1]{0,2,1:T(2,128)(2,1)S(1)}, bf16[96,6,1]{0,2,1:T(2,128)(2,1)S(1)}, u32[]{:S(2)}, u32[]{:S(2)}) collective-permute-start(bf16[96,6,1]{0,2,1:T(2,128)(2,1)S(1)} %get-tuple-element.48), channel_id=1, source_target_pairs={{0,1},{1,2},{2,3},{3,4},{4,5},{5,6},{6,7},{8,9},{9,10},{10,11},{11... | collective-permute-start | bytes 3464 | tf_op jit(solution)/shard_map/ppermute | solution.py:14
  359.4 2.8 collective-permute-done.62
  364.3 9.2 %all_to_all.22 = bf16[4,2,1024]{2,1,0:T(2,128)(2,1)S(1)} all-to-all(bf16[4,2,1024]{2,1,0:T(2,128)(2,1)S(1)} %reshape.258), channel_id=1, replica_groups=mesh['section'=4,'ha'=16,'wa'=8] {'section'}, dimensions={0} | all-to-all | bytes 32768 | tf_op jit(solution)/shard_map/all_to_all | solution.py:86
  (475 shorter events, 122.1 us)
Async XLA Ops:
  6.5 67.3 %all-gather.2.cloned.1.call-start = ((), (), s32[]{:S(2)}) async-start(), calls=%async_computation.2 | async-start | bytes 7520256 | tf_op jit(solution)/shard_map/all_gather | solution.py:72
  28.1 45.1 %collective-permute-start.3 = (bf16[384,4,1]{0,2,1:T(2,128)(2,1)S(1)}, bf16[384,4,1]{0,2,1:T(2,128)(2,1)S(1)}, u32[]{:S(2)}, u32[]{:S(2)}) collective-permute-start(bf16[384,4,1]{0,2,1:T(2,128)(2,1)S(1)} %get-tuple-element.47), channel_id=1, source_target_pairs={{1,0},{2,1},{3,2},{4,3},{5,4},{6,5},{7,6},{9,8},{10,9},{11,10},{12... | collective-permute-start | bytes 9224 | tf_op jit(solution)/shard_map/ppermute | solution.py:15
  30.0 43.2 %collective-permute-start.2 = (bf16[384,4,1]{0,2,1:T(2,128)(2,1)S(1)}, bf16[384,4,1]{0,2,1:T(2,128)(2,1)S(1)}, u32[]{:S(2)}, u32[]{:S(2)}) collective-permute-start(bf16[384,4,1]{0,2,1:T(2,128)(2,1)S(1)} %get-tuple-element.46), channel_id=1, source_target_pairs={{0,1},{1,2},{2,3},{3,4},{4,5},{5,6},{6,7},{8,9},{9,10},{10,11},{11... | collective-permute-start | bytes 9224 | tf_op jit(solution)/shard_map/ppermute | solution.py:14
  85.0 11.1 %collective-permute-start.5 = (bf16[192,1,16]{0,2,1:T(8,128)(2,1)S(1)}, bf16[192,1,16]{0,2,1:T(8,128)(2,1)S(1)}, u32[]{:S(2)}, u32[]{:S(2)}) collective-permute-start(bf16[192,1,16]{0,2,1:T(8,128)(2,1)S(1)} %get-tuple-element.87), channel_id=1, source_target_pairs={{8,0},{16,8},{24,16},{32,24},{40,32},{48,40},{56,48},{64,56},{72,6... | collective-permute-start | bytes 18440 | tf_op jit(solution)/shard_map/ppermute | solution.py:15
  87.0 9.0 %collective-permute-start.4 = (bf16[192,1,16]{0,2,1:T(8,128)(2,1)S(1)}, bf16[192,1,16]{0,2,1:T(8,128)(2,1)S(1)}, u32[]{:S(2)}, u32[]{:S(2)}) collective-permute-start(bf16[192,1,16]{0,2,1:T(8,128)(2,1)S(1)} %get-tuple-element.86), channel_id=1, source_target_pairs={{0,8},{8,16},{16,24},{24,32},{32,40},{40,48},{48,56},{56,64},{64,7... | collective-permute-start | bytes 18440 | tf_op jit(solution)/shard_map/ppermute | solution.py:14
  96.1 13.4 %collective-permute-start.7 = (bf16[192,4,1]{0,2,1:T(2,128)(2,1)S(1)}, bf16[192,4,1]{0,2,1:T(2,128)(2,1)S(1)}, u32[]{:S(2)}, u32[]{:S(2)}) collective-permute-start(bf16[192,4,1]{0,2,1:T(2,128)(2,1)S(1)} %get-tuple-element.77), channel_id=1, source_target_pairs={{1,0},{2,1},{3,2},{4,3},{5,4},{6,5},{7,6},{9,8},{10,9},{11,10},{12... | collective-permute-start | bytes 4616 | tf_op jit(solution)/shard_map/ppermute | solution.py:15
  98.4 11.1 %collective-permute-start.6 = (bf16[192,4,1]{0,2,1:T(2,128)(2,1)S(1)}, bf16[192,4,1]{0,2,1:T(2,128)(2,1)S(1)}, u32[]{:S(2)}, u32[]{:S(2)}) collective-permute-start(bf16[192,4,1]{0,2,1:T(2,128)(2,1)S(1)} %get-tuple-element.76), channel_id=1, source_target_pairs={{0,1},{1,2},{2,3},{3,4},{4,5},{5,6},{6,7},{8,9},{9,10},{10,11},{11... | collective-permute-start | bytes 4616 | tf_op jit(solution)/shard_map/ppermute | solution.py:14
  112.2 12.6 %collective-permute-start.9 = (bf16[192,1,32]{0,2,1:T(8,128)(2,1)S(1)}, bf16[192,1,32]{0,2,1:T(8,128)(2,1)S(1)}, u32[]{:S(2)}, u32[]{:S(2)}) collective-permute-start(bf16[192,1,32]{0,2,1:T(8,128)(2,1)S(1)} %get-tuple-element.28), channel_id=1, source_target_pairs={{8,0},{16,8},{24,16},{32,24},{40,32},{48,40},{56,48},{64,56},{72,6... | collective-permute-start | bytes 36872 | tf_op jit(solution)/shard_map/ppermute | solution.py:15
  116.0 8.8 %collective-permute-start.8 = (bf16[192,1,32]{0,2,1:T(8,128)(2,1)S(1)}, bf16[192,1,32]{0,2,1:T(8,128)(2,1)S(1)}, u32[]{:S(2)}, u32[]{:S(2)}) collective-permute-start(bf16[192,1,32]{0,2,1:T(8,128)(2,1)S(1)} %get-tuple-element.27), channel_id=1, source_target_pairs={{0,8},{8,16},{16,24},{24,32},{32,40},{40,48},{48,56},{56,64},{64,7... | collective-permute-start | bytes 36872 | tf_op jit(solution)/shard_map/ppermute | solution.py:14
  118.0 12.8 %collective-permute-start.17 = (bf16[384,1,16]{0,2,1:T(8,128)(2,1)S(1)}, bf16[384,1,16]{0,2,1:T(8,128)(2,1)S(1)}, u32[]{:S(2)}, u32[]{:S(2)}) collective-permute-start(bf16[384,1,16]{0,2,1:T(8,128)(2,1)S(1)} %get-tuple-element.75), channel_id=1, source_target_pairs={{8,0},{16,8},{24,16},{32,24},{40,32},{48,40},{56,48},{64,56},{72,6... | collective-permute-start | bytes 36872 | tf_op jit(solution)/shard_map/ppermute | solution.py:15
  124.9 13.2 %collective-permute-start.11 = (bf16[192,6,1]{0,2,1:T(2,128)(2,1)S(1)}, bf16[192,6,1]{0,2,1:T(2,128)(2,1)S(1)}, u32[]{:S(2)}, u32[]{:S(2)}) collective-permute-start(bf16[192,6,1]{0,2,1:T(2,128)(2,1)S(1)} %get-tuple-element.20), channel_id=1, source_target_pairs={{1,0},{2,1},{3,2},{4,3},{5,4},{6,5},{7,6},{9,8},{10,9},{11,10},{12... | collective-permute-start | bytes 6920 | tf_op jit(solution)/shard_map/ppermute | solution.py:15
  128.4 9.7 %collective-permute-start.10 = (bf16[192,6,1]{0,2,1:T(2,128)(2,1)S(1)}, bf16[192,6,1]{0,2,1:T(2,128)(2,1)S(1)}, u32[]{:S(2)}, u32[]{:S(2)}) collective-permute-start(bf16[192,6,1]{0,2,1:T(2,128)(2,1)S(1)} %get-tuple-element.19), channel_id=1, source_target_pairs={{0,1},{1,2},{2,3},{3,4},{4,5},{5,6},{6,7},{8,9},{9,10},{10,11},{11... | collective-permute-start | bytes 6920 | tf_op jit(solution)/shard_map/ppermute | solution.py:14
  131.4 19.0 %collective-permute-start.19 = (bf16[384,4,1]{0,2,1:T(2,128)(2,1)}, bf16[384,4,1]{0,2,1:T(2,128)(2,1)S(1)}, u32[]{:S(2)}, u32[]{:S(2)}) collective-permute-start(bf16[384,4,1]{0,2,1:T(2,128)(2,1)} %get-tuple-element.43), channel_id=1, source_target_pairs={{1,0},{2,1},{3,2},{4,3},{5,4},{6,5},{7,6},{9,8},{10,9},{11,10},{12... | collective-permute-start | bytes 9224 | tf_op jit(solution)/shard_map/ppermute | solution.py:15
  136.2 14.3 %collective-permute-start.18 = (bf16[384,4,1]{0,2,1:T(2,128)(2,1)}, bf16[384,4,1]{0,2,1:T(2,128)(2,1)S(1)}, u32[]{:S(2)}, u32[]{:S(2)}) collective-permute-start(bf16[384,4,1]{0,2,1:T(2,128)(2,1)} %get-tuple-element.42), channel_id=1, source_target_pairs={{0,1},{1,2},{2,3},{3,4},{4,5},{5,6},{6,7},{8,9},{9,10},{10,11},{11... | collective-permute-start | bytes 9224 | tf_op jit(solution)/shard_map/ppermute | solution.py:14
  144.5 14.0 %collective-permute-start.13 = (bf16[96,1,32]{0,2,1:T(8,128)(2,1)S(1)}, bf16[96,1,32]{0,2,1:T(8,128)(2,1)S(1)}, u32[]{:S(2)}, u32[]{:S(2)}) collective-permute-start(bf16[96,1,32]{0,2,1:T(8,128)(2,1)S(1)} %get-tuple-element.63), channel_id=1, source_target_pairs={{8,0},{16,8},{24,16},{32,24},{40,32},{48,40},{56,48},{64,56},{72,6... | collective-permute-start | bytes 18440 | tf_op jit(solution)/shard_map/ppermute | solution.py:15
  148.5 10.0 %collective-permute-start.12 = (bf16[96,1,32]{0,2,1:T(8,128)(2,1)S(1)}, bf16[96,1,32]{0,2,1:T(8,128)(2,1)S(1)}, u32[]{:S(2)}, u32[]{:S(2)}) collective-permute-start(bf16[96,1,32]{0,2,1:T(8,128)(2,1)S(1)} %get-tuple-element.62), channel_id=1, source_target_pairs={{0,8},{8,16},{16,24},{24,32},{32,40},{40,48},{48,56},{56,64},{64,7... | collective-permute-start | bytes 18440 | tf_op jit(solution)/shard_map/ppermute | solution.py:14
  151.7 13.6 %collective-permute-start.21 = (bf16[192,1,16]{0,2,1:T(8,128)(2,1)S(1)}, bf16[192,1,16]{0,2,1:T(8,128)(2,1)S(1)}, u32[]{:S(2)}, u32[]{:S(2)}) collective-permute-start(bf16[192,1,16]{0,2,1:T(8,128)(2,1)S(1)} %get-tuple-element.85), channel_id=1, source_target_pairs={{8,0},{16,8},{24,16},{32,24},{40,32},{48,40},{56,48},{64,56},{72,6... | collective-permute-start | bytes 18440 | tf_op jit(solution)/shard_map/ppermute | solution.py:15
  158.5 14.7 %collective-permute-start.15 = (bf16[96,6,1]{0,2,1:T(2,128)(2,1)S(1)}, bf16[96,6,1]{0,2,1:T(2,128)(2,1)S(1)}, u32[]{:S(2)}, u32[]{:S(2)}) collective-permute-start(bf16[96,6,1]{0,2,1:T(2,128)(2,1)S(1)} %get-tuple-element.55), channel_id=1, source_target_pairs={{1,0},{2,1},{3,2},{4,3},{5,4},{6,5},{7,6},{9,8},{10,9},{11,10},{12... | collective-permute-start | bytes 3464 | tf_op jit(solution)/shard_map/ppermute | solution.py:15
  163.4 9.8 %collective-permute-start.14 = (bf16[96,6,1]{0,2,1:T(2,128)(2,1)S(1)}, bf16[96,6,1]{0,2,1:T(2,128)(2,1)S(1)}, u32[]{:S(2)}, u32[]{:S(2)}) collective-permute-start(bf16[96,6,1]{0,2,1:T(2,128)(2,1)S(1)} %get-tuple-element.54), channel_id=1, source_target_pairs={{0,1},{1,2},{2,3},{3,4},{4,5},{5,6},{6,7},{8,9},{9,10},{10,11},{11... | collective-permute-start | bytes 3464 | tf_op jit(solution)/shard_map/ppermute | solution.py:14
  166.0 13.1 %collective-permute-start.23 = (bf16[192,4,1]{0,2,1:T(2,128)(2,1)}, bf16[192,4,1]{0,2,1:T(2,128)(2,1)}, u32[]{:S(2)}, u32[]{:S(2)}) collective-permute-start(bf16[192,4,1]{0,2,1:T(2,128)(2,1)} %get-tuple-element.73), channel_id=1, source_target_pairs={{1,0},{2,1},{3,2},{4,3},{5,4},{6,5},{7,6},{9,8},{10,9},{11,10},{12... | collective-permute-start | bytes 4616 | tf_op jit(solution)/shard_map/ppermute | solution.py:15
  182.4 12.8 %collective-permute-start.25 = (bf16[192,1,32]{0,2,1:T(8,128)(2,1)S(1)}, bf16[192,1,32]{0,2,1:T(8,128)(2,1)S(1)}, u32[]{:S(2)}, u32[]{:S(2)}) collective-permute-start(bf16[192,1,32]{0,2,1:T(8,128)(2,1)S(1)} %get-tuple-element.26), channel_id=1, source_target_pairs={{8,0},{16,8},{24,16},{32,24},{40,32},{48,40},{56,48},{64,56},{72,6... | collective-permute-start | bytes 36872 | tf_op jit(solution)/shard_map/ppermute | solution.py:15
  186.4 8.8 %collective-permute-start.24 = (bf16[192,1,32]{0,2,1:T(8,128)(2,1)S(1)}, bf16[192,1,32]{0,2,1:T(8,128)(2,1)S(1)}, u32[]{:S(2)}, u32[]{:S(2)}) collective-permute-start(bf16[192,1,32]{0,2,1:T(8,128)(2,1)S(1)} %get-tuple-element.25), channel_id=1, source_target_pairs={{0,8},{8,16},{16,24},{24,32},{32,40},{40,48},{48,56},{56,64},{64,7... | collective-permute-start | bytes 36872 | tf_op jit(solution)/shard_map/ppermute | solution.py:14
  188.4 13.7 %collective-permute-start.33 = (bf16[384,1,16]{0,2,1:T(8,128)(2,1)S(1)}, bf16[384,1,16]{0,2,1:T(8,128)(2,1)S(1)}, u32[]{:S(2)}, u32[]{:S(2)}) collective-permute-start(bf16[384,1,16]{0,2,1:T(8,128)(2,1)S(1)} %get-tuple-element.71), channel_id=1, source_target_pairs={{8,0},{16,8},{24,16},{32,24},{40,32},{48,40},{56,48},{64,56},{72,6... | collective-permute-start | bytes 36872 | tf_op jit(solution)/shard_map/ppermute | solution.py:15
  193.3 8.9 %collective-permute-start.32 = (bf16[384,1,16]{0,2,1:T(8,128)(2,1)S(1)}, bf16[384,1,16]{0,2,1:T(8,128)(2,1)S(1)}, u32[]{:S(2)}, u32[]{:S(2)}) collective-permute-start(bf16[384,1,16]{0,2,1:T(8,128)(2,1)S(1)} %get-tuple-element.70), channel_id=1, source_target_pairs={{0,8},{8,16},{16,24},{24,32},{32,40},{40,48},{48,56},{56,64},{64,7... | collective-permute-start | bytes 36872 | tf_op jit(solution)/shard_map/ppermute | solution.py:14
  195.3 14.0 %collective-permute-start.27 = (bf16[192,6,1]{0,2,1:T(2,128)(2,1)S(1)}, bf16[192,6,1]{0,2,1:T(2,128)(2,1)S(1)}, u32[]{:S(2)}, u32[]{:S(2)}) collective-permute-start(bf16[192,6,1]{0,2,1:T(2,128)(2,1)S(1)} %get-tuple-element.16), channel_id=1, source_target_pairs={{1,0},{2,1},{3,2},{4,3},{5,4},{6,5},{7,6},{9,8},{10,9},{11,10},{12... | collective-permute-start | bytes 6920 | tf_op jit(solution)/shard_map/ppermute | solution.py:15
  200.2 9.1 %collective-permute-start.26 = (bf16[192,6,1]{0,2,1:T(2,128)(2,1)S(1)}, bf16[192,6,1]{0,2,1:T(2,128)(2,1)S(1)}, u32[]{:S(2)}, u32[]{:S(2)}) collective-permute-start(bf16[192,6,1]{0,2,1:T(2,128)(2,1)S(1)} %get-tuple-element.15), channel_id=1, source_target_pairs={{0,1},{1,2},{2,3},{3,4},{4,5},{5,6},{6,7},{8,9},{9,10},{10,11},{11... | collective-permute-start | bytes 6920 | tf_op jit(solution)/shard_map/ppermute | solution.py:14
  202.2 19.4 %collective-permute-start.35 = (bf16[384,4,1]{0,2,1:T(2,128)(2,1)S(1)}, bf16[384,4,1]{0,2,1:T(2,128)(2,1)S(1)}, u32[]{:S(2)}, u32[]{:S(2)}) collective-permute-start(bf16[384,4,1]{0,2,1:T(2,128)(2,1)S(1)} %get-tuple-element.39), channel_id=1, source_target_pairs={{1,0},{2,1},{3,2},{4,3},{5,4},{6,5},{7,6},{9,8},{10,9},{11,10},{12... | collective-permute-start | bytes 9224 | tf_op jit(solution)/shard_map/ppermute | solution.py:15
  207.3 14.3 %collective-permute-start.34 = (bf16[384,4,1]{0,2,1:T(2,128)(2,1)S(1)}, bf16[384,4,1]{0,2,1:T(2,128)(2,1)S(1)}, u32[]{:S(2)}, u32[]{:S(2)}) collective-permute-start(bf16[384,4,1]{0,2,1:T(2,128)(2,1)S(1)} %get-tuple-element.38), channel_id=1, source_target_pairs={{0,1},{1,2},{2,3},{3,4},{4,5},{5,6},{6,7},{8,9},{9,10},{10,11},{11... | collective-permute-start | bytes 9224 | tf_op jit(solution)/shard_map/ppermute | solution.py:14
  215.7 14.0 %collective-permute-start.29 = (bf16[96,1,32]{0,2,1:T(8,128)(2,1)S(1)}, bf16[96,1,32]{0,2,1:T(8,128)(2,1)S(1)}, u32[]{:S(2)}, u32[]{:S(2)}) collective-permute-start(bf16[96,1,32]{0,2,1:T(8,128)(2,1)S(1)} %get-tuple-element.61), channel_id=1, source_target_pairs={{8,0},{16,8},{24,16},{32,24},{40,32},{48,40},{56,48},{64,56},{72,6... | collective-permute-start | bytes 18440 | tf_op jit(solution)/shard_map/ppermute | solution.py:15
  219.7 10.0 %collective-permute-start.28 = (bf16[96,1,32]{0,2,1:T(8,128)(2,1)S(1)}, bf16[96,1,32]{0,2,1:T(8,128)(2,1)S(1)}, u32[]{:S(2)}, u32[]{:S(2)}) collective-permute-start(bf16[96,1,32]{0,2,1:T(8,128)(2,1)S(1)} %get-tuple-element.60), channel_id=1, source_target_pairs={{0,8},{8,16},{16,24},{24,32},{32,40},{40,48},{48,56},{56,64},{64,7... | collective-permute-start | bytes 18440 | tf_op jit(solution)/shard_map/ppermute | solution.py:14
  222.9 13.6 %collective-permute-start.37 = (bf16[192,1,16]{0,2,1:T(8,128)(2,1)S(1)}, bf16[192,1,16]{0,2,1:T(8,128)(2,1)S(1)}, u32[]{:S(2)}, u32[]{:S(2)}) collective-permute-start(bf16[192,1,16]{0,2,1:T(8,128)(2,1)S(1)} %get-tuple-element.83), channel_id=1, source_target_pairs={{8,0},{16,8},{24,16},{32,24},{40,32},{48,40},{56,48},{64,56},{72,6... | collective-permute-start | bytes 18440 | tf_op jit(solution)/shard_map/ppermute | solution.py:15
  229.7 14.5 %collective-permute-start.31 = (bf16[96,6,1]{0,2,1:T(2,128)(2,1)S(1)}, bf16[96,6,1]{0,2,1:T(2,128)(2,1)S(1)}, u32[]{:S(2)}, u32[]{:S(2)}) collective-permute-start(bf16[96,6,1]{0,2,1:T(2,128)(2,1)S(1)} %get-tuple-element.53), channel_id=1, source_target_pairs={{1,0},{2,1},{3,2},{4,3},{5,4},{6,5},{7,6},{9,8},{10,9},{11,10},{12... | collective-permute-start | bytes 3464 | tf_op jit(solution)/shard_map/ppermute | solution.py:15
  234.6 9.6 %collective-permute-start.30 = (bf16[96,6,1]{0,2,1:T(2,128)(2,1)S(1)}, bf16[96,6,1]{0,2,1:T(2,128)(2,1)S(1)}, u32[]{:S(2)}, u32[]{:S(2)}) collective-permute-start(bf16[96,6,1]{0,2,1:T(2,128)(2,1)S(1)} %get-tuple-element.52), channel_id=1, source_target_pairs={{0,1},{1,2},{2,3},{3,4},{4,5},{5,6},{6,7},{8,9},{9,10},{10,11},{11... | collective-permute-start | bytes 3464 | tf_op jit(solution)/shard_map/ppermute | solution.py:14
  237.1 12.9 %collective-permute-start.39 = (bf16[192,4,1]{0,2,1:T(2,128)(2,1)}, bf16[192,4,1]{0,2,1:T(2,128)(2,1)}, u32[]{:S(2)}, u32[]{:S(2)}) collective-permute-start(bf16[192,4,1]{0,2,1:T(2,128)(2,1)} %get-tuple-element.69), channel_id=1, source_target_pairs={{1,0},{2,1},{3,2},{4,3},{5,4},{6,5},{7,6},{9,8},{10,9},{11,10},{12... | collective-permute-start | bytes 4616 | tf_op jit(solution)/shard_map/ppermute | solution.py:15
  253.3 12.8 %collective-permute-start.41 = (bf16[192,1,32]{0,2,1:T(8,128)(2,1)S(1)}, bf16[192,1,32]{0,2,1:T(8,128)(2,1)S(1)}, u32[]{:S(2)}, u32[]{:S(2)}) collective-permute-start(bf16[192,1,32]{0,2,1:T(8,128)(2,1)S(1)} %get-tuple-element.24), channel_id=1, source_target_pairs={{8,0},{16,8},{24,16},{32,24},{40,32},{48,40},{56,48},{64,56},{72,6... | collective-permute-start | bytes 36872 | tf_op jit(solution)/shard_map/ppermute | solution.py:15
  257.4 8.8 %collective-permute-start.40 = (bf16[192,1,32]{0,2,1:T(8,128)(2,1)S(1)}, bf16[192,1,32]{0,2,1:T(8,128)(2,1)S(1)}, u32[]{:S(2)}, u32[]{:S(2)}) collective-permute-start(bf16[192,1,32]{0,2,1:T(8,128)(2,1)S(1)} %get-tuple-element.23), channel_id=1, source_target_pairs={{0,8},{8,16},{16,24},{24,32},{32,40},{40,48},{48,56},{56,64},{64,7... | collective-permute-start | bytes 36872 | tf_op jit(solution)/shard_map/ppermute | solution.py:14
  259.4 13.7 %collective-permute-start.49 = (bf16[384,1,16]{0,2,1:T(8,128)(2,1)S(1)}, bf16[384,1,16]{0,2,1:T(8,128)(2,1)S(1)}, u32[]{:S(2)}, u32[]{:S(2)}) collective-permute-start(bf16[384,1,16]{0,2,1:T(8,128)(2,1)S(1)} %get-tuple-element.67), channel_id=1, source_target_pairs={{8,0},{16,8},{24,16},{32,24},{40,32},{48,40},{56,48},{64,56},{72,6... | collective-permute-start | bytes 36872 | tf_op jit(solution)/shard_map/ppermute | solution.py:15
  264.2 8.9 %collective-permute-start.48 = (bf16[384,1,16]{0,2,1:T(8,128)(2,1)S(1)}, bf16[384,1,16]{0,2,1:T(8,128)(2,1)S(1)}, u32[]{:S(2)}, u32[]{:S(2)}) collective-permute-start(bf16[384,1,16]{0,2,1:T(8,128)(2,1)S(1)} %get-tuple-element.66), channel_id=1, source_target_pairs={{0,8},{8,16},{16,24},{24,32},{32,40},{40,48},{48,56},{56,64},{64,7... | collective-permute-start | bytes 36872 | tf_op jit(solution)/shard_map/ppermute | solution.py:14
  266.3 14.0 %collective-permute-start.43 = (bf16[192,6,1]{0,2,1:T(2,128)(2,1)S(1)}, bf16[192,6,1]{0,2,1:T(2,128)(2,1)S(1)}, u32[]{:S(2)}, u32[]{:S(2)}) collective-permute-start(bf16[192,6,1]{0,2,1:T(2,128)(2,1)S(1)} %get-tuple-element.12), channel_id=1, source_target_pairs={{1,0},{2,1},{3,2},{4,3},{5,4},{6,5},{7,6},{9,8},{10,9},{11,10},{12... | collective-permute-start | bytes 6920 | tf_op jit(solution)/shard_map/ppermute | solution.py:15
  271.1 9.1 %collective-permute-start.42 = (bf16[192,6,1]{0,2,1:T(2,128)(2,1)S(1)}, bf16[192,6,1]{0,2,1:T(2,128)(2,1)S(1)}, u32[]{:S(2)}, u32[]{:S(2)}) collective-permute-start(bf16[192,6,1]{0,2,1:T(2,128)(2,1)S(1)} %get-tuple-element.11), channel_id=1, source_target_pairs={{0,1},{1,2},{2,3},{3,4},{4,5},{5,6},{6,7},{8,9},{9,10},{10,11},{11... | collective-permute-start | bytes 6920 | tf_op jit(solution)/shard_map/ppermute | solution.py:14
  273.2 19.6 %collective-permute-start.51 = (bf16[384,4,1]{0,2,1:T(2,128)(2,1)S(1)}, bf16[384,4,1]{0,2,1:T(2,128)(2,1)S(1)}, u32[]{:S(2)}, u32[]{:S(2)}) collective-permute-start(bf16[384,4,1]{0,2,1:T(2,128)(2,1)S(1)} %get-tuple-element.35), channel_id=1, source_target_pairs={{1,0},{2,1},{3,2},{4,3},{5,4},{6,5},{7,6},{9,8},{10,9},{11,10},{12... | collective-permute-start | bytes 9224 | tf_op jit(solution)/shard_map/ppermute | solution.py:15
  278.3 14.5 %collective-permute-start.50 = (bf16[384,4,1]{0,2,1:T(2,128)(2,1)S(1)}, bf16[384,4,1]{0,2,1:T(2,128)(2,1)S(1)}, u32[]{:S(2)}, u32[]{:S(2)}) collective-permute-start(bf16[384,4,1]{0,2,1:T(2,128)(2,1)S(1)} %get-tuple-element.34), channel_id=1, source_target_pairs={{0,1},{1,2},{2,3},{3,4},{4,5},{5,6},{6,7},{8,9},{9,10},{10,11},{11... | collective-permute-start | bytes 9224 | tf_op jit(solution)/shard_map/ppermute | solution.py:14
  286.6 14.2 %collective-permute-start.45 = (bf16[96,1,32]{0,2,1:T(8,128)(2,1)S(1)}, bf16[96,1,32]{0,2,1:T(8,128)(2,1)S(1)}, u32[]{:S(2)}, u32[]{:S(2)}) collective-permute-start(bf16[96,1,32]{0,2,1:T(8,128)(2,1)S(1)} %get-tuple-element.59), channel_id=1, source_target_pairs={{8,0},{16,8},{24,16},{32,24},{40,32},{48,40},{56,48},{64,56},{72,6... | collective-permute-start | bytes 18440 | tf_op jit(solution)/shard_map/ppermute | solution.py:15
  290.7 10.2 %collective-permute-start.44 = (bf16[96,1,32]{0,2,1:T(8,128)(2,1)S(1)}, bf16[96,1,32]{0,2,1:T(8,128)(2,1)S(1)}, u32[]{:S(2)}, u32[]{:S(2)}) collective-permute-start(bf16[96,1,32]{0,2,1:T(8,128)(2,1)S(1)} %get-tuple-element.58), channel_id=1, source_target_pairs={{0,8},{8,16},{16,24},{24,32},{32,40},{40,48},{48,56},{56,64},{64,7... | collective-permute-start | bytes 18440 | tf_op jit(solution)/shard_map/ppermute | solution.py:14
  294.1 13.6 %collective-permute-start.53 = (bf16[192,1,16]{0,2,1:T(8,128)(2,1)S(1)}, bf16[192,1,16]{0,2,1:T(8,128)(2,1)S(1)}, u32[]{:S(2)}, u32[]{:S(2)}) collective-permute-start(bf16[192,1,16]{0,2,1:T(8,128)(2,1)S(1)} %get-tuple-element.81), channel_id=1, source_target_pairs={{8,0},{16,8},{24,16},{32,24},{40,32},{48,40},{56,48},{64,56},{72,6... | collective-permute-start | bytes 18440 | tf_op jit(solution)/shard_map/ppermute | solution.py:15
  300.9 14.5 %collective-permute-start.47 = (bf16[96,6,1]{0,2,1:T(2,128)(2,1)S(1)}, bf16[96,6,1]{0,2,1:T(2,128)(2,1)S(1)}, u32[]{:S(2)}, u32[]{:S(2)}) collective-permute-start(bf16[96,6,1]{0,2,1:T(2,128)(2,1)S(1)} %get-tuple-element.51), channel_id=1, source_target_pairs={{1,0},{2,1},{3,2},{4,3},{5,4},{6,5},{7,6},{9,8},{10,9},{11,10},{12... | collective-permute-start | bytes 3464 | tf_op jit(solution)/shard_map/ppermute | solution.py:15
  305.7 9.6 %collective-permute-start.46 = (bf16[96,6,1]{0,2,1:T(2,128)(2,1)S(1)}, bf16[96,6,1]{0,2,1:T(2,128)(2,1)S(1)}, u32[]{:S(2)}, u32[]{:S(2)}) collective-permute-start(bf16[96,6,1]{0,2,1:T(2,128)(2,1)S(1)} %get-tuple-element.50), channel_id=1, source_target_pairs={{0,1},{1,2},{2,3},{3,4},{4,5},{5,6},{6,7},{8,9},{9,10},{10,11},{11... | collective-permute-start | bytes 3464 | tf_op jit(solution)/shard_map/ppermute | solution.py:14
  308.3 10.8 %collective-permute-start.55 = (bf16[192,4,1]{0,2,1:T(2,128)(2,1)}, bf16[192,4,1]{0,2,1:T(2,128)(2,1)}, u32[]{:S(2)}, u32[]{:S(2)}) collective-permute-start(bf16[192,4,1]{0,2,1:T(2,128)(2,1)} %get-tuple-element.65), channel_id=1, source_target_pairs={{1,0},{2,1},{3,2},{4,3},{5,4},{6,5},{7,6},{9,8},{10,9},{11,10},{12... | collective-permute-start | bytes 4616 | tf_op jit(solution)/shard_map/ppermute | solution.py:15
  (69 other events, 842.6 us)
Sparse Core Ops, SparseCore 0:
  9.5 63.8 all-gather.1
where the time goes:
time: 384 us; the launch traced here: 381 us
  starting transfers between devices  200 us (52%)
  blocking collectives  58.4 us (15%)
  local copies, waits for them, and re-layouts  55.1 us (14%)
  waiting for transfers between devices  20.1 us (5%)
  matrix products  18.9 us (5%)
  between operations  16.4 us (4%)
  other arithmetic  12.2 us (3%)
    ppermute x32, starting transfers between devices, extended(): after = lax.ppermute(leading, axis, down)  131 us
    ppermute x32, starting transfers between devices, extended(): before = lax.ppermute(last, axis, up)  69.5 us
    all_gather x1, blocking collectives, local(): lax.all_gather(weight_level4, 'ha', axis=0, tiled=True)  39.3 us
    ppermute x32, waiting for transfers between devices, extended(): before = lax.ppermute(last, axis, up)  19.9 us
    slice x7, local copies, waits for them, and re-layouts, apply_rows(): matrix = weight[row_start:row_start + row_count].reshape(row_count, -1)  19 us
    dot_general x15, matrix products, apply_rows(): jnp.dot(matrix, unfold(padded, tile_rows, tile_cols), preferred_element_t...  17.8 us
    reshape x8, local copies, waits for them, and re-layouts, unfold(): return stacked.reshape(9 * padded.shape[0], tile_rows * tile_cols)  15.5 us
    unnamed x221, local copies, waits for them, and re-layouts  10.5 us
  transfers between devices with their start and end apart: 65, of which 6 were waited for; matrix products, arithmetic and copies ran while one was open for 15% of the time, Pallas kernels for 0%

commit v1 on v0

v1 whole, which is shorter than its diff:
```python
import jax
import jax.numpy as jnp
from jax import lax
from jax.experimental import pallas as pl
from jax.experimental.pallas import tpu as pltpu
from jax.sharding import PartitionSpec as P

MESH = pl.DeviceIdType.MESH
BF16 = jnp.bfloat16
F32 = jnp.float32

NS, NH, NW = 4, 16, 8
LEADS = 4

Z3, Z4, X3, X4 = 1, 1, 5, 3
H3R, H4R = 288, 144
WIN3, WIN4 = 48, 32
ZR = Z3 * H3R + Z4 * H4R
XR = X3 * H3R + X4 * H4R
ZWIN = Z3 * WIN3 + Z4 * WIN4
XWIN = X3 * WIN3 + X4 * WIN4
XBASE = NW * ZR
WROWS = NW * ZR + NS * XR
SROWS = NW * ZWIN + NS * XWIN

NEIGHBOURS = [(dy, dx) for dy in (-1, 0, 1) for dx in (-1, 0, 1) if (dy, dx) != (0, 0)]


def off3(kb):
    if kb < NW * Z3:
        return (kb // Z3) * ZR + (kb % Z3) * H3R
    kb -= NW * Z3
    return XBASE + (kb // X3) * XR + (kb % X3) * H3R


def off4(kb):
    if kb < NW * Z4:
        return (kb // Z4) * ZR + Z3 * H3R + (kb % Z4) * H4R
    kb -= NW * Z4
    return XBASE + (kb // X4) * XR + X3 * H3R + (kb % X4) * H4R


def nt(a, b):
    return lax.dot_general(a, b, (((1,), (1,)), ((), ())), preferred_element_type=F32)


def kernel(
    ws_ref, x_ref, i3_ref, i4_ref, lm_ref, ro_ref, up_ref, o_ref,
    s1, wb, xb, s3, s4, j3, j4, pt, po,
    ss1, rs1, ssz, rsz, ssx, rsx, fsz, frz, fsx, frx,
    sxa, rxa, sxb, rxb, si3, ri3, si4, ri4, st3, rt3, st4, rt4, so, ro_sem,
):
    s = lax.axis_index("section")
    h = lax.axis_index("ha")
    w = lax.axis_index("wa")
    core = lax.rem(h, 2)
    half = h // 8
    slot = lax.rem(h, 8)
    sister = h + 1 - 2 * core

    xb[...] = jnp.zeros_like(xb)
    s3[...] = jnp.zeros_like(s3)
    s4[...] = jnp.zeros_like(s4)
    s3[0, 2:4, 16:32, :] = i3_ref[...]
    s4[0, 2:6, 16:48, :] = i4_ref[...]
    xb[pl.ds(s, 1), 2:4, 16:32, :] = x_ref[pl.ds(s, 1)]

    barrier = pltpu.get_barrier_semaphore()
    count = 0
    for d in range(1, NH):
        pl.semaphore_signal(barrier, inc=1, device_id={"ha": lax.rem(h + d, NH)}, device_id_type=MESH)
        count += 1
    for d in range(1, NW):
        pl.semaphore_signal(barrier, inc=1, device_id={"wa": lax.rem(w + d, NW)}, device_id_type=MESH)
        count += 1
    for d in range(1, NS):
        pl.semaphore_signal(barrier, inc=1, device_id={"section": lax.rem(s + d, NS)}, device_id_type=MESH)
        count += 1
    for dy in (1, NH - 1):
        for dx in (1, NW - 1):
            pl.semaphore_signal(
                barrier, inc=1,
                device_id={"ha": lax.rem(h + dy, NH), "wa": lax.rem(w + dx, NW)},
                device_id_type=MESH,
            )
            count += 1
    pl.semaphore_wait(barrier, count)

    def remote(src, dst, send, recv, **where):
        return pltpu.make_async_remote_copy(
            src_ref=src, dst_ref=dst, send_sem=send, recv_sem=recv, device_id=where, device_id_type=MESH
        )

    def exists(dy, dx):
        hh, ww = h + dy, w + dx
        ok = None
        for cond in ([hh >= 0] if dy < 0 else [hh < NH] if dy > 0 else []) + (
            [ww >= 0] if dx < 0 else [ww < NW] if dx > 0 else []
        ):
            ok = cond if ok is None else jnp.logical_and(ok, cond)
        return ok

    def each_neighbour(make, action):
        for n, (dy, dx) in enumerate(NEIGHBOURS):
            @pl.when(exists(dy, dx))
            def _(n=n, dy=dy, dx=dx):
                getattr(make(n, dy, dx), action)()

    def copy_x(n, dy, dx):
        return remote(
            xb.at[:, 2:4, 16:32, :],
            xb.at[:, 2 - 2 * dy : 4 - 2 * dy, 16 - 16 * dx : 32 - 16 * dx, :],
            sxb.at[n], rxb.at[n], ha=h + dy, wa=w + dx,
        )

    def copy_3(src, t, ss, rs):
        def make(n, dy, dx):
            return remote(
                src, s3.at[t, 2 - 2 * dy : 4 - 2 * dy, 16 - 16 * dx : 32 - 16 * dx, :],
                ss.at[n], rs.at[n], ha=h + dy, wa=w + dx,
            )
        return make

    def copy_4(src, row0, col0, t, ss, rs):
        def make(n, dy, dx):
            r0, r1 = {-1: (0, 2), 0: (0, 4), 1: (2, 4)}[dy]
            c0, c1 = {-1: (0, 16), 0: (0, 32), 1: (16, 32)}[dx]
            q0, q1 = {-1: (6, 8), 0: (2, 6), 1: (0, 2)}[dy]
            d0, d1 = {-1: (48, 64), 0: (16, 48), 1: (0, 16)}[dx]
            return remote(
                src.at[row0 + r0 : row0 + r1, col0 + c0 : col0 + c1, :],
                s4.at[t, q0:q1, d0:d1, :], ss.at[n], rs.at[n], ha=h + dy, wa=w + dx,
            )
        return make

    def arrive(make):
        def incoming(n, dy, dx):
            return make(NEIGHBOURS.index((-dy, -dx)), -dy, -dx)
        for n, (dy, dx) in enumerate(NEIGHBOURS):
            @pl.when(exists(dy, dx))
            def _(n=n, dy=dy, dx=dx):
                incoming(n, dy, dx).wait_recv()

    def to_column(y, part):
        lo, n, dst = ((w * ZWIN, ZWIN, 0), (NW * ZWIN + s * XWIN, XWIN, ZWIN))[part]
        return remote(
            ws_ref.at[pl.ds(pl.multiple_of(lo, 16), n), :],
            s1.at[slot, dst : dst + n, :],
            ss1.at[part, y], rs1.at[part, slot], ha=2 * y + half,
        )

    def from_column(i, part):
        n, dst = ((ZWIN, 0), (XWIN, ZWIN))[part]
        return remote(
            ws_ref.at[pl.ds(0, n), :], s1.at[i, dst : dst + n, :],
            ss1.at[part, i], rs1.at[part, i], ha=sister,
        )

    def column(action, part):
        for y in range(8):
            @pl.when(2 * y + half != h)
            def _(y=y):
                getattr(to_column(y, part), action)()

    @pl.when(half == core)
    def _():
        s1[pl.ds(slot, 1), 0:ZWIN, :] = ws_ref[pl.ds(pl.multiple_of(w * ZWIN, 16), ZWIN), :][None]
        s1[pl.ds(slot, 1), ZWIN : ZWIN + XWIN, :] = ws_ref[
            pl.ds(pl.multiple_of(NW * ZWIN + s * XWIN, 16), XWIN), :
        ][None]

    def to_member(d):
        m = lax.rem(s + d, NS)
        return remote(x_ref.at[m], xb.at[s, 2:4, 16:32, :], sxa.at[d], rxa.at[d], section=m)

    def from_lead(d):
        src = lax.rem(s + NS - d, NS)
        return remote(x_ref.at[0], xb.at[src, 2:4, 16:32, :], sxa.at[d], rxa.at[d], section=src)

    for d in range(1, NS):
        to_member(d).start()
    column("start", 1)
    column("start", 0)
    init3 = copy_3(i3_ref, 0, si3, ri3)
    init4 = copy_4(i4_ref, 0, 0, 0, si4, ri4)
    each_neighbour(init3, "start")
    each_neighbour(init4, "start")
    for d in range(1, NS):
        from_lead(d).wait_recv()
    each_neighbour(copy_x, "start")

    def wait_column(part):
        for i in range(8):
            @pl.when(8 * core + i != h)
            def _(i=i):
                from_column(i, part).wait_recv()

    def merged3(at):
        tiles = []
        for group in range(2):
            part = lambda i, j: s1[4 * group + i, at + 16 * j : at + 16 * j + 16, :]
            tiles += [
                part(0, 0), part(0, 1), part(0, 2) + part(1, 0), part(1, 1), part(1, 2) + part(2, 0),
                part(2, 1), part(2, 2) + part(3, 0), part(3, 1), part(3, 2),
            ]
        return jnp.concatenate(tiles, 0)

    def merged4(at):
        part = lambda i, j: s1[i, at + 16 * j : at + 16 * j + 16, :]
        tiles = [part(0, 0)] + [part(i, 1) + part(i + 1, 0) for i in range(7)] + [part(7, 1)]
        return jnp.concatenate(tiles, 0)

    def place(base, rows, value):
        wb[pl.ds(core, 1), pl.ds(pl.multiple_of(base, 16), rows), :] = value[None]

    def z_piece(c, z):
        return wb.at[c, pl.ds(pl.multiple_of(z * ZR, 16), ZR), :]

    def x_piece(c, x):
        return wb.at[c, pl.ds(pl.multiple_of(XBASE + x * XR, 16), XR), :]

    def z_copy(d):
        return remote(z_piece(core, w), z_piece(core, w), ssz.at[d], rsz.at[d], wa=lax.rem(w + d, NW))

    def z_from(d):
        z = lax.rem(w + NW - d, NW)
        return remote(z_piece(core, z), z_piece(core, z), ssz.at[d], rsz.at[d], wa=z)

    def x_copy(d):
        return remote(x_piece(core, s), x_piece(core, s), ssx.at[d], rsx.at[d], section=lax.rem(s + d, NS))

    def x_from(d):
        x = lax.rem(s + NS - d, NS)
        return remote(x_piece(core, x), x_piece(core, x), ssx.at[d], rsx.at[d], section=x)

    def z_share(d, c):
        z = lax.rem(w + NW - d, NW)
        return remote(z_piece(c, z), z_piece(c, z), fsz.at[d], frz.at[d], ha=sister)

    def x_share(d, c):
        x = lax.rem(s + NS - d, NS)
        return remote(x_piece(c, x), x_piece(c, x), fsx.at[d], frx.at[d], ha=sister)

    x_order = (1, 3, 2)
    z_order = (1, 7, 2, 6, 3, 5, 4)
    wait_column(1)
    for j in range(X3):
        place(XBASE + s * XR + j * H3R, H3R, merged3(ZWIN + j * WIN3))
    for j in range(X4):
        place(XBASE + s * XR + X3 * H3R + j * H4R, H4R, merged4(ZWIN + X3 * WIN3 + j * WIN4))
    for d in x_order:
        x_copy(d).start()
    x_share(0, core).start()
    wait_column(0)
    for j in range(Z3):
        place(w * ZR + j * H3R, H3R, merged3(j * WIN3))
    for j in range(Z4):
        place(w * ZR + Z3 * H3R + j * H4R, H4R, merged4(Z3 * WIN3 + j * WIN4))
    for d in z_order:
        z_copy(d).start()
    z_share(0, core).start()
    for d in x_order[:2]:
        x_from(d).wait_recv()
        x_share(d, core).start()
    for d in z_order:
        z_from(d).wait_recv()
        z_share(d, core).start()
    for d in x_order[2:]:
        x_from(d).wait_recv()
        x_share(d, core).start()
    arrive(init3)
    arrive(init4)
    arrive(copy_x)
    for d in range(NW):
        z_share(d, 1 - core).wait_recv()
    for d in range(NS):
        x_share(d, 1 - core).wait_recv()

    def rows3(kb, c, lo, hi):
        return wb[c, off3(kb) + lo : off3(kb) + hi, :]

    def rows4(kb, c, lo, hi):
        return wb[c, off4(kb) + lo : off4(kb) + hi, :]

    def gates3(a):
        blocks = []
        for kb in range(9 * a, 9 * a + 9):
            blocks.append(jnp.concatenate([
                rows3(kb, 0, 0, 192), rows3(kb, 0, 128, 192),
                rows3(kb, 0, 192, 288), rows3(kb, 1, 0, 32), rows3(kb, 1, 32, 96), rows3(kb, 1, 32, 96),
            ], 0))
        return jnp.concatenate(blocks, 1)

    def cand3(a):
        zero = jnp.zeros((64, 128), BF16)
        blocks = [
            jnp.concatenate([rows3(kb, 1, 96, 224), zero, rows3(kb, 1, 224, 288)], 0)
            for kb in range(9 * a, 9 * a + 9)
        ]
        return jnp.concatenate(blocks, 1)

    def gates4(a):
        blocks = []
        for kb in range(6 * a, 6 * a + 6):
            blocks.append(jnp.concatenate([
                rows4(kb, 0, 0, 96), rows4(kb, 0, 0, 32),
                rows4(kb, 0, 96, 144), rows4(kb, 1, 0, 48), rows4(kb, 0, 0, 32),
            ], 0))
        return jnp.concatenate(blocks, 1)

    def cand4(a):
        zero = jnp.zeros((32, 128), BF16)
        blocks = [jnp.concatenate([rows4(kb, 1, 48, 144), zero], 0) for kb in range(6 * a, 6 * a + 6)]
        return jnp.concatenate(blocks, 1)

    def taps(ref, r0, r1, c0, c1):
        return jnp.concatenate([ref[r0:r1, c0 + b - 1 : c1 + b - 1, :].astype(BF16) for b in range(3)], 2)

    def level3(t):
        x = xb[t].astype(F32)
        p = s3[t].astype(F32)
        j3[:, :, 0:128] = x[:, :, :128]
        j3[:, :, 128:256] = p[:, :, :128]
        j3[:, :, 256:384] = x[:, :, 128:] + p[:, :, 128:]
        u = taps(j3, 0, 6, 8, 40)
        sums = sum(nt(u[a : a + 4].reshape(128, 1152), gates3(a)) for a in range(3))
        reset = jax.nn.sigmoid(sums[:, :256]).reshape(4, 32, 256)
        update = jax.nn.sigmoid(sums[:, 256:]).reshape(4, 32, 256)[1:3, 8:24, :]
        gated = reset * p[1:5, 8:40, :]
        j3[1:5, 8:40, 128:256] = gated[:, :, :128]
        j3[1:5, 8:40, 256:384] = x[1:5, 8:40, 128:] + gated[:, :, 128:]
        v = taps(j3, 1, 5, 16, 32)
        fresh = sum(nt(v[a : a + 2].reshape(32, 1152), cand3(a)) for a in range(3))
        fresh = jnp.maximum(fresh, 0.0).reshape(2, 16, 256)
        prior = p[2:4, 16:32, :]
        s3[t + 1, 2:4, 16:32, :] = (update * prior + (1.0 - update) * fresh).astype(BF16)

    def level4(t):
        coarse = s3[t + 1, 1:5].astype(F32)[:, 8:40, :].astype(BF16).reshape(128, 256)
        lift = nt(coarse, lm_ref[...]).astype(BF16)
        lifted = jnp.dot(up_ref[...], lift, preferred_element_type=F32).reshape(4, 64, 128)
        p = s4[t].astype(F32)
        for i in range(8):
            j4[i, :, 0:128] = lifted[i // 2]
        j4[:, :, 128:256] = p
        u = taps(j4, 0, 8, 8, 56)
        sums = sum(nt(u[a : a + 6].reshape(288, 768), gates4(a)) for a in range(3))
        reset = jax.nn.sigmoid(sums[:, :128]).reshape(6, 48, 128)
        update = jax.nn.sigmoid(sums[:, 128:]).reshape(6, 48, 128)[1:5, 8:40, :]
        j4[1:7, 8:56, 128:256] = reset * p[1:7, 8:56, :]
        v = taps(j4, 1, 7, 16, 48)
        fresh = sum(nt(v[a : a + 4].reshape(128, 768), cand4(a)) for a in range(3))
        fresh = jnp.maximum(fresh, 0.0).reshape(4, 32, 128)
        prior = p[2:6, 16:48, :]
        state = (update * prior + (1.0 - update) * fresh).astype(BF16)
        if t < LEADS - 1:
            s4[t + 1, 2:6, 16:48, :] = state
        pt[t] = nt(ro_ref[...], state.reshape(128, 128))

        @pl.when(s == t)
        def _():
            po[t] = pt[t]

        @pl.when(s != t)
        def _():
            to_lead(t).start()

    def to_lead(t):
        return remote(pt.at[t], po.at[s], so.at[t], ro_sem.at[s], section=t)

    def from_member(m):
        return remote(pt.at[0], po.at[m], so.at[0], ro_sem.at[m], section=m)

    def exchange3(t):
        return copy_3(s3.at[t + 1, 2:4, 16:32, :], t + 1, st3.at[t], rt3.at[t])

    def exchange4(t):
        return copy_4(s4.at[t + 1], 2, 16, t + 1, st4.at[t], rt4.at[t])

    level3(0)
    each_neighbour(exchange3(0), "start")
    for t in range(LEADS):
        arrive(exchange3(t))
        if t + 1 < LEADS:
            level3(t + 1)
            each_neighbour(exchange3(t + 1), "start")
        if t > 0:
            arrive(exchange4(t - 1))
        level4(t)
        if t + 1 < LEADS:
            each_neighbour(exchange4(t), "start")

    for m in range(NS):
        @pl.when(s != m)
        def _(m=m):
            from_member(m).wait_recv()
    o_ref[...] = po[...]

    for d in range(1, NS):
        to_member(d).wait_send()
        x_copy(d).wait_send()
    for d in range(1, NW):
        z_copy(d).wait_send()
    for d in range(NW):
        z_share(d, core).wait_send()
    for d in range(NS):
        x_share(d, core).wait_send()
    column("wait_send", 0)
    column("wait_send", 1)
    each_neighbour(init3, "wait_send")
    each_neighbour(init4, "wait_send")
    each_neighbour(copy_x, "wait_send")
    for t in range(LEADS):
        each_neighbour(exchange3(t), "wait_send")
        if t + 1 < LEADS:
            each_neighbour(exchange4(t), "wait_send")
    for t in range(LEADS):
        @pl.when(s != t)
        def _(t=t):
            to_lead(t).wait_send()


def shard_windows(weight_level3, weight_level4):
    h = lax.axis_index("ha")
    w3 = weight_level3
    joint = jnp.stack(
        [w3[:, :, :128], w3[:, :, 192:320], jnp.concatenate([w3[:, :, 128:192], w3[:, :, 320:]], 2)], 2
    )
    blocks3 = joint.transpose(1, 2, 0, 3).reshape(27, 36, 128)
    wide3 = lax.dynamic_update_slice(
        jnp.zeros((NW * Z3 + NS * X3, WIN3, 128), BF16), blocks3, (0, 4 * lax.rem(h, 4), 0)
    )
    w4 = jnp.pad(weight_level4.reshape(18, 9, 2, 96), ((0, 0), (0, 0), (0, 0), (0, 32)))
    blocks4 = w4.transpose(1, 2, 0, 3).reshape(18, 18, 128)
    wide4 = lax.dynamic_update_slice(
        jnp.zeros((NW * Z4 + NS * X4, WIN4, 128), BF16), blocks4, (0, 2 * lax.rem(h, 8), 0)
    )
    def pieces(start3, n3, start4, n4, count):
        a = wide3[start3 : start3 + n3 * count].reshape(count, n3 * WIN3, 128)
        b = wide4[start4 : start4 + n4 * count].reshape(count, n4 * WIN4, 128)
        return jnp.concatenate([a, b], 1).reshape(-1, 128)
    return jnp.concatenate(
        [pieces(0, Z3, 0, Z4, NW), pieces(NW * Z3, X3, NW * Z4, X4, NS)], 0
    )


def state_lanes(v):
    gap = jnp.zeros(v.shape[:-1] + (64,), v.dtype)
    return jnp.concatenate([v[..., :128], gap, v[..., 128:]], -1)


def local(coarse_inputs, init_level3, init_level4, weight_level3, weight_level4, lift_map, readout):
    ws = shard_windows(weight_level3, weight_level4)
    x = jnp.pad(coarse_inputs[0].transpose(0, 2, 3, 1), ((0, 0), (0, 0), (0, 0), (0, 64)))
    i3 = state_lanes(init_level3.transpose(1, 2, 0))
    i4 = jnp.pad(init_level4.transpose(1, 2, 0), ((0, 0), (0, 0), (0, 32)))
    lm = jnp.pad(state_lanes(lift_map), ((0, 32), (0, 0)))
    ro = jnp.pad(readout, ((0, 0), (0, 32)))
    fine = jnp.arange(256)
    up = ((fine // 64) * 32 + (fine % 64) // 2)[:, None] == jnp.arange(128)[None, :]
    vmem = pl.BlockSpec(memory_space=pltpu.VMEM)
    dma = pltpu.SemaphoreType.DMA
    fields = pl.pallas_call(
        kernel,
        out_shape=jax.ShapeDtypeStruct((4, 16, 128), F32),
        in_specs=[vmem] * 7,
        out_specs=vmem,
        scratch_shapes=[
            pltpu.VMEM((8, ZWIN + XWIN, 128), BF16),
            pltpu.VMEM((2, WROWS, 128), BF16),
            pltpu.VMEM((4, 6, 48, 256), BF16),
            pltpu.VMEM((5, 6, 48, 256), BF16),
            pltpu.VMEM((4, 8, 64, 128), BF16),
            pltpu.VMEM((6, 48, 384), F32),
            pltpu.VMEM((8, 64, 256), F32),
            pltpu.VMEM((4, 16, 128), F32),
            pltpu.VMEM((4, 16, 128), F32),
            dma((2, 8)), dma((2, 8)),
            dma((NW,)), dma((NW,)), dma((NS,)), dma((NS,)),
            dma((NW,)), dma((NW,)), dma((NS,)), dma((NS,)),
            dma((NS,)), dma((NS,)), dma((8,)), dma((8,)),
            dma((8,)), dma((8,)), dma((8,)), dma((8,)),
            dma((4, 8)), dma((4, 8)), dma((4, 8)), dma((4, 8)),
            dma((4,)), dma((4,)),
        ],
        compiler_params=pltpu.CompilerParams(
            collective_id=0, has_side_effects=True, vmem_limit_bytes=40 << 20
        ),
        name="nowcast",
    )(ws, x, i3, i4, lm, ro, up.astype(BF16))
    return fields.reshape(1, 4, 16, 4, 32)


def solution(mesh):
    return jax.shard_map(
        local,
        mesh=mesh,
        in_specs=(
            P("section", None, None, "ha", "wa"),
            P(None, "ha", "wa"),
            P(None, "ha", "wa"),
            P("ha", None, None),
            P("ha", None, None),
            P(),
            P(),
        ),
        out_specs=P("section", None, None, "ha", "wa"),
        check_vma=False,
    )
```

time: 384 us -> 101 us (0.26)
  the two profiles are of different devices: /device:TPU:288 before, /device:TPU:6 now
where the time goes in v1:
time: 101 us; the launch traced here: 99.1 us
  Pallas kernels  88.7 us (88%)
  local copies, waits for them, and re-layouts  9.69 us (10%)
    pallas_call x1, Pallas kernels, local(): pl.pallas_call(kernel, out_shape=jax.ShapeDtypeStruct((4, 16, 128), F32),...  88.7 us
    unnamed x12, local copies, waits for them, and re-layouts  3.66 us
    dynamic_update_slice x1, local copies, waits for them, and re-layouts, shard_windows(): lax.dynamic_update_slice(jnp.zeros((NW * Z3 + NS * X3, WIN3, 128), BF16),...  2.59 us

profile of v1, /device:TPU:6, one launch (start us, length us, event | category | flops | bytes accessed | tf_op | source)
XLA Modules:
  0.0 99.1 jit_solution(10551678159302660973)
XLA Ops:
  0.0 0.0 copy-start
  0.0 1.1 %fusion.5 = (bf16[36,9,64]{2,0,1:T(8,128)(2,1)S(1)}, bf16[36,9,64]{2,0,1:T(8,128)(2,1)S(1)}) fusion(bf16[36,9,384]{2,0,1:T(8,128)(2,1)} %param.10), kind=kLoop, calls=%fused_computation.25 | loop fusion | bytes 165888 | tf_op jit(solution)/shard_map/slice | solution.py:427
  1.1 0.0 copy-done
  1.1 0.1 slice_bitcast_fusion.1
  1.3 2.6 %dynamic_update_slice.6 = bf16[28,48,128]{2,1,0:T(8,128)(2,1)S(1)} dynamic-update-slice(bf16[28,48,128]{2,1,0:T(8,128)(2,1)S(1)} %broadcast_in_dim.14, bf16[27,36,128]{2,1,0:T(8,128)(2,1)S(1)} %bitcast.24, s32[]{:T(128)} %constant.54.clone.1, s32[]{:T(128)S(6)} %select_n.33, s32[]{:T(128)} %constant.54.clone.1) | dynamic-update-slice | bytes 497668 | tf_op jit(solution)/shard_map/dynamic_update_slice | solution.py:430
  3.9 0.0 copy-start.1
  3.9 0.9 copy-done.1
  4.8 0.2 reshape.62
  5.0 0.1 pad_bitcast_fusion
  5.1 0.4 dynamic_update_slice.7
  5.7 0.0 copy-start.4
  5.7 0.7 copy-done.4
  6.4 0.1 pad_maximum_fusion.5.i3_ref
  6.5 0.0 slice-start
  6.5 0.0 slice-start.1
  6.5 0.7 slice-done
  7.2 0.0 slice-done.1
  7.2 0.1 pad_maximum_fusion.4
  7.3 0.0 copy-start.2
  7.4 0.1 fusion.up_ref
  7.5 0.7 copy-done.2
  8.2 0.0 copy-start.3
  8.2 0.7 copy-done.3
  8.9 0.0 copy-start.5
  8.9 0.7 copy-done.5
  9.6 88.7 %nowcast.1 = f32[4,16,128]{2,1,0:T(8,128)S(1)} custom-call(bf16[1984,128]{1,0:T(8,128)(2,1)S(1)} %pad_maximum_fusion.ws_ref, bf16[4,2,16,256]{3,2,1,0:T(8,128)(2,1)S(1)} %pad.21.x_ref, bf16[2,16,256]{2,1,0:T(8,128)(2,1)S(1)} %pad_maximum_fusion.5.i3_ref, bf16[4,32,128]{2,1,0:T(8,128)(2,1)S(1)} %pad.22.i4_ref, bf16[128,256]{1,0:T(8,128)(2,1)S(1)} %pad.23.lm_ref, ...), custom_call_target="tpu_custom_call" | custom-call | tf_op jit(solution)/shard_map/nowcast/pallas_call | solution.py:463
  98.3 0.8 reshape.68
  (20 shorter events, 0.3 us)
Async XLA Ops:
  0.0 1.1 %copy-start = (bf16[36,9,384]{2,0,1:T(8,128)(2,1)S(1)}, bf16[36,9,384]{2,0,1:T(8,128)(2,1)}, u32[]{:S(2)}) copy-start(bf16[36,9,384]{2,0,1:T(8,128)(2,1)} %param.10) | copy-start | bytes 746500
  3.9 0.9 copy-start.1
  5.7 0.7 copy-start.4
  6.5 0.7 slice-start
  6.5 0.8 slice-start.1
  7.3 0.8 copy-start.2
  8.2 0.8 copy-start.3
  8.9 0.7 copy-start.5

commit v2 on v0

v2 whole, which is shorter than its diff:
```python
import jax
import jax.numpy as jnp
from jax import lax
from jax.experimental import pallas as pl
from jax.experimental.pallas import tpu as pltpu
from jax.sharding import PartitionSpec as P

MESH = pl.DeviceIdType.MESH
BF16 = jnp.bfloat16
F32 = jnp.float32

NS, NH, NW = 4, 16, 8
LEADS = 4

X3, X4 = 5, 3
K3, K4 = 8 + NS * X3, 8 + NS * X4
H3R, H4R = 288, 144
WIN3, WIN4 = 80, 48

CHUNKS = [(3, 1, 1), (3, 2, 1), (3, 0, 1), (3, 3, 2), (3, 5, 1), (4, 1, 3), (4, 0, 1)]
CH3, CH4 = range(5), range(5, 7)

NEIGHBOURS = [(dy, dx) for dy in (-1, 0, 1) for dx in (-1, 0, 1) if (dy, dx) != (0, 0)]
X_ORDER = (1, 3, 2)
Z_ORDER = (1, 7, 2, 6, 3, 5, 4)


def nt(a, b):
    return lax.dot_general(a, b, (((1,), (1,)), ((), ())), preferred_element_type=F32)


def kernel(
    x_ref, i3_ref, i4_ref, w3_ref, w4_ref, lm_ref, ro_ref, o_ref,
    i3v, i4v, lmv, rov, own3, own4, sis3, sis4, cw3, cw4, s13, s14, wb3, wb4,
    xb, s3, s4, j3, j4, tmp, lm, ro, up, pt, po,
    load_sem, raw_s, raw_r, col_s, col_r, x_s, x_r, z_s, z_r, f_s, f_r,
    xa_s, xa_r, xn_s, xn_r, n3_s, n3_r, n4_s, n4_r, out_s, out_r,
):
    s = lax.axis_index("section")
    h = lax.axis_index("ha")
    w = lax.axis_index("wa")
    core = lax.rem(h, 2)
    y = h // 2
    sister = h + 1 - 2 * core
    half = y // 4

    def remote(src, dst, send, recv, **where):
        return pltpu.make_async_remote_copy(
            src_ref=src, dst_ref=dst, send_sem=send, recv_sem=recv, device_id=where, device_id_type=MESH
        )

    def wait_bytes(view, sem):
        pltpu.make_async_copy(view, view, sem).wait()

    xb[0] = jnp.zeros(xb.shape[1:], BF16)
    s3[0:5] = jnp.zeros((5,) + s3.shape[1:], BF16)
    s4[0:4] = jnp.zeros((4,) + s4.shape[1:], BF16)
    loads = [
        pltpu.make_async_copy(src, dst, load_sem.at[k])
        for k, (src, dst) in enumerate([
            (w3_ref, own3), (w4_ref, own4), (x_ref.at[s], xb.at[0, s, 2:4, 16:32, :]),
            (i3_ref, i3v), (i4_ref, i4v), (lm_ref, lmv), (ro_ref, rov),
        ])
    ]
    for load in loads:
        load.start()

    barrier = pltpu.get_barrier_semaphore()
    alone = (half == core) & (lax.rem(y, 2) == core)
    count = 0
    greet = [{"ha": sister}, {"ha": lax.rem(h + 2 * core + NH - 1, NH)}]
    greet += [{"wa": lax.rem(w + d, NW)} for d in range(1, NW)]
    greet += [{"section": lax.rem(s + d, NS)} for d in range(1, NS)]
    greet += [
        {"ha": lax.rem(h + dy, NH), "wa": lax.rem(w + dx, NW)} for dy in (1, NH - 1) for dx in (1, NW - 1)
    ]
    for where in greet:
        pl.semaphore_signal(barrier, inc=1, device_id=where, device_id_type=MESH)
    for i in range(4):
        source = 2 * (4 * core + i) + lax.rem(y, 2)
        @pl.when(source != h)
        def _(source=source):
            pl.semaphore_signal(barrier, inc=1, device_id={"ha": source}, device_id_type=MESH)
    pl.semaphore_wait(barrier, len(greet) + 4 - alone.astype(jnp.int32))

    raw3 = remote(w3_ref, sis3, raw_s.at[0], raw_r.at[0], ha=sister)
    raw4 = remote(w4_ref, sis4, raw_s.at[1], raw_r.at[1], ha=sister)
    raw3.start()
    raw4.start()
    for d in range(1, NS):
        m = lax.rem(s + d, NS)
        remote(x_ref.at[m], xb.at[0, s, 2:4, 16:32, :], xa_s, xa_r, section=m).start()

    def placed(rows, count, offset):
        r = lax.broadcasted_iota(jnp.int32, (rows, count), 0)
        c = lax.broadcasted_iota(jnp.int32, (rows, count), 1)
        return jnp.where(r == c + offset, 1.0, 0.0).astype(BF16)

    lane = lax.broadcasted_iota(jnp.int32, (1, 128), 1)
    low = lane < 64
    base3 = 8 * lax.rem(y, 2)
    base4 = 4 * lax.rem(y, 4)
    mine3, other3 = placed(WIN3, 36, base3 + 36 * core), placed(WIN3, 36, base3 + 36 * (1 - core))
    mine4, other4 = placed(WIN4, 18, base4 + 18 * core), placed(WIN4, 18, base4 + 18 * (1 - core))
    loads[0].wait()
    loads[1].wait()
    raw3.wait_recv()
    for tap in range(9):
        rows = jnp.dot(mine3, own3[tap], preferred_element_type=F32) + jnp.dot(
            other3, sis3[tap], preferred_element_type=F32
        )
        v1, v2 = rows[:, 128:256], rows[:, 256:384]
        cw3[3 * tap] = rows[:, :128].astype(BF16)
        cw3[3 * tap + 1] = jnp.where(low, v2, v1).astype(BF16)
        cw3[3 * tap + 2] = jnp.where(low, v1, v2).astype(BF16)
    cw3[27] = jnp.zeros((WIN3, 128), BF16)

    def column_parts(chunk):
        level, slot, n = CHUNKS[chunk]
        cw, s1, per = (cw3, s13, X3) if level == 3 else (cw4, s14, X4)
        first = w if slot == 0 else 8 + s * per + slot - 1
        return cw.at[pl.ds(first, n)], s1.at[lax.rem(y, 4), slot : slot + n], s1.at[:, slot : slot + n]

    def column_start(chunk):
        src, dst, _ = column_parts(chunk)
        for i in range(4):
            target = 2 * (2 * i + core) + half
            @pl.when(target != h)
            def _(target=target):
                remote(src, dst, col_s.at[chunk], col_r.at[chunk], ha=target).start()
        @pl.when(alone)
        def _():
            pltpu.make_async_copy(src, dst, col_r.at[chunk]).start()

    def column_wait(chunk):
        wait_bytes(column_parts(chunk)[2], col_r.at[chunk])

    for chunk in CH3:
        column_start(chunk)
    raw4.wait_recv()
    for tap in range(9):
        rows = jnp.dot(mine4, own4[tap], preferred_element_type=F32) + jnp.dot(
            other4, sis4[tap], preferred_element_type=F32
        )
        cw4[2 * tap] = rows[:, :128].astype(BF16)
        tmp[0:WIN4, 0:64] = rows[:, 128:192]
        tmp[0:WIN4, 64:128] = jnp.zeros((WIN4, 64), F32)
        cw4[2 * tap + 1] = tmp[0:WIN4, 0:128].astype(BF16)
    cw4[18:20] = jnp.zeros((2, WIN4, 128), BF16)
    for chunk in CH4:
        column_start(chunk)

    for load in loads[2:]:
        load.wait()
    tmp[...] = jnp.zeros_like(tmp)
    tmp[0:32, 0:192] = i3v[...].reshape(32, 192).astype(F32)
    tmp[32:128, 0:192] = lmv[...].astype(F32)
    tmp[128:256, 0:96] = i4v[...].reshape(128, 96).astype(F32)
    tmp[256:272, 0:96] = rov[...].astype(F32)
    first = pltpu.roll(tmp[0:128, 0:128], 64, 1).astype(BF16)
    second = pltpu.roll(tmp[0:128, 128:256], 64, 1).astype(BF16)
    s3[0, 2:4, 16:32, 0:128] = first[0:32].reshape(2, 16, 128)
    s3[0, 2:4, 16:32, 128:256] = second[0:32].reshape(2, 16, 128)
    lm[0:96, 0:128] = first[32:128]
    lm[0:96, 128:256] = second[32:128]
    lm[96:128, :] = jnp.zeros((32, 256), BF16)
    third = pltpu.roll(tmp[128:272, 0:128], 96, 1).astype(BF16)
    s4[0, 2:6, 16:48, :] = third[0:128].reshape(4, 32, 128)
    ro[...] = third[128:144]
    fine = lax.broadcasted_iota(jnp.int32, (256, 128), 0)
    cell = lax.broadcasted_iota(jnp.int32, (256, 128), 1)
    up[...] = jnp.where((fine // 64) * 32 + lax.rem(fine, 64) // 2 == cell, 1.0, 0.0).astype(BF16)
    j4[:, :, 192:256] = jnp.zeros((8, 64, 64), F32)

    def away(dy, dx):
        oy = 1 - (h + NH - 1) // NH if dy < 0 else (h + 1) // NH if dy > 0 else 0
        ox = 1 - (w + NW - 1) // NW if dx < 0 else (w + 1) // NW if dx > 0 else 0
        return oy + ox - oy * ox

    def neighbour(dy, dx):
        where = {}
        if dy:
            where["ha"] = lax.rem(h + dy + NH, NH)
        if dx:
            where["wa"] = lax.rem(w + dx + NW, NW)
        return where

    def send_3(t):
        for dy, dx in NEIGHBOURS:
            remote(
                s3.at[t, 2:4, 16:32, :],
                s3.at[t + 5 * away(dy, dx), 2 - 2 * dy : 4 - 2 * dy, 16 - 16 * dx : 32 - 16 * dx, :],
                n3_s.at[t], n3_r.at[t], **neighbour(dy, dx),
            ).start()

    def send_4(t):
        for dy, dx in NEIGHBOURS:
            r0, r1 = {-1: (2, 4), 0: (2, 6), 1: (4, 6)}[dy]
            c0, c1 = {-1: (16, 32), 0: (16, 48), 1: (32, 48)}[dx]
            q0, q1 = {-1: (6, 8), 0: (2, 6), 1: (0, 2)}[dy]
            d0, d1 = {-1: (48, 64), 0: (16, 48), 1: (0, 16)}[dx]
            remote(
                s4.at[t, r0:r1, c0:c1, :], s4.at[t + 4 * away(dy, dx), q0:q1, d0:d1, :],
                n4_s.at[t], n4_r.at[t], **neighbour(dy, dx),
            ).start()

    view_3 = s3.at[0:4, 0:2, 0:32, :]
    view_4 = s4.at[0:3, 2:6, 16:48, :]
    view_x = xb.at[0:2, 0:4, 0:4, 0:32, :]
    view_a = xb.at[0, 0:3, 2:4, 16:32, :]

    send_3(0)
    wait_bytes(view_a, xa_r)
    for dy, dx in NEIGHBOURS:
        remote(
            xb.at[0, :, 2:4, 16:32, :],
            xb.at[away(dy, dx), :, 2 - 2 * dy : 4 - 2 * dy, 16 - 16 * dx : 32 - 16 * dx, :],
            xn_s, xn_r, **neighbour(dy, dx),
        ).start()
    send_4(0)

    def merged3(slot):
        out = []
        for g in (0, 2):
            a, b = s13[g, slot], s13[g + 1, slot]
            out += [a[0:64], a[64:80] + b[0:16], b[16:80]]
        return jnp.concatenate(out, 0)

    def merged4(slot):
        a, b, c, d = (s14[i, slot] for i in range(4))
        return jnp.concatenate(
            [a[0:32], a[32:48] + b[0:16], b[16:32], b[32:48] + c[0:16], c[16:32], c[32:48] + d[0:16], d[16:48]], 0
        )

    def piece(chunk, c, owner):
        level, slot, n = CHUNKS[chunk]
        wb, per = (wb3, X3) if level == 3 else (wb4, X4)
        first = owner if slot == 0 else 8 + owner * per + slot - 1
        return wb.at[c, pl.ds(first, n)]

    def along_wa(chunk):
        return CHUNKS[chunk][1] == 0

    def plane_copy(chunk, d, owner):
        part = piece(chunk, core, owner)
        if along_wa(chunk):
            return remote(part, part, z_s.at[chunk, d], z_r.at[chunk, d], wa=lax.rem(w + d, NW))
        return remote(part, part, x_s.at[chunk, d], x_r.at[chunk, d], section=lax.rem(s + d, NS))

    def owner_of(chunk, d):
        return lax.rem(w + NW - d, NW) if along_wa(chunk) else lax.rem(s + NS - d, NS)

    def order(chunk):
        return Z_ORDER if along_wa(chunk) else X_ORDER

    def share(chunk, d):
        part = piece(chunk, core, owner_of(chunk, d))
        remote(part, part, f_s.at[chunk], f_r.at[chunk], ha=sister).start()

    def shared_view(chunk):
        level, slot, n = CHUNKS[chunk]
        return (wb3 if level == 3 else wb4).at[0, 0 : 8 if slot == 0 else NS * n]

    def plane_start(chunk):
        level, slot, n = CHUNKS[chunk]
        column_wait(chunk)
        wb, merged, per = (wb3, merged3, X3) if level == 3 else (wb4, merged4, X4)
        for k in range(n):
            kb = w if slot == 0 else 8 + s * per + slot - 1 + k
            wb[pl.ds(core, 1), pl.ds(kb, 1)] = merged(slot + k)[None, None]
        for d in order(chunk):
            plane_copy(chunk, d, owner_of(chunk, 0)).start()
        share(chunk, 0)

    def plane_pass(chunk, ds):
        for d in ds:
            plane_copy(chunk, d, owner_of(chunk, d)).wait_recv()
            share(chunk, d)

    for chunk in (0, 1, 2):
        plane_start(chunk)
    plane_pass(0, X_ORDER)
    plane_start(3)
    plane_pass(1, X_ORDER)
    plane_start(4)
    plane_pass(2, Z_ORDER[:4])
    plane_pass(3, X_ORDER)
    for chunk in CH4:
        plane_start(chunk)
    plane_pass(2, Z_ORDER[4:])
    plane_pass(4, X_ORDER)
    wait_bytes(view_3, n3_r.at[0])
    wait_bytes(view_x, xn_r)
    wait_bytes(view_4, n4_r.at[0])
    for chunk in CH3:
        wait_bytes(shared_view(chunk), f_r.at[chunk])

    def gates3(a):
        blocks = []
        for kb in range(9 * a, 9 * a + 9):
            lo, hi = wb3.at[0, kb], wb3.at[1, kb]
            blocks.append(jnp.concatenate([
                lo[64:128, :], lo[0:64, :], lo[128:192, :], lo[128:192, :],
                lo[256:288, :], hi[0:32, :], lo[192:256, :], hi[32:96, :], hi[32:96, :],
            ], 0))
        return jnp.concatenate(blocks, 1)

    def cand3(a):
        zero = jnp.zeros((64, 128), BF16)
        blocks = []
        for kb in range(9 * a, 9 * a + 9):
            hi = wb3.at[1, kb]
            blocks.append(jnp.concatenate([hi[160:224, :], hi[96:160, :], zero, hi[224:288, :]], 0))
        return jnp.concatenate(blocks, 1)

    def gates4(a):
        blocks = []
        for kb in range(6 * a, 6 * a + 6):
            lo, hi = wb4.at[0, kb], wb4.at[1, kb]
            blocks.append(jnp.concatenate([
                lo[32:96, :], lo[0:32, :], lo[0:32, :],
                lo[128:144, :], hi[0:48, :], lo[96:128, :], lo[96:128, :],
            ], 0))
        return jnp.concatenate(blocks, 1)

    def cand4(a):
        zero = jnp.zeros((32, 128), BF16)
        blocks = []
        for kb in range(6 * a, 6 * a + 6):
            hi = wb4.at[1, kb]
            blocks.append(jnp.concatenate([hi[80:144, :], zero, hi[48:80, :]], 0))
        return jnp.concatenate(blocks, 1)

    def taps(ref, r0, r1, c0, c1):
        return jnp.concatenate([ref[r0:r1, c0 + b - 1 : c1 + b - 1, :].astype(BF16) for b in range(3)], 2)

    def level3(t):
        x = xb[0, t].astype(F32)
        p = s3[t].astype(F32)
        j3[:, :, 0:128] = x[:, :, 0:128]
        j3[:, :, 128:256] = p[:, :, 0:128]
        j3[:, :, 256:320] = x[:, :, 128:192]
        j3[:, :, 320:384] = p[:, :, 192:256]
        u = taps(j3, 0, 6, 8, 40)
        sums = sum(nt(u[a : a + 4].reshape(128, 1152), gates3(a)) for a in range(3))
        reset = jax.nn.sigmoid(sums[:, :256]).reshape(4, 32, 256)
        update = jax.nn.sigmoid(sums[:, 256:]).reshape(4, 32, 256)[1:3, 8:24, :]
        gated = reset * p[1:5, 8:40, :]
        j3[1:5, 8:40, 128:256] = gated[:, :, 0:128]
        j3[1:5, 8:40, 320:384] = gated[:, :, 192:256]
        v = taps(j3, 1, 5, 16, 32)
        fresh = sum(nt(v[a : a + 2].reshape(32, 1152), cand3(a)) for a in range(3))
        fresh = jnp.maximum(fresh, 0.0).reshape(2, 16, 256)
        prior = p[2:4, 16:32, :]
        s3[t + 1, 2:4, 16:32, :] = (update * prior + (1.0 - update) * fresh).astype(BF16)

    def to_lead(t):
        return remote(pt.at[t], po.at[s], out_s.at[t], out_r, section=t)

    def level4(t):
        coarse = s3[t + 1, 1:5].astype(F32)[:, 8:40, :].astype(BF16).reshape(128, 256)
        lift = nt(coarse, lm[...]).astype(BF16)
        lifted = jnp.dot(up[...], lift, preferred_element_type=F32).reshape(4, 64, 128)
        p = s4[t].astype(F32)
        for i in range(8):
            j4[i, :, 0:96] = lifted[i // 2, :, 0:96]
        j4[:, :, 96:128] = p[:, :, 96:128]
        j4[:, :, 128:192] = p[:, :, 0:64]
        u = taps(j4, 0, 8, 8, 56)
        sums = sum(nt(u[a : a + 6].reshape(288, 768), gates4(a)) for a in range(3))
        reset = jax.nn.sigmoid(sums[:, :128]).reshape(6, 48, 128)
        update = jax.nn.sigmoid(sums[:, 128:]).reshape(6, 48, 128)[1:5, 8:40, :]
        gated = reset * p[1:7, 8:56, :]
        j4[1:7, 8:56, 96:128] = gated[:, :, 96:128]
        j4[1:7, 8:56, 128:192] = gated[:, :, 0:64]
        v = taps(j4, 1, 7, 16, 48)
        fresh = sum(nt(v[a : a + 4].reshape(128, 768), cand4(a)) for a in range(3))
        fresh = jnp.maximum(fresh, 0.0).reshape(4, 32, 128)
        prior = p[2:6, 16:48, :]
        state = (update * prior + (1.0 - update) * fresh).astype(BF16)
        if t < LEADS - 1:
            s4[t + 1, 2:6, 16:48, :] = state
            send_4(t + 1)
        pt[t] = nt(ro[...], state.reshape(128, 128))

        @pl.when(s == t)
        def _():
            po[t] = pt[t]

        @pl.when(s != t)
        def _():
            to_lead(t).start()

    level3(0)
    send_3(1)
    for chunk in CH4:
        plane_pass(chunk, order(chunk))
    for t in range(LEADS):
        wait_bytes(view_3, n3_r.at[t + 1])
        if t + 1 < LEADS:
            level3(t + 1)
            send_3(t + 2)
        if t == 0:
            for chunk in CH4:
                wait_bytes(shared_view(chunk), f_r.at[chunk])
        else:
            wait_bytes(view_4, n4_r.at[t])
        level4(t)

    wait_bytes(po.at[0:3], out_r)
    o_ref[...] = po[...]

    raw3.wait_send()
    raw4.wait_send()
    wait_bytes(view_a, xa_s)
    wait_bytes(view_x, xn_s)
    for t in range(LEADS + 1):
        wait_bytes(view_3, n3_s.at[t])
    for t in range(LEADS):
        wait_bytes(view_4, n4_s.at[t])
    for chunk in range(len(CHUNKS)):
        level, slot, n = CHUNKS[chunk]
        s1 = s13 if level == 3 else s14
        @pl.when(alone)
        def _(s1=s1, slot=slot, n=n, chunk=chunk):
            wait_bytes(s1.at[0:3, slot : slot + n], col_s.at[chunk])
        @pl.when(jnp.logical_not(alone))
        def _(s1=s1, slot=slot, n=n, chunk=chunk):
            wait_bytes(s1.at[:, slot : slot + n], col_s.at[chunk])
        for d in order(chunk):
            plane_copy(chunk, d, owner_of(chunk, 0)).wait_send()
        wait_bytes(shared_view(chunk), f_s.at[chunk])
    for t in range(LEADS):
        @pl.when(s != t)
        def _(t=t):
            to_lead(t).wait_send()


def local(coarse_inputs, init_level3, init_level4, weight_level3, weight_level4, lift_map, readout):
    n = len(CHUNKS)
    dma = pltpu.SemaphoreType.DMA
    fields = pl.pallas_call(
        kernel,
        out_shape=jax.ShapeDtypeStruct((4, 16, 128), F32),
        in_specs=[pl.BlockSpec(memory_space=pl.ANY)] * 7,
        out_specs=pl.BlockSpec(memory_space=pltpu.VMEM),
        scratch_shapes=[
            pltpu.VMEM((2, 16, 192), BF16),
            pltpu.VMEM((4, 32, 96), BF16),
            pltpu.VMEM((96, 192), BF16),
            pltpu.VMEM((16, 96), BF16),
            pltpu.VMEM((9, 36, 384), BF16),
            pltpu.VMEM((9, 18, 192), BF16),
            pltpu.VMEM((9, 36, 384), BF16),
            pltpu.VMEM((9, 18, 192), BF16),
            pltpu.VMEM((K3, WIN3, 128), BF16),
            pltpu.VMEM((K4, WIN4, 128), BF16),
            pltpu.VMEM((4, 1 + X3, WIN3, 128), BF16),
            pltpu.VMEM((4, 1 + X4, WIN4, 128), BF16),
            pltpu.VMEM((2, K3, H3R, 128), BF16),
            pltpu.VMEM((2, K4, H4R, 128), BF16),
            pltpu.VMEM((2, 4, 6, 48, 192), BF16),
            pltpu.VMEM((10, 6, 48, 256), BF16),
            pltpu.VMEM((8, 8, 64, 128), BF16),
            pltpu.VMEM((6, 48, 384), F32),
            pltpu.VMEM((8, 64, 256), F32),
            pltpu.VMEM((272, 256), F32),
            pltpu.VMEM((128, 256), BF16),
            pltpu.VMEM((16, 128), BF16),
            pltpu.VMEM((256, 128), BF16),
            pltpu.VMEM((4, 16, 128), F32),
            pltpu.VMEM((4, 16, 128), F32),
            dma((7,)), dma((2,)), dma((2,)), dma((n,)), dma((n,)),
            dma((n, NS)), dma((n, NS)), dma((n, NW)), dma((n, NW)), dma((n,)), dma((n,)),
            dma, dma, dma, dma, dma((5,)), dma((5,)), dma((4,)), dma((4,)), dma((4,)), dma,
        ],
        compiler_params=pltpu.CompilerParams(
            collective_id=0, has_side_effects=True, vmem_limit_bytes=64 << 20
        ),
        name="nowcast",
    )(
        coarse_inputs[0].transpose(0, 2, 3, 1),
        init_level3.transpose(1, 2, 0),
        init_level4.transpose(1, 2, 0),
        weight_level3.transpose(1, 0, 2),
        weight_level4.transpose(1, 0, 2),
        lift_map,
        readout,
    )
    return fields.reshape(1, 4, 16, 4, 32)


def solution(mesh):
    return jax.shard_map(
        local,
        mesh=mesh,
        in_specs=(
            P("section", None, None, "ha", "wa"),
            P(None, "ha", "wa"),
            P(None, "ha", "wa"),
            P("ha", None, None),
            P("ha", None, None),
            P(),
            P(),
        ),
        out_specs=P("section", None, None, "ha", "wa"),
        check_vma=False,
    )
```

time: 384 us -> 82 us (0.21)
  the two profiles are of different devices: /device:TPU:288 before, /device:TPU:6 now
where the time goes in v2:
time: 82 us; the launch traced here: 81.9 us
  Pallas kernels  80.3 us (98%)
  local copies, waits for them, and re-layouts  1.53 us (2%)
    pallas_call x1, Pallas kernels, local(): pl.pallas_call(kernel, out_shape=jax.ShapeDtypeStruct((4, 16, 128), F32),...  80.3 us

profile of v2, /device:TPU:6, one launch (start us, length us, event | category | flops | bytes accessed | tf_op | source)
XLA Modules:
  0.0 81.9 jit_solution(9410018422365884096)
XLA Ops:
  0.0 80.3 %nowcast.1 = f32[4,16,128]{2,1,0:T(8,128)} custom-call(bf16[4,2,16,192]{3,2,1,0:T(8,128)(2,1)} %bitcast.9, bf16[2,16,192]{2,1,0:T(8,128)(2,1)} %bitcast.11, bf16[4,32,96]{2,1,0:T(8,128)(2,1)} %bitcast.10, bf16[9,36,384]{2,1,0:T(8,128)(2,1)} %bitcast.7, bf16[9,18,192]{2,1,0:T(8,128)(2,1)} %bitcast.8, bf16[96,192]{1,0:T(8,128)(2,1)} %lm_ref.1, ...), custom_call_target="tpu_custom_call" | custom-call | tf_op jit(solution)/shard_map/nowcast/pallas_call | solution.py:442
  80.3 1.5 %reshape.3 = f32[1,4,16,4,32]{4,3,2,1,0:T(4,128)} reshape(f32[4,16,128]{2,1,0:T(8,128)} %nowcast.1) | data formatting | bytes 65536 | tf_op jit(solution)/shard_map/reshape | solution.py:490

commit v3 on v2

v3 whole, which is shorter than its diff:
```python
import jax
import jax.numpy as jnp
from jax import lax
from jax.experimental import pallas as pl
from jax.experimental.pallas import tpu as pltpu
from jax.sharding import PartitionSpec as P

MESH = pl.DeviceIdType.MESH
BF16 = jnp.bfloat16
F32 = jnp.float32

NS, NH, NW = 4, 16, 8
LEADS = 4

X3, X4 = 4, 2
C3, C4 = 3, 2
K3, K4 = 8 + NS * X3 + C3, 8 + NS * X4 + C4
H3R, H4R = 288, 144
WIN3, WIN4 = 80, 48

CHUNKS = [(3, 0, 1), (3, 1, 1), (3, 2, 1), (3, 3, 2), (4, 0, 1), (4, 1, 2), (3, 5, 3), (4, 3, 2)]
CH3, CH4 = (0, 1, 2, 3, 6), (4, 5, 7)

NEIGHBOURS = [(-1, -1), (-1, 1), (1, -1), (1, 1), (0, -1), (0, 1), (-1, 0), (1, 0)]
X_ORDER = (1, 3, 2)
Z_ORDER = (1, 7, 2, 6, 3, 5, 4)


def nt(a, b):
    return lax.dot_general(a, b, (((1,), (1,)), ((), ())), preferred_element_type=F32)


def kernel(
    x_ref, i3_ref, i4_ref, w3_ref, w4_ref, lm_ref, ro_ref, o_ref,
    i3v, i4v, lmv, rov, own3, own4, sis3, sis4, cw3, cw4, s13, s14, wb3, wb4,
    xc, xe, xh, s3c, s3e, s3h, s4c, s4e, s4h, jx, j3, j4, p4, xg, xk, tmp, lm, ro, up, pt, po,
    load_sem, raw_s, raw_r, col_s, col_r, x_s, x_r, z_s, z_r, f_s, f_r,
    xa_s, xa_r, xn_s, xn_r, n3_s, n3_r, n4_s, n4_r, out_s, out_r,
):
    s = lax.axis_index("section")
    h = lax.axis_index("ha")
    w = lax.axis_index("wa")
    core = lax.rem(h, 2)
    y = h // 2
    sister = h + 1 - 2 * core
    half = y // 4

    def remote(src, dst, send, recv, **where):
        return pltpu.make_async_remote_copy(
            src_ref=src, dst_ref=dst, send_sem=send, recv_sem=recv, device_id=where, device_id_type=MESH
        )

    def wait_bytes(view, sem):
        pltpu.make_async_copy(view, view, sem).wait()

    for ref, n in ((xc, 1), (xh, 1), (s3c, 5), (s3h, 5), (s4c, 3), (s4h, 3)):
        ref[0:n] = jnp.zeros((n,) + ref.shape[1:], BF16)
    loads = [
        pltpu.make_async_copy(src, dst, load_sem.at[k])
        for k, (src, dst) in enumerate([
            (w3_ref, own3), (w4_ref, own4), (x_ref.at[s], xc.at[0, s, 2:4]),
            (i3_ref, i3v), (i4_ref, i4v), (lm_ref, lmv), (ro_ref, rov),
        ])
    ]
    for load in loads:
        load.start()

    def shifted(rows, count, offset):
        r = lax.broadcasted_iota(jnp.int32, (rows, count), 0)
        c = lax.broadcasted_iota(jnp.int32, (rows, count), 1)
        return jnp.where(r == c + offset, 1.0, 0.0).astype(BF16)

    low = lax.broadcasted_iota(jnp.int32, (1, 128), 1) < 64

    def place3(shard, which, add):
        put = shifted(WIN3, 36, 8 * lax.rem(y, 2) + 36 * which)
        for tap in range(9):
            rows = jnp.dot(put, shard[tap], preferred_element_type=F32)
            v1, v2 = rows[:, 128:256], rows[:, 256:384]
            for k, v in enumerate((rows[:, :128], jnp.where(low, v2, v1), jnp.where(low, v1, v2))):
                v = v.astype(BF16)
                cw3[3 * tap + k] = cw3[3 * tap + k] + v if add else v

    def place4(shard, which, add):
        put = shifted(WIN4, 18, 4 * lax.rem(y, 4) + 18 * which)
        for tap in range(9):
            rows = jnp.dot(put, shard[tap], preferred_element_type=F32)
            tmp[0:WIN4, 0:64] = rows[:, 128:192]
            tmp[0:WIN4, 64:128] = jnp.zeros((WIN4, 64), F32)
            for k, v in enumerate((rows[:, :128], tmp[0:WIN4, 0:128])):
                v = v.astype(BF16)
                cw4[2 * tap + k] = cw4[2 * tap + k] + v if add else v

    barrier = pltpu.get_barrier_semaphore()
    alone = (half == core) & (lax.rem(y, 2) == core)
    count = 0
    greet = [{"ha": sister}, {"ha": lax.rem(h + 2 * core + NH - 1, NH)}]
    greet += [{"wa": lax.rem(w + d, NW)} for d in range(1, NW)]
    greet += [{"section": lax.rem(s + d, NS)} for d in range(1, NS)]
    greet += [
        {"ha": lax.rem(h + dy, NH), "wa": lax.rem(w + dx, NW)} for dy in (1, NH - 1) for dx in (1, NW - 1)
    ]
    for where in greet:
        pl.semaphore_signal(barrier, inc=1, device_id=where, device_id_type=MESH)
    for i in range(4):
        source = 2 * (4 * core + i) + lax.rem(y, 2)
        @pl.when(source != h)
        def _(source=source):
            pl.semaphore_signal(barrier, inc=1, device_id={"ha": source}, device_id_type=MESH)
    loads[0].wait()
    place3(own3, core, False)
    loads[1].wait()
    place4(own4, core, False)
    pl.semaphore_wait(barrier, len(greet) + 4 - alone.astype(jnp.int32))

    raw3 = remote(w3_ref, sis3, raw_s.at[0], raw_r.at[0], ha=sister)
    raw4 = remote(w4_ref, sis4, raw_s.at[1], raw_r.at[1], ha=sister)
    raw3.start()
    raw4.start()
    for d in range(1, NS):
        m = lax.rem(s + d, NS)
        remote(x_ref.at[m], xc.at[0, s, 2:4], xa_s, xa_r, section=m).start()

    raw3.wait_recv()
    place3(sis3, 1 - core, True)

    def first_block(chunk, z, x):
        level, slot, n = CHUNKS[chunk]
        per = X3 if level == 3 else X4
        if slot == 0:
            return z
        return 8 + x * per + slot - 1 if slot <= per else 8 + (NS - 1) * per + slot - 1

    def column_parts(chunk):
        level, slot, n = CHUNKS[chunk]
        cw, s1 = (cw3, s13) if level == 3 else (cw4, s14)
        first = first_block(chunk, w, s)
        return cw.at[pl.ds(first, n)], s1.at[lax.rem(y, 4), slot : slot + n], s1.at[:, slot : slot + n]

    def column_start(chunk):
        src, dst, _ = column_parts(chunk)
        for i in range(4):
            target = 2 * (2 * i + core) + half
            @pl.when(target != h)
            def _(target=target):
                remote(src, dst, col_s.at[chunk], col_r.at[chunk], ha=target).start()
        @pl.when(alone)
        def _():
            pltpu.make_async_copy(src, dst, col_r.at[chunk]).start()

    def column_wait(chunk):
        wait_bytes(column_parts(chunk)[2], col_r.at[chunk])

    for chunk in range(4):
        column_start(chunk)
    raw4.wait_recv()
    place4(sis4, 1 - core, True)
    for chunk in range(4, 8):
        column_start(chunk)

    def edges(e, t, tile, rows):
        lanes = tile.shape[-1]
        e[t, 0] = tile[:, 0:8, :].reshape(rows * 8, lanes).astype(BF16)
        e[t, 1] = tile[:, tile.shape[1] - 8 :, :].reshape(rows * 8, lanes).astype(BF16)

    def keep3(t, tile):
        s3c[t, 2:4] = tile.astype(BF16)
        edges(s3e, t, tile, 2)

    def keep4(t, tile):
        s4c[t, 4:8] = tile.astype(BF16)
        edges(s4e, t, tile, 4)

    for load in loads[2:]:
        load.wait()
    tmp[...] = jnp.zeros_like(tmp)
    tmp[0:32, 0:192] = i3v[...].reshape(32, 192).astype(F32)
    tmp[32:128, 0:192] = lmv[...].astype(F32)
    tmp[128:256, 0:96] = i4v[...].reshape(128, 96).astype(F32)
    tmp[256:272, 0:96] = rov[...].astype(F32)
    first = pltpu.roll(tmp[0:128, 0:128], 64, 1).astype(BF16)
    second = pltpu.roll(tmp[0:128, 128:256], 64, 1).astype(BF16)
    tmp[0:32, 0:128] = pltpu.roll(tmp[0:32, 0:128], 64, 1)
    tmp[0:32, 128:256] = pltpu.roll(tmp[0:32, 128:256], 64, 1)
    keep3(0, tmp[0:32, 0:256].reshape(2, 16, 256))
    lm[0:96, 0:128] = first[32:128]
    lm[0:96, 128:256] = second[32:128]
    lm[96:128, :] = jnp.zeros((32, 256), BF16)
    third = pltpu.roll(tmp[128:272, 0:128], 96, 1)
    keep4(0, third[0:128].reshape(4, 32, 128))
    ro[...] = third[128:144].astype(BF16)
    fine = lax.broadcasted_iota(jnp.int32, (384, 192), 0)
    cell = lax.broadcasted_iota(jnp.int32, (384, 192), 1)
    up[...] = jnp.where((fine // 64) * 32 + lax.rem(fine, 64) // 2 == cell, 1.0, 0.0).astype(BF16)
    j4[:, :, 192:256] = jnp.zeros((12, 64, 64), F32)

    def away(dy, dx):
        oy = 1 - (h + NH - 1) // NH if dy < 0 else (h + 1) // NH if dy > 0 else 0
        ox = 1 - (w + NW - 1) // NW if dx < 0 else (w + 1) // NW if dx > 0 else 0
        return oy + ox - oy * ox

    def neighbour(dy, dx):
        where = {}
        if dy:
            where["ha"] = lax.rem(h + dy + NH, NH)
        if dx:
            where["wa"] = lax.rem(w + dx + NW, NW)
        return where

    def send_tiles(c, e, halo, t, steps, rows, send, recv):
        for dy, dx in NEIGHBOURS:
            to = t + steps * away(dy, dx)
            if dx == 0:
                src, dst = c.at[t, rows : 2 * rows], c.at[to, rows * (1 - dy) : rows * (2 - dy)]
            else:
                src, dst = e.at[t, (dx + 1) // 2], halo.at[to, (1 - dx) // 2, 1 - dy]
            remote(src, dst, send, recv, **neighbour(dy, dx)).start()

    def send_3(t):
        send_tiles(s3c, s3e, s3h, t, 5, 2, n3_s.at[t], n3_r.at[t])

    def send_4(t):
        send_tiles(s4c, s4e, s4h, t, 3, 4, n4_s.at[t], n4_r.at[t])

    view_3 = s3c.at[0:2, 0:5]
    view_4 = s4c.at[0:2, 0:7]
    view_x = xc.at[0:2, :, 0:5]
    view_a = xc.at[0, 0:3, 2:4]

    send_3(0)
    wait_bytes(view_a, xa_r)
    for lead in range(LEADS):
        edges(xe.at[lead], 0, xc[0, lead, 2:4].astype(F32), 2)
    for dy, dx in NEIGHBOURS:
        if dx == 0:
            src, dst = xc.at[0, :, 2:4], xc.at[away(dy, dx), :, 2 - 2 * dy : 4 - 2 * dy]
        else:
            src, dst = xe.at[:, 0, (dx + 1) // 2], xh.at[away(dy, dx), (1 - dx) // 2, 1 - dy]
        remote(src, dst, xn_s, xn_r, **neighbour(dy, dx)).start()
    send_4(0)

    def merged3(slot):
        out = []
        for g in (0, 2):
            a, b = s13[g, slot], s13[g + 1, slot]
            out += [a[0:64], a[64:80] + b[0:16], b[16:80]]
        return jnp.concatenate(out, 0)

    def merged4(slot):
        a, b, c, d = (s14[i, slot] for i in range(4))
        return jnp.concatenate(
            [a[0:32], a[32:48] + b[0:16], b[16:32], b[32:48] + c[0:16], c[16:32], c[32:48] + d[0:16], d[16:48]], 0
        )

    def piece(chunk, c, owner):
        level, slot, n = CHUNKS[chunk]
        return (wb3 if level == 3 else wb4).at[c, pl.ds(first_block(chunk, owner, owner), n)]

    def along_wa(chunk):
        return CHUNKS[chunk][1] == 0

    def plane_copy(chunk, d, owner):
        part = piece(chunk, core, owner)
        if along_wa(chunk):
            return remote(part, part, z_s.at[chunk, d], z_r.at[chunk, d], wa=lax.rem(w + d, NW))
        return remote(part, part, x_s.at[chunk, d], x_r.at[chunk, d], section=lax.rem(s + d, NS))

    def owner_of(chunk, d):
        return lax.rem(w + NW - d, NW) if along_wa(chunk) else lax.rem(s + NS - d, NS)

    def order(chunk):
        level, slot, n = CHUNKS[chunk]
        return Z_ORDER if slot == 0 else X_ORDER if slot <= (X3 if level == 3 else X4) else ()

    def share(chunk, d):
        part = piece(chunk, core, owner_of(chunk, d))
        remote(part, part, f_s.at[chunk], f_r.at[chunk], ha=sister).start()

    def shared_view(chunk):
        level, slot, n = CHUNKS[chunk]
        return (wb3 if level == 3 else wb4).at[0, 0 : (1 + len(order(chunk))) * n]

    def plane_start(chunk):
        level, slot, n = CHUNKS[chunk]
        column_wait(chunk)
        wb, merged = (wb3, merged3) if level == 3 else (wb4, merged4)
        for k in range(n):
            kb = first_block(chunk, w, s) + k
            wb[pl.ds(core, 1), pl.ds(kb, 1)] = merged(slot + k)[None, None]
        for d in order(chunk):
            plane_copy(chunk, d, owner_of(chunk, 0)).start()
        share(chunk, 0)

    def plane_pass(chunk, ds):
        for d in ds:
            plane_copy(chunk, d, owner_of(chunk, d)).wait_recv()
            share(chunk, d)

    for chunk in (0, 1, 2, 3):
        plane_start(chunk)
    plane_pass(1, X_ORDER)
    plane_pass(0, Z_ORDER[:4])
    plane_pass(2, X_ORDER)
    plane_pass(0, Z_ORDER[4:6])
    plane_start(4)
    plane_pass(3, X_ORDER[:2])
    plane_start(5)
    plane_start(6)
    plane_pass(0, Z_ORDER[6:])
    plane_pass(3, X_ORDER[2:])
    wait_bytes(view_3, n3_r.at[0])
    wait_bytes(view_x, xn_r)
    wait_bytes(view_4, n4_r.at[0])
    for chunk in CH3:
        wait_bytes(shared_view(chunk), f_r.at[chunk])

    def wide(halo, centre, rows):
        sides = [halo[k].astype(F32).reshape(rows, 8, centre.shape[-1]) for k in range(2)]
        return jnp.concatenate([sides[0], centre.astype(F32), sides[1]], 1)

    def blocks3(a, kinds):
        return [3 * (3 * a + b) + kind for b in range(3) for kind in kinds]

    def gates3(a, kinds):
        blocks = []
        for kb in blocks3(a, kinds):
            lo, hi = wb3.at[0, kb], wb3.at[1, kb]
            blocks.append(jnp.concatenate([
                lo[64:128, :], lo[0:64, :], lo[128:192, :], lo[128:192, :],
                lo[256:288, :], hi[0:32, :], lo[192:256, :], hi[32:96, :], hi[32:96, :],
            ], 0))
        return jnp.concatenate(blocks, 1)

    def cand3(a, kinds):
        zero = jnp.zeros((64, 128), BF16)
        blocks = []
        for kb in blocks3(a, kinds):
            hi = wb3.at[1, kb]
            blocks.append(jnp.concatenate([hi[160:224, :], hi[96:160, :], zero, hi[224:288, :]], 0))
        return jnp.concatenate(blocks, 1)

    def gates4(a):
        blocks = []
        for kb in range(6 * a, 6 * a + 6):
            lo, hi = wb4.at[0, kb], wb4.at[1, kb]
            blocks.append(jnp.concatenate([
                lo[32:96, :], lo[0:32, :], lo[0:32, :],
                lo[128:144, :], hi[0:48, :], lo[96:128, :], lo[96:128, :],
            ], 0))
        return jnp.concatenate(blocks, 1)

    def cand4(a):
        zero = jnp.zeros((32, 128), BF16)
        blocks = []
        for kb in range(6 * a, 6 * a + 6):
            hi = wb4.at[1, kb]
            blocks.append(jnp.concatenate([hi[80:144, :], zero, hi[48:80, :]], 0))
        return jnp.concatenate(blocks, 1)

    def conv(ref, r0, rows, c0, cols, weights):
        u = jnp.concatenate(
            [ref[r0 - 1 : r0 + rows + 1, c0 + b - 1 : c0 + b - 1 + cols, :].astype(BF16) for b in range(3)], 2
        )
        return sum(nt(u[a : a + rows].reshape(rows * cols, u.shape[2]), weights(a)) for a in range(3))

    def input_sums(t):
        jx[:, 8:40, :] = wide(xh.at[0, :, :, t], xc[0, t], 6)[:, :, 0:128]
        xg[t] = conv(jx, 1, 4, 8, 32, lambda a: gates3(a, (0,)))
        xk[t] = conv(jx, 2, 2, 16, 16, lambda a: cand3(a, (0,)))

    def level3(t):
        p = wide(s3h.at[t], s3c[t], 6)
        j3[:, 8:40, 0:128] = p[:, :, 0:128]
        j3[:, 8:40, 128:192] = wide(xh.at[0, :, :, t], xc[0, t], 6)[:, :, 128:192]
        j3[:, 8:40, 192:256] = p[:, :, 192:256]
        sums = xg[t] + conv(j3, 1, 4, 8, 32, lambda a: gates3(a, (1, 2)))
        reset = jax.nn.sigmoid(sums[:, :256]).reshape(4, 32, 256)
        update = jax.nn.sigmoid(sums[:, 256:]).reshape(4, 32, 256)[1:3, 8:24, :]
        gated = reset * p[1:5]
        j3[1:5, 8:40, 0:128] = gated[:, :, 0:128]
        j3[1:5, 8:40, 192:256] = gated[:, :, 192:256]
        fresh = xk[t] + conv(j3, 2, 2, 16, 16, lambda a: cand3(a, (1, 2)))
        fresh = jnp.maximum(fresh, 0.0).reshape(2, 16, 256)
        prior = p[2:4, 8:24, :]
        keep3(t + 1, update * prior + (1.0 - update) * fresh)
        send_3(t + 1)

    def to_lead(t):
        return remote(pt.at[t], po.at[s], out_s.at[t], out_r, section=t)

    def lift(t):
        coarse = wide(s3h.at[t + 1], s3c[t + 1], 6).astype(BF16).reshape(192, 256)
        lifted = nt(coarse, lm[...]).astype(BF16)
        lifted = jnp.dot(up[...], lifted, preferred_element_type=F32).reshape(6, 64, 128)
        for i in range(12):
            j4[i, :, 0:96] = lifted[i // 2, :, 0:96]

    def level4(t):
        border = 2 if t == LEADS - 2 else 0
        g0, g1 = 3 - border, 9 + border
        p = p4[...] if t == LEADS - 1 else wide(s4h.at[t], s4c[t], 12)
        j4[:, 8:56, 96:128] = p[:, :, 96:128]
        j4[:, 8:56, 128:192] = p[:, :, 0:64]
        sums = conv(j4, g0, g1 - g0, 8, 48, gates4)
        reset = jax.nn.sigmoid(sums[:, :128]).reshape(g1 - g0, 48, 128)
        update = jax.nn.sigmoid(sums[:, 128:]).reshape(g1 - g0, 48, 128)
        gated = reset * p[g0:g1]
        j4[g0:g1, 8:56, 96:128] = gated[:, :, 96:128]
        j4[g0:g1, 8:56, 128:192] = gated[:, :, 0:64]
        c0, cols = (8, 48) if border else (16, 32)
        rows = g1 - g0 - 2
        fresh = conv(j4, g0 + 1, rows, c0, cols, cand4)
        fresh = jnp.maximum(fresh, 0.0).reshape(rows, cols, 128)
        update, prior = update[1 : rows + 1, c0 - 8 : c0 - 8 + cols], p[g0 + 1 : g1 - 1, c0 - 8 : c0 - 8 + cols]
        state = update * prior + (1.0 - update) * fresh
        if border:
            row = lax.broadcasted_iota(jnp.int32, state.shape, 0) + (4 * h + g0 + 1 - 4)
            col = lax.broadcasted_iota(jnp.int32, state.shape, 1) + (32 * w + c0 - 16)
            inside = (row >= 0) & (row < 4 * NH) & (col >= 0) & (col < 32 * NW)
            p4[g0 + 1 : g1 - 1] = jnp.where(inside, state, 0.0).astype(BF16).astype(F32)
            state = state[border : border + 4, 8:40]
        elif t < LEADS - 2:
            keep4(t + 1, state)
            send_4(t + 1)
        pt[t] = nt(ro[...], state.astype(BF16).reshape(128, 128))

        @pl.when(s == t)
        def _():
            po[t] = pt[t]

        @pl.when(s != t)
        def _():
            to_lead(t).start()

    input_sums(0)
    level3(0)
    plane_start(7)
    for t in range(1, LEADS):
        input_sums(t)
    plane_pass(5, X_ORDER)
    for t in range(LEADS):
        wait_bytes(view_3, n3_r.at[t + 1])
        if t + 1 < LEADS:
            level3(t + 1)
        if t == 0:
            plane_pass(4, Z_ORDER)
        lift(t)
        if t == 0:
            for chunk in CH4:
                wait_bytes(shared_view(chunk), f_r.at[chunk])
        if 0 < t < LEADS - 1:
            wait_bytes(view_4, n4_r.at[t])
        level4(t)

    wait_bytes(po.at[0:3], out_r)
    o_ref[...] = po[...]

    raw3.wait_send()
    raw4.wait_send()
    wait_bytes(view_a, xa_s)
    wait_bytes(view_x, xn_s)
    for t in range(LEADS + 1):
        wait_bytes(view_3, n3_s.at[t])
    for t in range(LEADS - 1):
        wait_bytes(view_4, n4_s.at[t])
    for chunk in range(len(CHUNKS)):
        level, slot, n = CHUNKS[chunk]
        s1 = s13 if level == 3 else s14
        @pl.when(alone)
        def _(s1=s1, slot=slot, n=n, chunk=chunk):
            wait_bytes(s1.at[0:3, slot : slot + n], col_s.at[chunk])
        @pl.when(jnp.logical_not(alone))
        def _(s1=s1, slot=slot, n=n, chunk=chunk):
            wait_bytes(s1.at[:, slot : slot + n], col_s.at[chunk])
        for d in order(chunk):
            plane_copy(chunk, d, owner_of(chunk, 0)).wait_send()
        wait_bytes(shared_view(chunk), f_s.at[chunk])
    for t in range(LEADS):
        @pl.when(s != t)
        def _(t=t):
            to_lead(t).wait_send()


def local(coarse_inputs, init_level3, init_level4, weight_level3, weight_level4, lift_map, readout):
    n = len(CHUNKS)
    dma = pltpu.SemaphoreType.DMA
    fields = pl.pallas_call(
        kernel,
        out_shape=jax.ShapeDtypeStruct((4, 16, 128), F32),
        in_specs=[pl.BlockSpec(memory_space=pl.ANY)] * 7,
        out_specs=pl.BlockSpec(memory_space=pltpu.VMEM),
        scratch_shapes=[
            pltpu.VMEM((2, 16, 192), BF16),
            pltpu.VMEM((4, 32, 96), BF16),
            pltpu.VMEM((96, 192), BF16),
            pltpu.VMEM((16, 96), BF16),
            pltpu.VMEM((9, 36, 384), BF16),
            pltpu.VMEM((9, 18, 192), BF16),
            pltpu.VMEM((9, 36, 384), BF16),
            pltpu.VMEM((9, 18, 192), BF16),
            pltpu.VMEM((K3, WIN3, 128), BF16),
            pltpu.VMEM((K4, WIN4, 128), BF16),
            pltpu.VMEM((4, 1 + X3 + C3, WIN3, 128), BF16),
            pltpu.VMEM((4, 1 + X4 + C4, WIN4, 128), BF16),
            pltpu.VMEM((2, K3, H3R, 128), BF16),
            pltpu.VMEM((2, K4, H4R, 128), BF16),
            pltpu.VMEM((2, 4, 6, 16, 192), BF16),
            pltpu.VMEM((4, 1, 2, 16, 192), BF16),
            pltpu.VMEM((2, 2, 3, 4, 16, 192), BF16),
            pltpu.VMEM((10, 6, 16, 256), BF16),
            pltpu.VMEM((5, 2, 16, 256), BF16),
            pltpu.VMEM((10, 2, 3, 16, 256), BF16),
            pltpu.VMEM((6, 12, 32, 128), BF16),
            pltpu.VMEM((3, 2, 32, 128), BF16),
            pltpu.VMEM((6, 2, 3, 32, 128), BF16),
            pltpu.VMEM((6, 48, 128), F32),
            pltpu.VMEM((6, 48, 256), F32),
            pltpu.VMEM((12, 64, 256), F32),
            pltpu.VMEM((12, 48, 128), F32),
            pltpu.VMEM((4, 128, 512), F32),
            pltpu.VMEM((4, 32, 256), F32),
            pltpu.VMEM((272, 256), F32),
            pltpu.VMEM((128, 256), BF16),
            pltpu.VMEM((16, 128), BF16),
            pltpu.VMEM((384, 192), BF16),
            pltpu.VMEM((4, 16, 128), F32),
            pltpu.VMEM((4, 16, 128), F32),
            dma((7,)), dma((2,)), dma((2,)), dma((n,)), dma((n,)),
            dma((n, NS)), dma((n, NS)), dma((n, NW)), dma((n, NW)), dma((n,)), dma((n,)),
            dma, dma, dma, dma, dma((5,)), dma((5,)), dma((3,)), dma((3,)), dma((4,)), dma,
        ],
        compiler_params=pltpu.CompilerParams(
            collective_id=0, has_side_effects=True, vmem_limit_bytes=64 << 20
        ),
        name="nowcast",
    )(
        coarse_inputs[0].transpose(0, 2, 3, 1),
        init_level3.transpose(1, 2, 0),
        init_level4.transpose(1, 2, 0),
        weight_level3.transpose(1, 0, 2),
        weight_level4.transpose(1, 0, 2),
        lift_map,
        readout,
    )
    return fields.reshape(1, 4, 16, 4, 32)


def solution(mesh):
    return jax.shard_map(
        local,
        mesh=mesh,
        in_specs=(
            P("section", None, None, "ha", "wa"),
            P(None, "ha", "wa"),
            P(None, "ha", "wa"),
            P("ha", None, None),
            P("ha", None, None),
            P(),
            P(),
        ),
        out_specs=P("section", None, None, "ha", "wa"),
        check_vma=False,
    )
```

time: 82 us -> 71.6 us (0.87)
  Pallas kernels: 80.3 us -> 69.8 us
    pallas_call x1, Pallas kernels: 80.3 us -> 69.8 us  [local(): pl.pallas_call(kernel, out_shape=jax.ShapeDtypeStruct((4, 16, 128), F32),...]
where the time goes in v3:
time: 71.6 us; the launch traced here: 71.4 us
  Pallas kernels  69.8 us (97%)
  local copies, waits for them, and re-layouts  1.53 us (2%)
    pallas_call x1, Pallas kernels, local(): pl.pallas_call(kernel, out_shape=jax.ShapeDtypeStruct((4, 16, 128), F32),...  69.8 us
    reshape x1, local copies, waits for them, and re-layouts, local(): return fields.reshape(1, 4, 16, 4, 32)  1.53 us

profile of v3, /device:TPU:6, one launch (start us, length us, event | category | flops | bytes accessed | tf_op | source)
XLA Modules:
  0.0 71.4 jit_solution(9770881493474447767)
XLA Ops:
  0.0 69.8 %nowcast.1 = f32[4,16,128]{2,1,0:T(8,128)} custom-call(bf16[4,2,16,192]{3,2,1,0:T(8,128)(2,1)} %bitcast.9, bf16[2,16,192]{2,1,0:T(8,128)(2,1)} %bitcast.11, bf16[4,32,96]{2,1,0:T(8,128)(2,1)} %bitcast.10, bf16[9,36,384]{2,1,0:T(8,128)(2,1)} %bitcast.7, bf16[9,18,192]{2,1,0:T(8,128)(2,1)} %bitcast.8, bf16[96,192]{1,0:T(8,128)(2,1)} %lm_ref.1, ...), custom_call_target="tpu_custom_call" | custom-call | tf_op jit(solution)/shard_map/nowcast/pallas_call | solution.py:487
  69.9 1.5 %reshape.3 = f32[1,4,16,4,32]{4,3,2,1,0:T(4,128)} reshape(f32[4,16,128]{2,1,0:T(8,128)} %nowcast.1) | data formatting | bytes 65536 | tf_op jit(solution)/shard_map/reshape | solution.py:545

commit v4 on v3

--- a/solution.py
+++ b/solution.py
@@ -18,12 +18,18 @@
 H3R, H4R = 288, 144
 WIN3, WIN4 = 80, 48
 
-CHUNKS = [(3, 0, 1), (3, 1, 1), (3, 2, 1), (3, 3, 2), (4, 0, 1), (4, 1, 2), (3, 5, 3), (4, 3, 2)]
-CH3, CH4 = (0, 1, 2, 3, 6), (4, 5, 7)
+CHUNKS = [(3, 0, 1), (3, 1, 1), (3, 2, 1), (3, 3, 1), (3, 4, 1), (4, 0, 1), (3, 5, 3), (4, 1, 2), (4, 3, 2)]
+CH3, CH4 = (0, 1, 2, 3, 4, 6), (5, 7, 8)
 
 NEIGHBOURS = [(-1, -1), (-1, 1), (1, -1), (1, 1), (0, -1), (0, 1), (-1, 0), (1, 0)]
-X_ORDER = (1, 3, 2)
-Z_ORDER = (1, 7, 2, 6, 3, 5, 4)
+
+Z_HOPS = [(1, 1, 0), (7, -1, 0), (2, 2, 0), (6, -2, 0), (3, 1, 0), (5, -1, 0), (4, 2, 1), (4, -2, 2)]
+Z_RELAY = {2: (4, 6), 3: (5, 7)}
+X_HOPS = [(1, 1, 0), (3, -1, 0), (2, 2, 0)]
+X_RELAY = {}
+XR_HOPS = [(1, 1, 0), (3, -1, 0), (2, 1, 1), (2, -1, 2)]
+XR_RELAY = {0: (2,), 1: (3,)}
+RELAYED = (1, 2)
 
 
 def nt(a, b):
@@ -33,9 +39,9 @@
 def kernel(
     x_ref, i3_ref, i4_ref, w3_ref, w4_ref, lm_ref, ro_ref, o_ref,
     i3v, i4v, lmv, rov, own3, own4, sis3, sis4, cw3, cw4, s13, s14, wb3, wb4,
-    xc, xe, xh, s3c, s3e, s3h, s4c, s4e, s4h, jx, j3, j4, p4, xg, xk, tmp, lm, ro, up, pt, po,
+    xa, xi, xc, xe, xh, s3i, s3w, s4c, s4e, s4h, s4w, jx, j3, j4, p4, xg, xk, tmp, lm, ro, up, pt, po,
     load_sem, raw_s, raw_r, col_s, col_r, x_s, x_r, z_s, z_r, f_s, f_r,
-    xa_s, xa_r, xn_s, xn_r, n3_s, n3_r, n4_s, n4_r, out_s, out_r,
+    xa_s, xa_r, x0_s, x0_r, xn_s, xn_r, n3_s, n3_r, n4_s, n4_r, out_s, out_r,
 ):
     s = lax.axis_index("section")
     h = lax.axis_index("ha")
@@ -53,12 +59,14 @@
     def wait_bytes(view, sem):
         pltpu.make_async_copy(view, view, sem).wait()
 
-    for ref, n in ((xc, 1), (xh, 1), (s3c, 5), (s3h, 5), (s4c, 3), (s4h, 3)):
+    for ref, n in ((xi, 1), (xc, 1), (xh, 1), (s3i, 1), (s3w, 4), (s4c, 1), (s4h, 1), (s4w, 2)):
         ref[0:n] = jnp.zeros((n,) + ref.shape[1:], BF16)
+    j3[...] = jnp.zeros_like(j3)
+    j4[...] = jnp.zeros_like(j4)
     loads = [
         pltpu.make_async_copy(src, dst, load_sem.at[k])
         for k, (src, dst) in enumerate([
-            (w3_ref, own3), (w4_ref, own4), (x_ref.at[s], xc.at[0, s, 2:4]),
+            (w3_ref, own3), (w4_ref, own4), (x_ref.at[s], xa.at[s]),
             (i3_ref, i3v), (i4_ref, i4v), (lm_ref, lmv), (ro_ref, rov),
         ])
     ]
@@ -79,7 +87,7 @@
             v1, v2 = rows[:, 128:256], rows[:, 256:384]
             for k, v in enumerate((rows[:, :128], jnp.where(low, v2, v1), jnp.where(low, v1, v2))):
                 v = v.astype(BF16)
-                cw3[3 * tap + k] = cw3[3 * tap + k] + v if add else v
+                cw3[9 * k + tap] = cw3[9 * k + tap] + v if add else v
 
     def place4(shard, which, add):
         put = shifted(WIN4, 18, 4 * lax.rem(y, 4) + 18 * which)
@@ -95,7 +103,7 @@
     alone = (half == core) & (lax.rem(y, 2) == core)
     count = 0
     greet = [{"ha": sister}, {"ha": lax.rem(h + 2 * core + NH - 1, NH)}]
-    greet += [{"wa": lax.rem(w + d, NW)} for d in range(1, NW)]
+    greet += [{"wa": lax.rem(w + d, NW)} for d in (1, 2, NW - 2, NW - 1)]
     greet += [{"section": lax.rem(s + d, NS)} for d in range(1, NS)]
     greet += [
         {"ha": lax.rem(h + dy, NH), "wa": lax.rem(w + dx, NW)} for dy in (1, NH - 1) for dx in (1, NW - 1)
@@ -119,7 +127,7 @@
     raw4.start()
     for d in range(1, NS):
         m = lax.rem(s + d, NS)
-        remote(x_ref.at[m], xc.at[0, s, 2:4], xa_s, xa_r, section=m).start()
+        remote(x_ref.at[m], xa.at[s], xa_s, xa_r, section=m).start()
 
     raw3.wait_recv()
     place3(sis3, 1 - core, True)
@@ -151,26 +159,10 @@
     def column_wait(chunk):
         wait_bytes(column_parts(chunk)[2], col_r.at[chunk])
 
-    for chunk in range(4):
+    for chunk in range(5):
         column_start(chunk)
     raw4.wait_recv()
     place4(sis4, 1 - core, True)
-    for chunk in range(4, 8):
-        column_start(chunk)
-
-    def edges(e, t, tile, rows):
-        lanes = tile.shape[-1]
-        e[t, 0] = tile[:, 0:8, :].reshape(rows * 8, lanes).astype(BF16)
-        e[t, 1] = tile[:, tile.shape[1] - 8 :, :].reshape(rows * 8, lanes).astype(BF16)
-
-    def keep3(t, tile):
-        s3c[t, 2:4] = tile.astype(BF16)
-        edges(s3e, t, tile, 2)
-
-    def keep4(t, tile):
-        s4c[t, 4:8] = tile.astype(BF16)
-        edges(s4e, t, tile, 4)
-
     for load in loads[2:]:
         load.wait()
     tmp[...] = jnp.zeros_like(tmp)
@@ -182,17 +174,18 @@
     second = pltpu.roll(tmp[0:128, 128:256], 64, 1).astype(BF16)
     tmp[0:32, 0:128] = pltpu.roll(tmp[0:32, 0:128], 64, 1)
     tmp[0:32, 128:256] = pltpu.roll(tmp[0:32, 128:256], 64, 1)
-    keep3(0, tmp[0:32, 0:256].reshape(2, 16, 256))
+    s3i[0, 2:4, 16:32, :] = tmp[0:32, 0:256].reshape(2, 16, 256).astype(BF16)
     lm[0:96, 0:128] = first[32:128]
     lm[0:96, 128:256] = second[32:128]
     lm[96:128, :] = jnp.zeros((32, 256), BF16)
     third = pltpu.roll(tmp[128:272, 0:128], 96, 1)
-    keep4(0, third[0:128].reshape(4, 32, 128))
+    s4c[0, 4:8] = third[0:128].reshape(4, 32, 128).astype(BF16)
+    for k in range(2):
+        s4e[k] = third[0:128].reshape(4, 32, 128)[:, 24 * k : 24 * k + 8, :].reshape(32, 128).astype(BF16)
     ro[...] = third[128:144].astype(BF16)
     fine = lax.broadcasted_iota(jnp.int32, (384, 192), 0)
     cell = lax.broadcasted_iota(jnp.int32, (384, 192), 1)
     up[...] = jnp.where((fine // 64) * 32 + lax.rem(fine, 64) // 2 == cell, 1.0, 0.0).astype(BF16)
-    j4[:, :, 192:256] = jnp.zeros((12, 64, 64), F32)
 
     def away(dy, dx):
         oy = 1 - (h + NH - 1) // NH if dy < 0 else (h + 1) // NH if dy > 0 else 0
@@ -207,37 +200,60 @@
             where["wa"] = lax.rem(w + dx + NW, NW)
         return where
 
-    def send_tiles(c, e, halo, t, steps, rows, send, recv):
+    def send_rows(ref, t, steps, rows, send, recv):
+        for dy in (-1, 1):
+            to = t + steps * away(dy, 0)
+            remote(
+                ref.at[t, rows : 2 * rows], ref.at[to, rows * (1 - dy) : rows * (2 - dy)], send, recv, **neighbour(dy, 0)
+            ).start()
+
+    def send_3(t):
+        send_rows(s3w, t, 4, 2, n3_s.at[t], n3_r.at[t])
+
+    def send_4(t):
+        send_rows(s4w, t, 2, 4, n4_s.at[t], n4_r.at[t])
+
+    view_3 = s3w.at[0, 0:4]
+    view_4 = s4w.at[0, 0:8]
+    view_a = xa.at[0:3]
+    view_s3 = s3i.at[0:2, 0:4, 0:32]
+    view_x0 = xi.at[0:2, 0:4, 0:32]
+    view_x = xc.at[0:2, 0:3, 0:5]
+    view_s4 = s4c.at[0:2, 0:7]
+
+    def send_whole(src, dst, send, recv):
         for dy, dx in NEIGHBOURS:
-            to = t + steps * away(dy, dx)
+            remote(
+                src, dst.at[away(dy, dx), 2 - 2 * dy : 4 - 2 * dy, 16 - 16 * dx : 32 - 16 * dx], send, recv,
+                **neighbour(dy, dx),
+            ).start()
+
+    def send_borders():
+        send_whole(s3i.at[0, 2:4, 16:32], s3i, n3_s.at[4], n3_r.at[4])
+        wait_bytes(view_a, xa_r)
+        xi[0, 2:4, 16:32, :] = xa[0]
+        send_whole(xa.at[0], xi, x0_s, x0_r)
+        for lead in range(1, LEADS):
+            xc[0, lead - 1, 2:4] = xa[lead]
+            tile = xa[lead].astype(F32)
+            for k in range(2):
+                xe[lead - 1, k] = tile[:, 8 * k : 8 * k + 8, :].reshape(16, 192).astype(BF16)
+        for dy, dx in NEIGHBOURS:
+            to = away(dy, dx)
             if dx == 0:
-                src, dst = c.at[t, rows : 2 * rows], c.at[to, rows * (1 - dy) : rows * (2 - dy)]
+                one = xa.at[1:4], xc.at[to, :, 2 - 2 * dy : 4 - 2 * dy]
+                two = s4c.at[0, 4:8], s4c.at[to, 4 - 4 * dy : 8 - 4 * dy]
             else:
-                src, dst = e.at[t, (dx + 1) // 2], halo.at[to, (1 - dx) // 2, 1 - dy]
-            remote(src, dst, send, recv, **neighbour(dy, dx)).start()
-
-    def send_3(t):
-        send_tiles(s3c, s3e, s3h, t, 5, 2, n3_s.at[t], n3_r.at[t])
-
-    def send_4(t):
-        send_tiles(s4c, s4e, s4h, t, 3, 4, n4_s.at[t], n4_r.at[t])
-
-    view_3 = s3c.at[0:2, 0:5]
-    view_4 = s4c.at[0:2, 0:7]
-    view_x = xc.at[0:2, :, 0:5]
-    view_a = xc.at[0, 0:3, 2:4]
-
-    send_3(0)
-    wait_bytes(view_a, xa_r)
-    for lead in range(LEADS):
-        edges(xe.at[lead], 0, xc[0, lead, 2:4].astype(F32), 2)
-    for dy, dx in NEIGHBOURS:
-        if dx == 0:
-            src, dst = xc.at[0, :, 2:4], xc.at[away(dy, dx), :, 2 - 2 * dy : 4 - 2 * dy]
-        else:
-            src, dst = xe.at[:, 0, (dx + 1) // 2], xh.at[away(dy, dx), (1 - dx) // 2, 1 - dy]
-        remote(src, dst, xn_s, xn_r, **neighbour(dy, dx)).start()
-    send_4(0)
+                one = xe.at[:, (dx + 1) // 2], xh.at[to, (1 - dx) // 2, 1 - dy]
+                two = s4e.at[(dx + 1) // 2], s4h.at[to, (1 - dx) // 2, 1 - dy]
+            remote(*one, xn_s, xn_r, **neighbour(dy, dx)).start()
+            remote(*two, n4_s.at[2], n4_r.at[2], **neighbour(dy, dx)).start()
+
+    def wait_borders():
+        wait_bytes(view_s3, n3_r.at[4])
+        wait_bytes(view_x0, x0_r)
+        wait_bytes(view_x, xn_r)
+        wait_bytes(view_s4, n4_r.at[2])
 
     def merged3(slot):
         out = []
@@ -252,74 +268,88 @@
             [a[0:32], a[32:48] + b[0:16], b[16:32], b[32:48] + c[0:16], c[16:32], c[32:48] + d[0:16], d[16:48]], 0
         )
 
-    def piece(chunk, c, owner):
+    def hops(chunk):
         level, slot, n = CHUNKS[chunk]
-        return (wb3 if level == 3 else wb4).at[c, pl.ds(first_block(chunk, owner, owner), n)]
-
-    def along_wa(chunk):
-        return CHUNKS[chunk][1] == 0
-
-    def plane_copy(chunk, d, owner):
-        part = piece(chunk, core, owner)
-        if along_wa(chunk):
-            return remote(part, part, z_s.at[chunk, d], z_r.at[chunk, d], wa=lax.rem(w + d, NW))
-        return remote(part, part, x_s.at[chunk, d], x_r.at[chunk, d], section=lax.rem(s + d, NS))
-
-    def owner_of(chunk, d):
-        return lax.rem(w + NW - d, NW) if along_wa(chunk) else lax.rem(s + NS - d, NS)
-
-    def order(chunk):
+        if slot == 0:
+            return Z_HOPS, Z_RELAY
+        if slot <= (X3 if level == 3 else X4):
+            return (XR_HOPS, XR_RELAY) if chunk in RELAYED else (X_HOPS, X_RELAY)
+        return [], {}
+
+    def piece(chunk, owner, part):
         level, slot, n = CHUNKS[chunk]
-        return Z_ORDER if slot == 0 else X_ORDER if slot <= (X3 if level == 3 else X4) else ()
-
-    def share(chunk, d):
-        part = piece(chunk, core, owner_of(chunk, d))
-        remote(part, part, f_s.at[chunk], f_r.at[chunk], ha=sister).start()
+        wb, rows, cut = (wb3, H3R, 144) if level == 3 else (wb4, H4R, 80)
+        lo, hi = ((0, rows), (0, cut), (cut, rows))[part]
+        return wb.at[core, pl.ds(first_block(chunk, owner, owner), n), lo:hi]
+
+    def along(chunk):
+        return (w, NW, "wa", z_s, z_r) if CHUNKS[chunk][1] == 0 else (s, NS, "section", x_s, x_r)
+
+    def hop(chunk, k):
+        d, step, part = hops(chunk)[0][k]
+        me, size, axis, send, recv = along(chunk)
+        view = piece(chunk, lax.rem(me + step - d + 2 * size, size), part)
+        return remote(view, view, send.at[chunk, k], recv.at[chunk, k], **{axis: lax.rem(me + step + size, size)})
+
+    def received(chunk, k):
+        d, step, part = hops(chunk)[0][k]
+        me, size, axis, send, recv = along(chunk)
+        return piece(chunk, lax.rem(me - d + size, size), part), recv.at[chunk, k]
+
+    def share(chunk, view):
+        remote(view, view, f_s.at[chunk], f_r.at[chunk], ha=sister).start()
 
     def shared_view(chunk):
         level, slot, n = CHUNKS[chunk]
-        return (wb3 if level == 3 else wb4).at[0, 0 : (1 + len(order(chunk))) * n]
+        owners = 8 if slot == 0 else NS if slot <= (X3 if level == 3 else X4) else 1
+        return (wb3 if level == 3 else wb4).at[0, 0 : owners * n]
 
     def plane_start(chunk):
         level, slot, n = CHUNKS[chunk]
         column_wait(chunk)
         wb, merged = (wb3, merged3) if level == 3 else (wb4, merged4)
+        first = first_block(chunk, w, s)
         for k in range(n):
-            kb = first_block(chunk, w, s) + k
-            wb[pl.ds(core, 1), pl.ds(kb, 1)] = merged(slot + k)[None, None]
-        for d in order(chunk):
-            plane_copy(chunk, d, owner_of(chunk, 0)).start()
-        share(chunk, 0)
-
-    def plane_pass(chunk, ds):
-        for d in ds:
-            plane_copy(chunk, d, owner_of(chunk, d)).wait_recv()
-            share(chunk, d)
-
-    for chunk in (0, 1, 2, 3):
-        plane_start(chunk)
-    plane_pass(1, X_ORDER)
-    plane_pass(0, Z_ORDER[:4])
-    plane_pass(2, X_ORDER)
-    plane_pass(0, Z_ORDER[4:6])
+            wb[pl.ds(core, 1), pl.ds(first + k, 1)] = merged(slot + k)[None, None]
+        relayed = [k for ks in hops(chunk)[1].values() for k in ks]
+        for k in range(len(hops(chunk)[0])):
+            if k not in relayed:
+                hop(chunk, k).start()
+        share(chunk, piece(chunk, w if slot == 0 else s, 0))
+
+    def plane_pass(chunk, *ks):
+        for k in ks:
+            view, sem = received(chunk, k)
+            wait_bytes(view, sem)
+            for j in hops(chunk)[1].get(k, ()):
+                hop(chunk, j).start()
+            share(chunk, view)
+
+    send_borders()
+    for chunk in range(5, len(CHUNKS)):
+        column_start(chunk)
+    plane_start(0)
+    plane_start(1)
+    plane_start(2)
+    plane_pass(0, 0, 1)
+    plane_pass(1, 0, 1)
+    plane_start(3)
+    plane_pass(0, 2, 3)
     plane_start(4)
-    plane_pass(3, X_ORDER[:2])
+    plane_pass(2, 0, 1)
+    plane_pass(1, 2, 3)
+    plane_pass(0, 4, 5, 6, 7)
     plane_start(5)
-    plane_start(6)
-    plane_pass(0, Z_ORDER[6:])
-    plane_pass(3, X_ORDER[2:])
-    wait_bytes(view_3, n3_r.at[0])
-    wait_bytes(view_x, xn_r)
-    wait_bytes(view_4, n4_r.at[0])
-    for chunk in CH3:
-        wait_bytes(shared_view(chunk), f_r.at[chunk])
+    plane_pass(2, 2, 3)
+    plane_pass(3, 0, 1, 2)
+    wait_borders()
 
     def wide(halo, centre, rows):
         sides = [halo[k].astype(F32).reshape(rows, 8, centre.shape[-1]) for k in range(2)]
         return jnp.concatenate([sides[0], centre.astype(F32), sides[1]], 1)
 
     def blocks3(a, kinds):
-        return [3 * (3 * a + b) + kind for b in range(3) for kind in kinds]
+        return [9 * kind + 3 * a + b for b in range(3) for kind in kinds]
 
     def gates3(a, kinds):
         blocks = []
@@ -363,34 +393,40 @@
         )
         return sum(nt(u[a : a + rows].reshape(rows * cols, u.shape[2]), weights(a)) for a in range(3))
 
+    def inputs(t):
+        return xi[0].astype(F32) if t == 0 else wide(xh.at[0, :, :, t - 1], xc[0, t - 1], 6)
+
     def input_sums(t):
-        jx[:, 8:40, :] = wide(xh.at[0, :, :, t], xc[0, t], 6)[:, :, 0:128]
+        c0, c1 = (0, 48) if t == 0 else (8, 40)
+        jx[:, c0:c1, :] = inputs(t)[:, :, 0:128]
         xg[t] = conv(jx, 1, 4, 8, 32, lambda a: gates3(a, (0,)))
-        xk[t] = conv(jx, 2, 2, 16, 16, lambda a: cand3(a, (0,)))
+        xk[t] = conv(jx, 2, 2, 8, 32, lambda a: cand3(a, (0,)))
 
     def level3(t):
-        p = wide(s3h.at[t], s3c[t], 6)
-        j3[:, 8:40, 0:128] = p[:, :, 0:128]
-        j3[:, 8:40, 128:192] = wide(xh.at[0, :, :, t], xc[0, t], 6)[:, :, 128:192]
-        j3[:, 8:40, 192:256] = p[:, :, 192:256]
+        c0, c1 = (0, 48) if t == 0 else (8, 40)
+        p = s3i[0].astype(F32) if t == 0 else s3w[t - 1].astype(F32)
+        j3[:, c0:c1, 0:128] = p[:, :, 0:128]
+        j3[:, c0:c1, 128:192] = inputs(t)[:, :, 128:192]
+        j3[:, c0:c1, 192:256] = p[:, :, 192:256]
+        p = p[:, 8 - c0 : 40 - c0, :]
         sums = xg[t] + conv(j3, 1, 4, 8, 32, lambda a: gates3(a, (1, 2)))
         reset = jax.nn.sigmoid(sums[:, :256]).reshape(4, 32, 256)
-        update = jax.nn.sigmoid(sums[:, 256:]).reshape(4, 32, 256)[1:3, 8:24, :]
+        update = jax.nn.sigmoid(sums[:, 256:]).reshape(4, 32, 256)[1:3]
         gated = reset * p[1:5]
         j3[1:5, 8:40, 0:128] = gated[:, :, 0:128]
         j3[1:5, 8:40, 192:256] = gated[:, :, 192:256]
-        fresh = xk[t] + conv(j3, 2, 2, 16, 16, lambda a: cand3(a, (1, 2)))
-        fresh = jnp.maximum(fresh, 0.0).reshape(2, 16, 256)
-        prior = p[2:4, 8:24, :]
-        keep3(t + 1, update * prior + (1.0 - update) * fresh)
-        send_3(t + 1)
+        fresh = xk[t] + conv(j3, 2, 2, 8, 32, lambda a: cand3(a, (1, 2)))
+        fresh = jnp.maximum(fresh, 0.0).reshape(2, 32, 256)
+        state = update * p[2:4] + (1.0 - update) * fresh
+        col = lax.broadcasted_iota(jnp.int32, state.shape, 1) + (16 * w - 8)
+        s3w[t, 2:4] = jnp.where((col >= 0) & (col < 16 * NW), state, 0.0).astype(BF16)
+        send_3(t)
 
     def to_lead(t):
         return remote(pt.at[t], po.at[s], out_s.at[t], out_r, section=t)
 
     def lift(t):
-        coarse = wide(s3h.at[t + 1], s3c[t + 1], 6).astype(BF16).reshape(192, 256)
-        lifted = nt(coarse, lm[...]).astype(BF16)
+        lifted = nt(s3w[t].reshape(192, 256), lm[...]).astype(BF16)
         lifted = jnp.dot(up[...], lifted, preferred_element_type=F32).reshape(6, 64, 128)
         for i in range(12):
             j4[i, :, 0:96] = lifted[i // 2, :, 0:96]
@@ -398,7 +434,10 @@
     def level4(t):
         border = 2 if t == LEADS - 2 else 0
         g0, g1 = 3 - border, 9 + border
-        p = p4[...] if t == LEADS - 1 else wide(s4h.at[t], s4c[t], 12)
+        if t == 0:
+            p = wide(s4h.at[0], s4c[0], 12)
+        else:
+            p = p4[...] if t == LEADS - 1 else s4w[t - 1].astype(F32)
         j4[:, 8:56, 96:128] = p[:, :, 96:128]
         j4[:, 8:56, 128:192] = p[:, :, 0:64]
         sums = conv(j4, g0, g1 - g0, 8, 48, gates4)
@@ -407,21 +446,23 @@
         gated = reset * p[g0:g1]
         j4[g0:g1, 8:56, 96:128] = gated[:, :, 96:128]
         j4[g0:g1, 8:56, 128:192] = gated[:, :, 0:64]
-        c0, cols = (8, 48) if border else (16, 32)
+        c0, cols = (16, 32) if t == LEADS - 1 else (8, 48)
         rows = g1 - g0 - 2
         fresh = conv(j4, g0 + 1, rows, c0, cols, cand4)
         fresh = jnp.maximum(fresh, 0.0).reshape(rows, cols, 128)
         update, prior = update[1 : rows + 1, c0 - 8 : c0 - 8 + cols], p[g0 + 1 : g1 - 1, c0 - 8 : c0 - 8 + cols]
         state = update * prior + (1.0 - update) * fresh
-        if border:
+        if t < LEADS - 1:
             row = lax.broadcasted_iota(jnp.int32, state.shape, 0) + (4 * h + g0 + 1 - 4)
-            col = lax.broadcasted_iota(jnp.int32, state.shape, 1) + (32 * w + c0 - 16)
+            col = lax.broadcasted_iota(jnp.int32, state.shape, 1) + (32 * w - 8)
             inside = (row >= 0) & (row < 4 * NH) & (col >= 0) & (col < 32 * NW)
-            p4[g0 + 1 : g1 - 1] = jnp.where(inside, state, 0.0).astype(BF16).astype(F32)
-            state = state[border : border + 4, 8:40]
-        elif t < LEADS - 2:
-            keep4(t + 1, state)
-            send_4(t + 1)
+            state = jnp.where(inside, state, 0.0).astype(BF16)
+            if border:
+                p4[g0 + 1 : g1 - 1] = state.astype(F32)
+            else:
+                s4w[t, 4:8] = state
+                send_4(t)
+            state = state.astype(F32)[border : border + 4, 8:40]
         pt[t] = nt(ro[...], state.astype(BF16).reshape(128, 128))
 
         @pl.when(s == t)
@@ -432,24 +473,32 @@
         def _():
             to_lead(t).start()
 
+    for chunk in (0, 1):
+        wait_bytes(shared_view(chunk), f_r.at[chunk])
     input_sums(0)
+    plane_pass(4, 0, 1, 2)
+    plane_start(6)
+    plane_start(7)
+    for chunk in CH3[2:]:
+        wait_bytes(shared_view(chunk), f_r.at[chunk])
     level3(0)
-    plane_start(7)
+    plane_start(8)
+    plane_pass(5, 0, 1, 2, 3)
     for t in range(1, LEADS):
         input_sums(t)
-    plane_pass(5, X_ORDER)
     for t in range(LEADS):
-        wait_bytes(view_3, n3_r.at[t + 1])
+        wait_bytes(view_3, n3_r.at[t])
         if t + 1 < LEADS:
             level3(t + 1)
         if t == 0:
-            plane_pass(4, Z_ORDER)
+            plane_pass(7, 0, 1, 2)
+            plane_pass(5, 4, 5, 6, 7)
         lift(t)
         if t == 0:
             for chunk in CH4:
                 wait_bytes(shared_view(chunk), f_r.at[chunk])
-        if 0 < t < LEADS - 1:
-            wait_bytes(view_4, n4_r.at[t])
+        elif t < LEADS - 1:
+            wait_bytes(view_4, n4_r.at[t - 1])
         level4(t)
 
     wait_bytes(po.at[0:3], out_r)
@@ -458,10 +507,13 @@
     raw3.wait_send()
     raw4.wait_send()
     wait_bytes(view_a, xa_s)
+    wait_bytes(view_s3, n3_s.at[4])
+    wait_bytes(view_x0, x0_s)
     wait_bytes(view_x, xn_s)
-    for t in range(LEADS + 1):
+    wait_bytes(view_s4, n4_s.at[2])
+    for t in range(LEADS):
         wait_bytes(view_3, n3_s.at[t])
-    for t in range(LEADS - 1):
+    for t in range(LEADS - 2):
         wait_bytes(view_4, n4_s.at[t])
     for chunk in range(len(CHUNKS)):
         level, slot, n = CHUNKS[chunk]
@@ -472,8 +524,8 @@
         @pl.when(jnp.logical_not(alone))
         def _(s1=s1, slot=slot, n=n, chunk=chunk):
             wait_bytes(s1.at[:, slot : slot + n], col_s.at[chunk])
-        for d in order(chunk):
-            plane_copy(chunk, d, owner_of(chunk, 0)).wait_send()
+        for k in range(len(hops(chunk)[0])):
+            hop(chunk, k).wait_send()
         wait_bytes(shared_view(chunk), f_s.at[chunk])
     for t in range(LEADS):
         @pl.when(s != t)
@@ -504,21 +556,23 @@
             pltpu.VMEM((4, 1 + X4 + C4, WIN4, 128), BF16),
             pltpu.VMEM((2, K3, H3R, 128), BF16),
             pltpu.VMEM((2, K4, H4R, 128), BF16),
-            pltpu.VMEM((2, 4, 6, 16, 192), BF16),
-            pltpu.VMEM((4, 1, 2, 16, 192), BF16),
-            pltpu.VMEM((2, 2, 3, 4, 16, 192), BF16),
-            pltpu.VMEM((10, 6, 16, 256), BF16),
-            pltpu.VMEM((5, 2, 16, 256), BF16),
-            pltpu.VMEM((10, 2, 3, 16, 256), BF16),
-            pltpu.VMEM((6, 12, 32, 128), BF16),
-            pltpu.VMEM((3, 2, 32, 128), BF16),
-            pltpu.VMEM((6, 2, 3, 32, 128), BF16),
+            pltpu.VMEM((4, 2, 16, 192), BF16),
+            pltpu.VMEM((2, 6, 48, 192), BF16),
+            pltpu.VMEM((2, 3, 6, 16, 192), BF16),
+            pltpu.VMEM((3, 2, 16, 192), BF16),
+            pltpu.VMEM((2, 2, 3, 3, 16, 192), BF16),
+            pltpu.VMEM((2, 6, 48, 256), BF16),
+            pltpu.VMEM((8, 6, 32, 256), BF16),
+            pltpu.VMEM((2, 12, 32, 128), BF16),
+            pltpu.VMEM((2, 32, 128), BF16),
+            pltpu.VMEM((2, 2, 3, 32, 128), BF16),
+            pltpu.VMEM((4, 12, 48, 128), BF16),
             pltpu.VMEM((6, 48, 128), F32),
             pltpu.VMEM((6, 48, 256), F32),
             pltpu.VMEM((12, 64, 256), F32),
             pltpu.VMEM((12, 48, 128), F32),
             pltpu.VMEM((4, 128, 512), F32),
-            pltpu.VMEM((4, 32, 256), F32),
+            pltpu.VMEM((4, 64, 256), F32),
             pltpu.VMEM((272, 256), F32),
             pltpu.VMEM((128, 256), BF16),
             pltpu.VMEM((16, 128), BF16),
@@ -527,7 +581,7 @@
             pltpu.VMEM((4, 16, 128), F32),
             dma((7,)), dma((2,)), dma((2,)), dma((n,)), dma((n,)),
             dma((n, NS)), dma((n, NS)), dma((n, NW)), dma((n, NW)), dma((n,)), dma((n,)),
-            dma, dma, dma, dma, dma((5,)), dma((5,)), dma((3,)), dma((3,)), dma((4,)), dma,
+            dma, dma, dma, dma, dma, dma, dma((5,)), dma((5,)), dma((3,)), dma((3,)), dma((4,)), dma,
         ],
         compiler_params=pltpu.CompilerParams(
             collective_id=0, has_side_effects=True, vmem_limit_bytes=64 << 20

time: 71.6 us -> 67.7 us (0.946)
  Pallas kernels: 69.8 us -> 66 us
    pallas_call x1, Pallas kernels: 69.8 us -> 66 us  [local(): pl.pallas_call(kernel, out_shape=jax.ShapeDtypeStruct((4, 16, 128), F32),...]
where the time goes in v4:
time: 67.7 us; the launch traced here: 67.5 us
  Pallas kernels  66 us (97%)
  local copies, waits for them, and re-layouts  1.53 us (2%)
    pallas_call x1, Pallas kernels, local(): pl.pallas_call(kernel, out_shape=jax.ShapeDtypeStruct((4, 16, 128), F32),...  66 us
    reshape x1, local copies, waits for them, and re-layouts, local(): return fields.reshape(1, 4, 16, 4, 32)  1.53 us

profile of v4, /device:TPU:6, one launch (start us, length us, event | category | flops | bytes accessed | tf_op | source)
XLA Modules:
  0.0 67.5 jit_solution(14179855470508391136)
XLA Ops:
  0.0 66.0 %nowcast.1 = f32[4,16,128]{2,1,0:T(8,128)} custom-call(bf16[4,2,16,192]{3,2,1,0:T(8,128)(2,1)} %bitcast.9, bf16[2,16,192]{2,1,0:T(8,128)(2,1)} %bitcast.11, bf16[4,32,96]{2,1,0:T(8,128)(2,1)} %bitcast.10, bf16[9,36,384]{2,1,0:T(8,128)(2,1)} %bitcast.7, bf16[9,18,192]{2,1,0:T(8,128)(2,1)} %bitcast.8, bf16[96,192]{1,0:T(8,128)(2,1)} %lm_ref.1, ...), custom_call_target="tpu_custom_call" | custom-call | tf_op jit(solution)/shard_map/nowcast/pallas_call | solution.py:539
  66.0 1.5 %reshape.3 = f32[1,4,16,4,32]{4,3,2,1,0:T(4,128)} reshape(f32[4,16,128]{2,1,0:T(8,128)} %nowcast.1) | data formatting | bytes 65536 | tf_op jit(solution)/shard_map/reshape | solution.py:599

commit v5 on v4

--- a/solution.py
+++ b/solution.py
@@ -25,11 +25,14 @@
 
 Z_HOPS = [(1, 1, 0), (7, -1, 0), (2, 2, 0), (6, -2, 0), (3, 1, 0), (5, -1, 0), (4, 2, 1), (4, -2, 2)]
 Z_RELAY = {2: (4, 6), 3: (5, 7)}
+ZD_HOPS = [(1, 1, 0), (7, -1, 0), (2, 2, 0), (6, -2, 0), (3, 3, 0), (5, -3, 0), (4, 4, 0)]
 X_HOPS = [(1, 1, 0), (3, -1, 0), (2, 2, 0)]
 X_RELAY = {}
 XR_HOPS = [(1, 1, 0), (3, -1, 0), (2, 1, 1), (2, -1, 2)]
 XR_RELAY = {0: (2,), 1: (3,)}
 RELAYED = (1, 2)
+Z_CHUNKS = [k for k, (level, slot, n) in enumerate(CHUNKS) if slot == 0]
+X_CHUNKS = [k for k, (level, slot, n) in enumerate(CHUNKS) if 0 < slot <= (X3 if level == 3 else X4)]
 
 
 def nt(a, b):
@@ -39,8 +42,8 @@
 def kernel(
     x_ref, i3_ref, i4_ref, w3_ref, w4_ref, lm_ref, ro_ref, o_ref,
     i3v, i4v, lmv, rov, own3, own4, sis3, sis4, cw3, cw4, s13, s14, wb3, wb4,
-    xa, xi, xc, xe, xh, s3i, s3w, s4c, s4e, s4h, s4w, jx, j3, j4, p4, xg, xk, tmp, lm, ro, up, pt, po,
-    load_sem, raw_s, raw_r, col_s, col_r, x_s, x_r, z_s, z_r, f_s, f_r,
+    xa, xi, xc, xe, xh, s3i, s3w, s4c, s4e, s4h, s4w, xw, pw, jx, j3, j4, p4, xg, xk, tmp, lm, ro, up, pt, po,
+    load_sem, raw_s, raw_r, col_s, col_r, plane_s, x_r, z_r, f_s, f_r,
     xa_s, xa_r, x0_s, x0_r, xn_s, xn_r, n3_s, n3_r, n4_s, n4_r, out_s, out_r,
 ):
     s = lax.axis_index("section")
@@ -59,10 +62,11 @@
     def wait_bytes(view, sem):
         pltpu.make_async_copy(view, view, sem).wait()
 
-    for ref, n in ((xi, 1), (xc, 1), (xh, 1), (s3i, 1), (s3w, 4), (s4c, 1), (s4h, 1), (s4w, 2)):
+    for ref, n in ((xi, 1), (xc, 1), (xh, 1), (s3i, 1), (s4c, 1), (s4h, 1)):
         ref[0:n] = jnp.zeros((n,) + ref.shape[1:], BF16)
-    j3[...] = jnp.zeros_like(j3)
-    j4[...] = jnp.zeros_like(j4)
+    for ref, n, rows in ((s3w, 4, 2), (s4w, 3, 4)):
+        for first in (0, 2 * rows):
+            ref[0:n, first : first + rows] = jnp.zeros((n, rows) + ref.shape[2:], BF16)
     loads = [
         pltpu.make_async_copy(src, dst, load_sem.at[k])
         for k, (src, dst) in enumerate([
@@ -102,12 +106,12 @@
     barrier = pltpu.get_barrier_semaphore()
     alone = (half == core) & (lax.rem(y, 2) == core)
     count = 0
-    greet = [{"ha": sister}, {"ha": lax.rem(h + 2 * core + NH - 1, NH)}]
-    greet += [{"wa": lax.rem(w + d, NW)} for d in (1, 2, NW - 2, NW - 1)]
-    greet += [{"section": lax.rem(s + d, NS)} for d in range(1, NS)]
-    greet += [
+    greet = [
         {"ha": lax.rem(h + dy, NH), "wa": lax.rem(w + dx, NW)} for dy in (1, NH - 1) for dx in (1, NW - 1)
     ]
+    greet += [{"wa": lax.rem(w + d, NW)} for d in (4, 3, 5, 2, 6, 1, 7)]
+    greet += [{"section": lax.rem(s + d, NS)} for d in (2, 1, 3)]
+    greet += [{"ha": lax.rem(h + 2 * core + NH - 1, NH)}, {"ha": sister}]
     for where in greet:
         pl.semaphore_signal(barrier, inc=1, device_id=where, device_id_type=MESH)
     for i in range(4):
@@ -115,6 +119,8 @@
         @pl.when(source != h)
         def _(source=source):
             pl.semaphore_signal(barrier, inc=1, device_id={"ha": source}, device_id_type=MESH)
+    for ref in (j3, j4, xw):
+        ref[...] = jnp.zeros_like(ref)
     loads[0].wait()
     place3(own3, core, False)
     loads[1].wait()
@@ -151,7 +157,7 @@
             target = 2 * (2 * i + core) + half
             @pl.when(target != h)
             def _(target=target):
-                remote(src, dst, col_s.at[chunk], col_r.at[chunk], ha=target).start()
+                remote(src, dst, col_s.at[CHUNKS[chunk][0] - 3], col_r.at[chunk], ha=target).start()
         @pl.when(alone)
         def _():
             pltpu.make_async_copy(src, dst, col_r.at[chunk]).start()
@@ -187,6 +193,10 @@
     cell = lax.broadcasted_iota(jnp.int32, (384, 192), 1)
     up[...] = jnp.where((fine // 64) * 32 + lax.rem(fine, 64) // 2 == cell, 1.0, 0.0).astype(BF16)
 
+    def wide(halo, centre, rows):
+        sides = [halo[k].astype(F32).reshape(rows, 8, centre.shape[-1]) for k in range(2)]
+        return jnp.concatenate([sides[0], centre.astype(F32), sides[1]], 1)
+
     def away(dy, dx):
         oy = 1 - (h + NH - 1) // NH if dy < 0 else (h + 1) // NH if dy > 0 else 0
         ox = 1 - (w + NW - 1) // NW if dx < 0 else (w + 1) // NW if dx > 0 else 0
@@ -208,10 +218,10 @@
             ).start()
 
     def send_3(t):
-        send_rows(s3w, t, 4, 2, n3_s.at[t], n3_r.at[t])
+        send_rows(s3w, t, 4, 2, n3_s.at[0], n3_r.at[t])
 
     def send_4(t):
-        send_rows(s4w, t, 2, 4, n4_s.at[t], n4_r.at[t])
+        send_rows(s4w, t, 3, 4, n4_s.at[1], n4_r.at[t])
 
     view_3 = s3w.at[0, 0:4]
     view_4 = s4w.at[0, 0:8]
@@ -229,7 +239,7 @@
             ).start()
 
     def send_borders():
-        send_whole(s3i.at[0, 2:4, 16:32], s3i, n3_s.at[4], n3_r.at[4])
+        send_whole(s3i.at[0, 2:4, 16:32], s3i, n3_s.at[1], n3_r.at[4])
         wait_bytes(view_a, xa_r)
         xi[0, 2:4, 16:32, :] = xa[0]
         send_whole(xa.at[0], xi, x0_s, x0_r)
@@ -247,13 +257,18 @@
                 one = xe.at[:, (dx + 1) // 2], xh.at[to, (1 - dx) // 2, 1 - dy]
                 two = s4e.at[(dx + 1) // 2], s4h.at[to, (1 - dx) // 2, 1 - dy]
             remote(*one, xn_s, xn_r, **neighbour(dy, dx)).start()
-            remote(*two, n4_s.at[2], n4_r.at[2], **neighbour(dy, dx)).start()
+            remote(*two, n4_s.at[0], n4_r.at[0], **neighbour(dy, dx)).start()
 
     def wait_borders():
         wait_bytes(view_s3, n3_r.at[4])
         wait_bytes(view_x0, x0_r)
         wait_bytes(view_x, xn_r)
-        wait_bytes(view_s4, n4_r.at[2])
+        wait_bytes(view_s4, n4_r.at[0])
+        s4w[0] = wide(s4h.at[0], s4c[0], 12).astype(BF16)
+        pw[...] = s3i[0].astype(F32)
+        xw[0] = xi[0].astype(F32)
+        for lead in range(1, LEADS):
+            xw[lead, :, 8:40, :] = wide(xh.at[0, :, :, lead - 1], xc[0, lead - 1], 6)
 
     def merged3(slot):
         out = []
@@ -271,7 +286,7 @@
     def hops(chunk):
         level, slot, n = CHUNKS[chunk]
         if slot == 0:
-            return Z_HOPS, Z_RELAY
+            return (Z_HOPS, Z_RELAY) if level == 3 else (ZD_HOPS, {})
         if slot <= (X3 if level == 3 else X4):
             return (XR_HOPS, XR_RELAY) if chunk in RELAYED else (X_HOPS, X_RELAY)
         return [], {}
@@ -283,21 +298,24 @@
         return wb.at[core, pl.ds(first_block(chunk, owner, owner), n), lo:hi]
 
     def along(chunk):
-        return (w, NW, "wa", z_s, z_r) if CHUNKS[chunk][1] == 0 else (s, NS, "section", x_s, x_r)
+        if chunk in Z_CHUNKS:
+            return w, NW, "wa", z_r.at[Z_CHUNKS.index(chunk)]
+        return s, NS, "section", x_r.at[X_CHUNKS.index(chunk)]
 
     def hop(chunk, k):
         d, step, part = hops(chunk)[0][k]
-        me, size, axis, send, recv = along(chunk)
+        me, size, axis, recv = along(chunk)
         view = piece(chunk, lax.rem(me + step - d + 2 * size, size), part)
-        return remote(view, view, send.at[chunk, k], recv.at[chunk, k], **{axis: lax.rem(me + step + size, size)})
+        to = lax.rem(me + step + size, size)
+        return remote(view, view, plane_s.at[CHUNKS[chunk][0] - 3], recv.at[k], **{axis: to})
 
     def received(chunk, k):
         d, step, part = hops(chunk)[0][k]
-        me, size, axis, send, recv = along(chunk)
-        return piece(chunk, lax.rem(me - d + size, size), part), recv.at[chunk, k]
+        me, size, axis, recv = along(chunk)
+        return piece(chunk, lax.rem(me - d + size, size), part), recv.at[k]
 
     def share(chunk, view):
-        remote(view, view, f_s.at[chunk], f_r.at[chunk], ha=sister).start()
+        remote(view, view, f_s.at[CHUNKS[chunk][0] - 3], f_r.at[chunk], ha=sister).start()
 
     def shared_view(chunk):
         level, slot, n = CHUNKS[chunk]
@@ -344,10 +362,6 @@
     plane_pass(3, 0, 1, 2)
     wait_borders()
 
-    def wide(halo, centre, rows):
-        sides = [halo[k].astype(F32).reshape(rows, 8, centre.shape[-1]) for k in range(2)]
-        return jnp.concatenate([sides[0], centre.astype(F32), sides[1]], 1)
-
     def blocks3(a, kinds):
         return [9 * kind + 3 * a + b for b in range(3) for kind in kinds]
 
@@ -393,22 +407,17 @@
         )
         return sum(nt(u[a : a + rows].reshape(rows * cols, u.shape[2]), weights(a)) for a in range(3))
 
-    def inputs(t):
-        return xi[0].astype(F32) if t == 0 else wide(xh.at[0, :, :, t - 1], xc[0, t - 1], 6)
-
     def input_sums(t):
-        c0, c1 = (0, 48) if t == 0 else (8, 40)
-        jx[:, c0:c1, :] = inputs(t)[:, :, 0:128]
+        jx[...] = xw[t, :, :, 0:128]
         xg[t] = conv(jx, 1, 4, 8, 32, lambda a: gates3(a, (0,)))
         xk[t] = conv(jx, 2, 2, 8, 32, lambda a: cand3(a, (0,)))
 
     def level3(t):
-        c0, c1 = (0, 48) if t == 0 else (8, 40)
-        p = s3i[0].astype(F32) if t == 0 else s3w[t - 1].astype(F32)
-        j3[:, c0:c1, 0:128] = p[:, :, 0:128]
-        j3[:, c0:c1, 128:192] = inputs(t)[:, :, 128:192]
-        j3[:, c0:c1, 192:256] = p[:, :, 192:256]
-        p = p[:, 8 - c0 : 40 - c0, :]
+        p = pw[...]
+        j3[:, :, 0:128] = p[:, :, 0:128]
+        j3[:, :, 128:192] = xw[t, :, :, 128:192]
+        j3[:, :, 192:256] = p[:, :, 192:256]
+        p = p[:, 8:40, :]
         sums = xg[t] + conv(j3, 1, 4, 8, 32, lambda a: gates3(a, (1, 2)))
         reset = jax.nn.sigmoid(sums[:, :256]).reshape(4, 32, 256)
         update = jax.nn.sigmoid(sums[:, 256:]).reshape(4, 32, 256)[1:3]
@@ -423,7 +432,7 @@
         send_3(t)
 
     def to_lead(t):
-        return remote(pt.at[t], po.at[s], out_s.at[t], out_r, section=t)
+        return remote(pt.at[t], po.at[s], out_s, out_r, section=t)
 
     def lift(t):
         lifted = nt(s3w[t].reshape(192, 256), lm[...]).astype(BF16)
@@ -431,13 +440,9 @@
         for i in range(12):
             j4[i, :, 0:96] = lifted[i // 2, :, 0:96]
 
-    def level4(t):
-        border = 2 if t == LEADS - 2 else 0
+    def level4(t, border=0, last=False):
         g0, g1 = 3 - border, 9 + border
-        if t == 0:
-            p = wide(s4h.at[0], s4c[0], 12)
-        else:
-            p = p4[...] if t == LEADS - 1 else s4w[t - 1].astype(F32)
+        p = p4[...] if last else s4w[t].astype(F32)
         j4[:, 8:56, 96:128] = p[:, :, 96:128]
         j4[:, 8:56, 128:192] = p[:, :, 0:64]
         sums = conv(j4, g0, g1 - g0, 8, 48, gates4)
@@ -446,13 +451,13 @@
         gated = reset * p[g0:g1]
         j4[g0:g1, 8:56, 96:128] = gated[:, :, 96:128]
         j4[g0:g1, 8:56, 128:192] = gated[:, :, 0:64]
-        c0, cols = (16, 32) if t == LEADS - 1 else (8, 48)
+        c0, cols = (16, 32) if last else (8, 48)
         rows = g1 - g0 - 2
         fresh = conv(j4, g0 + 1, rows, c0, cols, cand4)
         fresh = jnp.maximum(fresh, 0.0).reshape(rows, cols, 128)
         update, prior = update[1 : rows + 1, c0 - 8 : c0 - 8 + cols], p[g0 + 1 : g1 - 1, c0 - 8 : c0 - 8 + cols]
         state = update * prior + (1.0 - update) * fresh
-        if t < LEADS - 1:
+        if not last:
             row = lax.broadcasted_iota(jnp.int32, state.shape, 0) + (4 * h + g0 + 1 - 4)
             col = lax.broadcasted_iota(jnp.int32, state.shape, 1) + (32 * w - 8)
             inside = (row >= 0) & (row < 4 * NH) & (col >= 0) & (col < 32 * NW)
@@ -460,8 +465,8 @@
             if border:
                 p4[g0 + 1 : g1 - 1] = state.astype(F32)
             else:
-                s4w[t, 4:8] = state
-                send_4(t)
+                s4w[t + 1, 4:8] = state
+                send_4(t + 1)
             state = state.astype(F32)[border : border + 4, 8:40]
         pt[t] = nt(ro[...], state.astype(BF16).reshape(128, 128))
 
@@ -481,25 +486,47 @@
     plane_start(7)
     for chunk in CH3[2:]:
         wait_bytes(shared_view(chunk), f_r.at[chunk])
-    level3(0)
-    plane_start(8)
-    plane_pass(5, 0, 1, 2, 3)
-    for t in range(1, LEADS):
-        input_sums(t)
-    for t in range(LEADS):
-        wait_bytes(view_3, n3_r.at[t])
-        if t + 1 < LEADS:
-            level3(t + 1)
-        if t == 0:
+
+    @pl.loop(0, LEADS)
+    def _(t):
+        @pl.when(t > 0)
+        def _():
+            wait_bytes(view_3, n3_r.at[t - 1])
+            pw[:, 8:40, :] = s3w[t - 1].astype(F32)
+
+        level3(t)
+
+        @pl.when(t == 0)
+        def _():
+            plane_start(8)
+            pl.loop(1, LEADS)(input_sums)
+            plane_pass(5, 0, 1, 2, 3, 4, 5, 6)
             plane_pass(7, 0, 1, 2)
-            plane_pass(5, 4, 5, 6, 7)
-        lift(t)
-        if t == 0:
+
+        @pl.when(t > 0)
+        def _():
+            lift(t - 1)
+
+        @pl.when(t == 1)
+        def _():
             for chunk in CH4:
                 wait_bytes(shared_view(chunk), f_r.at[chunk])
-        elif t < LEADS - 1:
+
+        @pl.when(t > 1)
+        def _():
             wait_bytes(view_4, n4_r.at[t - 1])
-        level4(t)
+
+        @pl.when((t > 0) & (t < LEADS - 1))
+        def _():
+            level4(t - 1)
+
+        @pl.when(t == LEADS - 1)
+        def _():
+            level4(t - 1, border=2)
+
+    wait_bytes(view_3, n3_r.at[LEADS - 1])
+    lift(LEADS - 1)
+    level4(LEADS - 1, last=True)
 
     wait_bytes(po.at[0:3], out_r)
     o_ref[...] = po[...]
@@ -507,30 +534,22 @@
     raw3.wait_send()
     raw4.wait_send()
     wait_bytes(view_a, xa_s)
-    wait_bytes(view_s3, n3_s.at[4])
+    wait_bytes(view_s3, n3_s.at[1])
     wait_bytes(view_x0, x0_s)
     wait_bytes(view_x, xn_s)
-    wait_bytes(view_s4, n4_s.at[2])
-    for t in range(LEADS):
-        wait_bytes(view_3, n3_s.at[t])
-    for t in range(LEADS - 2):
-        wait_bytes(view_4, n4_s.at[t])
-    for chunk in range(len(CHUNKS)):
-        level, slot, n = CHUNKS[chunk]
-        s1 = s13 if level == 3 else s14
+    wait_bytes(view_s4, n4_s.at[0])
+    wait_bytes(s3w.at[0:4, 0:4], n3_s.at[0])
+    wait_bytes(s4w.at[0:2, 0:8], n4_s.at[1])
+    for k, (wb, s1, per) in enumerate(((wb3, s13, X3), (wb4, s14, X4))):
+        wait_bytes(wb.at[0, 0 : 7 + 3 * per], plane_s.at[k])
+        wait_bytes(wb.at[0], f_s.at[k])
         @pl.when(alone)
-        def _(s1=s1, slot=slot, n=n, chunk=chunk):
-            wait_bytes(s1.at[0:3, slot : slot + n], col_s.at[chunk])
+        def _(s1=s1, k=k):
+            wait_bytes(s1.at[0:3], col_s.at[k])
         @pl.when(jnp.logical_not(alone))
-        def _(s1=s1, slot=slot, n=n, chunk=chunk):
-            wait_bytes(s1.at[:, slot : slot + n], col_s.at[chunk])
-        for k in range(len(hops(chunk)[0])):
-            hop(chunk, k).wait_send()
-        wait_bytes(shared_view(chunk), f_s.at[chunk])
-    for t in range(LEADS):
-        @pl.when(s != t)
-        def _(t=t):
-            to_lead(t).wait_send()
+        def _(s1=s1, k=k):
+            wait_bytes(s1, col_s.at[k])
+    wait_bytes(pt.at[0:3], out_s)
 
 
 def local(coarse_inputs, init_level3, init_level4, weight_level3, weight_level4, lift_map, readout):
@@ -566,7 +585,9 @@
             pltpu.VMEM((2, 12, 32, 128), BF16),
             pltpu.VMEM((2, 32, 128), BF16),
             pltpu.VMEM((2, 2, 3, 32, 128), BF16),
-            pltpu.VMEM((4, 12, 48, 128), BF16),
+            pltpu.VMEM((6, 12, 48, 128), BF16),
+            pltpu.VMEM((4, 6, 48, 192), F32),
+            pltpu.VMEM((6, 48, 256), F32),
             pltpu.VMEM((6, 48, 128), F32),
             pltpu.VMEM((6, 48, 256), F32),
             pltpu.VMEM((12, 64, 256), F32),
@@ -579,9 +600,9 @@
             pltpu.VMEM((384, 192), BF16),
             pltpu.VMEM((4, 16, 128), F32),
             pltpu.VMEM((4, 16, 128), F32),
-            dma((7,)), dma((2,)), dma((2,)), dma((n,)), dma((n,)),
-            dma((n, NS)), dma((n, NS)), dma((n, NW)), dma((n, NW)), dma((n,)), dma((n,)),
-            dma, dma, dma, dma, dma, dma, dma((5,)), dma((5,)), dma((3,)), dma((3,)), dma((4,)), dma,
+            dma((7,)), dma((2,)), dma((2,)), dma((2,)), dma((n,)),
+            dma((2,)), dma((len(X_CHUNKS), NS)), dma((len(Z_CHUNKS), NW)), dma((2,)), dma((n,)),
+            dma, dma, dma, dma, dma, dma, dma((2,)), dma((5,)), dma((2,)), dma((3,)), dma, dma,
         ],
         compiler_params=pltpu.CompilerParams(
             collective_id=0, has_side_effects=True, vmem_limit_bytes=64 << 20

time: 67.7 us -> 64.9 us (0.959)
  Pallas kernels: 66 us -> 63.2 us
    pallas_call x1, Pallas kernels: 66 us -> 63.2 us  [local(): pl.pallas_call(kernel, out_shape=jax.ShapeDtypeStruct((4, 16, 128), F32),...]
where the time goes in v5:
time: 64.9 us; the launch traced here: 64.7 us
  Pallas kernels  63.2 us (97%)
  local copies, waits for them, and re-layouts  1.53 us (2%)
    pallas_call x1, Pallas kernels, local(): pl.pallas_call(kernel, out_shape=jax.ShapeDtypeStruct((4, 16, 128), F32),...  63.2 us
    reshape x1, local copies, waits for them, and re-layouts, local(): return fields.reshape(1, 4, 16, 4, 32)  1.53 us

profile of v5, /device:TPU:6, one launch (start us, length us, event | category | flops | bytes accessed | tf_op | source)
XLA Modules:
  0.0 64.7 jit_solution(16027093932470215865)
XLA Ops:
  0.0 63.2 %nowcast.1 = f32[4,16,128]{2,1,0:T(8,128)} custom-call(bf16[4,2,16,192]{3,2,1,0:T(8,128)(2,1)} %bitcast.9, bf16[2,16,192]{2,1,0:T(8,128)(2,1)} %bitcast.11, bf16[4,32,96]{2,1,0:T(8,128)(2,1)} %bitcast.10, bf16[9,36,384]{2,1,0:T(8,128)(2,1)} %bitcast.7, bf16[9,18,192]{2,1,0:T(8,128)(2,1)} %bitcast.8, bf16[96,192]{1,0:T(8,128)(2,1)} %lm_ref.1, ...), custom_call_target="tpu_custom_call" | custom-call | tf_op jit(solution)/shard_map/nowcast/pallas_call | solution.py:558
  63.2 1.5 %reshape.3 = f32[1,4,16,4,32]{4,3,2,1,0:T(4,128)} reshape(f32[4,16,128]{2,1,0:T(8,128)} %nowcast.1) | data formatting | bytes 65536 | tf_op jit(solution)/shard_map/reshape | solution.py:620

commit v6 on v5

--- a/solution.py
+++ b/solution.py
@@ -41,7 +41,7 @@
 
 def kernel(
     x_ref, i3_ref, i4_ref, w3_ref, w4_ref, lm_ref, ro_ref, o_ref,
-    i3v, i4v, lmv, rov, own3, own4, sis3, sis4, cw3, cw4, s13, s14, wb3, wb4,
+    i3v, i4v, lmv, rov, own3, own4, sis3, sis4, cw3, cw4, early, s1e, s13, s14, wb3, wb4,
     xa, xi, xc, xe, xh, s3i, s3w, s4c, s4e, s4h, s4w, xw, pw, jx, j3, j4, p4, xg, xk, tmp, lm, ro, up, pt, po,
     load_sem, raw_s, raw_r, col_s, col_r, plane_s, x_r, z_r, f_s, f_r,
     xa_s, xa_r, x0_s, x0_r, xn_s, xn_r, n3_s, n3_r, n4_s, n4_r, out_s, out_r,
@@ -114,8 +114,8 @@
     greet += [{"ha": lax.rem(h + 2 * core + NH - 1, NH)}, {"ha": sister}]
     for where in greet:
         pl.semaphore_signal(barrier, inc=1, device_id=where, device_id_type=MESH)
-    for i in range(4):
-        source = 2 * (4 * core + i) + lax.rem(y, 2)
+    for i in range(8):
+        source = 8 * core + i
         @pl.when(source != h)
         def _(source=source):
             pl.semaphore_signal(barrier, inc=1, device_id={"ha": source}, device_id_type=MESH)
@@ -123,14 +123,27 @@
         ref[...] = jnp.zeros_like(ref)
     loads[0].wait()
     place3(own3, core, False)
+    for j, block in enumerate((w, 8 + X3 * s)):
+        early[j] = cw3[block, pl.ds(pl.multiple_of(32 * core, 16), 48), :]
     loads[1].wait()
     place4(own4, core, False)
-    pl.semaphore_wait(barrier, len(greet) + 4 - alone.astype(jnp.int32))
+    pl.semaphore_wait(barrier, len(greet) + 8 - (half == core).astype(jnp.int32))
 
     raw3 = remote(w3_ref, sis3, raw_s.at[0], raw_r.at[0], ha=sister)
     raw4 = remote(w4_ref, sis4, raw_s.at[1], raw_r.at[1], ha=sister)
     raw3.start()
     raw4.start()
+
+    for j in range(2):
+        landing = s1e.at[j, lax.rem(h, 8)]
+        for i in range(8):
+            target = 2 * i + half
+            @pl.when(target != h)
+            def _(target=target, j=j, landing=landing):
+                remote(early.at[j], landing, col_s.at[2], col_r.at[j], ha=target).start()
+        @pl.when(half == core)
+        def _(j=j, landing=landing):
+            pltpu.make_async_copy(early.at[j], landing, col_r.at[j]).start()
     for d in range(1, NS):
         m = lax.rem(s + d, NS)
         remote(x_ref.at[m], xa.at[s], xa_s, xa_r, section=m).start()
@@ -163,12 +176,16 @@
             pltpu.make_async_copy(src, dst, col_r.at[chunk]).start()
 
     def column_wait(chunk):
+        if chunk < 2:
+            wait_bytes(s1e.at[chunk], col_r.at[chunk])
+            return
         wait_bytes(column_parts(chunk)[2], col_r.at[chunk])
 
-    for chunk in range(5):
+    for chunk in range(2, 5):
         column_start(chunk)
     raw4.wait_recv()
     place4(sis4, 1 - core, True)
+    column_start(5)
     for load in loads[2:]:
         load.wait()
     tmp[...] = jnp.zeros_like(tmp)
@@ -270,10 +287,16 @@
         for lead in range(1, LEADS):
             xw[lead, :, 8:40, :] = wide(xh.at[0, :, :, lead - 1], xc[0, lead - 1], 6)
 
+    def window3(i, slot):
+        if slot > 1:
+            return s13[i, slot]
+        a, b = s1e[slot, 2 * i], s1e[slot, 2 * i + 1]
+        return jnp.concatenate([a[0:32], a[32:48] + b[0:16], b[16:48]], 0)
+
     def merged3(slot):
         out = []
         for g in (0, 2):
-            a, b = s13[g, slot], s13[g + 1, slot]
+            a, b = window3(g, slot), window3(g + 1, slot)
             out += [a[0:64], a[64:80] + b[0:16], b[16:80]]
         return jnp.concatenate(out, 0)
 
@@ -344,11 +367,12 @@
             share(chunk, view)
 
     send_borders()
-    for chunk in range(5, len(CHUNKS)):
-        column_start(chunk)
+    column_start(6)
     plane_start(0)
     plane_start(1)
     plane_start(2)
+    column_start(7)
+    column_start(8)
     plane_pass(0, 0, 1)
     plane_pass(1, 0, 1)
     plane_start(3)
@@ -540,7 +564,15 @@
     wait_bytes(view_s4, n4_s.at[0])
     wait_bytes(s3w.at[0:4, 0:4], n3_s.at[0])
     wait_bytes(s4w.at[0:2, 0:8], n4_s.at[1])
-    for k, (wb, s1, per) in enumerate(((wb3, s13, X3), (wb4, s14, X4))):
+    @pl.when(half == core)
+    def _():
+        wait_bytes(s1e.at[:, 0:7], col_s.at[2])
+
+    @pl.when(half != core)
+    def _():
+        wait_bytes(s1e, col_s.at[2])
+
+    for k, (wb, s1, per) in enumerate(((wb3, s13.at[:, 2:], X3), (wb4, s14, X4))):
         wait_bytes(wb.at[0, 0 : 7 + 3 * per], plane_s.at[k])
         wait_bytes(wb.at[0], f_s.at[k])
         @pl.when(alone)
@@ -571,6 +603,8 @@
             pltpu.VMEM((9, 18, 192), BF16),
             pltpu.VMEM((K3, WIN3, 128), BF16),
             pltpu.VMEM((K4, WIN4, 128), BF16),
+            pltpu.VMEM((2, 48, 128), BF16),
+            pltpu.VMEM((2, 8, 48, 128), BF16),
             pltpu.VMEM((4, 1 + X3 + C3, WIN3, 128), BF16),
             pltpu.VMEM((4, 1 + X4 + C4, WIN4, 128), BF16),
             pltpu.VMEM((2, K3, H3R, 128), BF16),
@@ -600,7 +634,7 @@
             pltpu.VMEM((384, 192), BF16),
             pltpu.VMEM((4, 16, 128), F32),
             pltpu.VMEM((4, 16, 128), F32),
-            dma((7,)), dma((2,)), dma((2,)), dma((2,)), dma((n,)),
+            dma((7,)), dma((2,)), dma((2,)), dma((3,)), dma((n,)),
             dma((2,)), dma((len(X_CHUNKS), NS)), dma((len(Z_CHUNKS), NW)), dma((2,)), dma((n,)),
             dma, dma, dma, dma, dma, dma, dma((2,)), dma((5,)), dma((2,)), dma((3,)), dma, dma,
         ],

time: 64.9 us -> 63.4 us (0.977)
  Pallas kernels: 63.2 us -> 61.7 us
    pallas_call x1, Pallas kernels: 63.2 us -> 61.7 us  [local(): pl.pallas_call(kernel, out_shape=jax.ShapeDtypeStruct((4, 16, 128), F32),...]
where the time goes in v6:
time: 63.4 us; the launch traced here: 63.2 us
  Pallas kernels  61.7 us (97%)
  local copies, waits for them, and re-layouts  1.53 us (2%)
    pallas_call x1, Pallas kernels, local(): pl.pallas_call(kernel, out_shape=jax.ShapeDtypeStruct((4, 16, 128), F32),...  61.7 us
    reshape x1, local copies, waits for them, and re-layouts, local(): return fields.reshape(1, 4, 16, 4, 32)  1.53 us

profile of v6, /device:TPU:6, one launch (start us, length us, event | category | flops | bytes accessed | tf_op | source)
XLA Modules:
  0.0 63.2 jit_solution(8957033876088687704)
XLA Ops:
  0.0 61.7 %nowcast.1 = f32[4,16,128]{2,1,0:T(8,128)} custom-call(bf16[4,2,16,192]{3,2,1,0:T(8,128)(2,1)} %bitcast.9, bf16[2,16,192]{2,1,0:T(8,128)(2,1)} %bitcast.11, bf16[4,32,96]{2,1,0:T(8,128)(2,1)} %bitcast.10, bf16[9,36,384]{2,1,0:T(8,128)(2,1)} %bitcast.7, bf16[9,18,192]{2,1,0:T(8,128)(2,1)} %bitcast.8, bf16[96,192]{1,0:T(8,128)(2,1)} %lm_ref.1, ...), custom_call_target="tpu_custom_call" | custom-call | tf_op jit(solution)/shard_map/nowcast/pallas_call | solution.py:590
  61.7 1.5 %reshape.3 = f32[1,4,16,4,32]{4,3,2,1,0:T(4,128)} reshape(f32[4,16,128]{2,1,0:T(8,128)} %nowcast.1) | data formatting | bytes 65536 | tf_op jit(solution)/shard_map/reshape | solution.py:654

commit v7 on v6

--- a/solution.py
+++ b/solution.py
@@ -42,7 +42,7 @@
 def kernel(
     x_ref, i3_ref, i4_ref, w3_ref, w4_ref, lm_ref, ro_ref, o_ref,
     i3v, i4v, lmv, rov, own3, own4, sis3, sis4, cw3, cw4, early, s1e, s13, s14, wb3, wb4,
-    xa, xi, xc, xe, xh, s3i, s3w, s4c, s4e, s4h, s4w, xw, pw, jx, j3, j4, p4, xg, xk, tmp, lm, ro, up, pt, po,
+    xa, xi, xc, xe, xh, s3i, s3w, s4c, s4e, s4h, s4w, xw, pw, jx, j3, j4, p4, xg, xk, tmp, lm, ro, up, pt,
     load_sem, raw_s, raw_r, col_s, col_r, plane_s, x_r, z_r, f_s, f_r,
     xa_s, xa_r, x0_s, x0_r, xn_s, xn_r, n3_s, n3_r, n4_s, n4_r, out_s, out_r,
 ):
@@ -456,7 +456,7 @@
         send_3(t)
 
     def to_lead(t):
-        return remote(pt.at[t], po.at[s], out_s, out_r, section=t)
+        return remote(pt.at[t], o_ref.at[s], out_s, out_r, section=t)
 
     def lift(t):
         lifted = nt(s3w[t].reshape(192, 256), lm[...]).astype(BF16)
@@ -496,7 +496,7 @@
 
         @pl.when(s == t)
         def _():
-            po[t] = pt[t]
+            pltpu.make_async_copy(pt.at[t], o_ref.at[s], out_r).start()
 
         @pl.when(s != t)
         def _():
@@ -552,8 +552,7 @@
     lift(LEADS - 1)
     level4(LEADS - 1, last=True)
 
-    wait_bytes(po.at[0:3], out_r)
-    o_ref[...] = po[...]
+    wait_bytes(o_ref, out_r)
 
     raw3.wait_send()
     raw4.wait_send()
@@ -591,7 +590,7 @@
         kernel,
         out_shape=jax.ShapeDtypeStruct((4, 16, 128), F32),
         in_specs=[pl.BlockSpec(memory_space=pl.ANY)] * 7,
-        out_specs=pl.BlockSpec(memory_space=pltpu.VMEM),
+        out_specs=pl.BlockSpec(memory_space=pl.ANY),
         scratch_shapes=[
             pltpu.VMEM((2, 16, 192), BF16),
             pltpu.VMEM((4, 32, 96), BF16),
@@ -633,7 +632,6 @@
             pltpu.VMEM((16, 128), BF16),
             pltpu.VMEM((384, 192), BF16),
             pltpu.VMEM((4, 16, 128), F32),
-            pltpu.VMEM((4, 16, 128), F32),
             dma((7,)), dma((2,)), dma((2,)), dma((3,)), dma((n,)),
             dma((2,)), dma((len(X_CHUNKS), NS)), dma((len(Z_CHUNKS), NW)), dma((2,)), dma((n,)),
             dma, dma, dma, dma, dma, dma, dma((2,)), dma((5,)), dma((2,)), dma((3,)), dma, dma,

time: 63.4 us -> 62.9 us (level)
  no operation moved by 1% of the time
where the time goes in v7:
time: 62.9 us; the launch traced here: 62.7 us
  Pallas kernels  61.2 us (97%)
  local copies, waits for them, and re-layouts  1.53 us (2%)
    pallas_call x1, Pallas kernels, local(): pl.pallas_call(kernel, out_shape=jax.ShapeDtypeStruct((4, 16, 128), F32),...  61.2 us
    reshape x1, local copies, waits for them, and re-layouts, local(): return fields.reshape(1, 4, 16, 4, 32)  1.53 us

profile of v7, /device:TPU:6, one launch (start us, length us, event | category | flops | bytes accessed | tf_op | source)
XLA Modules:
  0.0 62.7 jit_solution(16889373950009212122)
XLA Ops:
  0.0 61.2 %nowcast.1 = f32[4,16,128]{2,1,0:T(8,128)} custom-call(bf16[4,2,16,192]{3,2,1,0:T(8,128)(2,1)} %bitcast.9, bf16[2,16,192]{2,1,0:T(8,128)(2,1)} %bitcast.11, bf16[4,32,96]{2,1,0:T(8,128)(2,1)} %bitcast.10, bf16[9,36,384]{2,1,0:T(8,128)(2,1)} %bitcast.7, bf16[9,18,192]{2,1,0:T(8,128)(2,1)} %bitcast.8, bf16[96,192]{1,0:T(8,128)(2,1)} %lm_ref.1, ...), custom_call_target="tpu_custom_call" | custom-call | tf_op jit(solution)/shard_map/nowcast/pallas_call | solution.py:589
  61.2 1.5 %reshape.3 = f32[1,4,16,4,32]{4,3,2,1,0:T(4,128)} reshape(f32[4,16,128]{2,1,0:T(8,128)} %nowcast.1) | data formatting | bytes 65536 | tf_op jit(solution)/shard_map/reshape | solution.py:652

commit v8 on v7

--- a/solution.py
+++ b/solution.py
@@ -30,7 +30,7 @@
 X_RELAY = {}
 XR_HOPS = [(1, 1, 0), (3, -1, 0), (2, 1, 1), (2, -1, 2)]
 XR_RELAY = {0: (2,), 1: (3,)}
-RELAYED = (1, 2)
+RELAYED = (1,)
 Z_CHUNKS = [k for k, (level, slot, n) in enumerate(CHUNKS) if slot == 0]
 X_CHUNKS = [k for k, (level, slot, n) in enumerate(CHUNKS) if 0 < slot <= (X3 if level == 3 else X4)]
 
@@ -382,7 +382,7 @@
     plane_pass(1, 2, 3)
     plane_pass(0, 4, 5, 6, 7)
     plane_start(5)
-    plane_pass(2, 2, 3)
+    plane_pass(2, 2)
     plane_pass(3, 0, 1, 2)
     wait_borders()
 

time: 62.9 us -> 62.8 us (level)
  no operation moved by 1% of the time
where the time goes in v8:
time: 62.8 us; the launch traced here: 62.7 us
  Pallas kernels  61.1 us (97%)
  local copies, waits for them, and re-layouts  1.53 us (2%)
    pallas_call x1, Pallas kernels, local(): pl.pallas_call(kernel, out_shape=jax.ShapeDtypeStruct((4, 16, 128), F32),...  61.1 us
    reshape x1, local copies, waits for them, and re-layouts, local(): return fields.reshape(1, 4, 16, 4, 32)  1.53 us

profile of v8, /device:TPU:6, one launch (start us, length us, event | category | flops | bytes accessed | tf_op | source)
XLA Modules:
  0.0 62.7 jit_solution(4171986099410849493)
XLA Ops:
  0.0 61.1 %nowcast.1 = f32[4,16,128]{2,1,0:T(8,128)} custom-call(bf16[4,2,16,192]{3,2,1,0:T(8,128)(2,1)} %bitcast.9, bf16[2,16,192]{2,1,0:T(8,128)(2,1)} %bitcast.11, bf16[4,32,96]{2,1,0:T(8,128)(2,1)} %bitcast.10, bf16[9,36,384]{2,1,0:T(8,128)(2,1)} %bitcast.7, bf16[9,18,192]{2,1,0:T(8,128)(2,1)} %bitcast.8, bf16[96,192]{1,0:T(8,128)(2,1)} %lm_ref.1, ...), custom_call_target="tpu_custom_call" | custom-call | tf_op jit(solution)/shard_map/nowcast/pallas_call | solution.py:589
  61.1 1.5 %reshape.3 = f32[1,4,16,4,32]{4,3,2,1,0:T(4,128)} reshape(f32[4,16,128]{2,1,0:T(8,128)} %nowcast.1) | data formatting | bytes 65536 | tf_op jit(solution)/shard_map/reshape | solution.py:652
